TPU v7x, 256 devices: a whole 4x4x8 slice. The times are simulated.
256 devices in a mesh: rows: 32 (over x, y, core), cols: 8 (over z).
Axes of the slice: x: 4, y: 4, z: 8, core: 2. Of those that a mesh axis runs over, the one named last changes fastest.
Arguments:
- vectors: float32 [256, 131072], P('cols', 'rows'), may hold values from -6 to 6
- onsite: float32 [131072], P('rows'), may hold values from -2 to 2
- h_blocks: float32 [1024, 9, 128, 128], P('rows'), may hold values from -0.1875 to 0.1875
- block_cols: int32 [1024, 9], P('rows'), may hold values from 0 to 1023, as said below
- block_counts: int32 [1024], P('rows'), may hold values from 3 to 9, as said below
Outputs:
- filtered: float32 [256, 131072], P('cols', 'rows')
- correlation: float32 [256, 256], P('cols')
Inputs may be any that keep to these rules, and one draw needn't show every extreme that they name: `block_cols`: entry k of block row r is (r + o) mod 1024 with -4 <= o <= 4; the offsets o of one block row are distinct, and its first three are 0, 4 and -4. `block_counts`: some block row uses all 9 slots.
All inputs are finite; a program needn't handle non-finite values.
Results may differ from a plain program's by a relative error of at most 0.0003.
Values sent between devices are 32-bit elements; how exact they have to be, the bound alone decides.
No kernel may reach another device: no remote copies, remote signals or barrier semaphores. Data moves between devices by JAX's collectives and lax.ppermute only.
A program may use at most 128 MiB of HBM per device.

v0:
```python
import jax
import jax.numpy as jnp
from jax import lax
from jax.sharding import PartitionSpec as P

REACH = 4


filter_center = 1.0
filter_half = 2.0


def padded(shard, sides, width):
    for axis, dim in sides:
        size, length = (lax.axis_size(axis), shard.shape[dim])
        up = [(i, (i + 1) % size) for i in range(size)]
        down = [(j, i) for i, j in up]
        last = lax.slice_in_dim(shard, length - width, length, axis=dim)
        first = lax.slice_in_dim(shard, 0, width, axis=dim)
        before = lax.ppermute(last, axis, up)
        after = lax.ppermute(first, axis, down)
        shard = jnp.concatenate([before, shard, after], axis=dim)
    return shard


def apply_hamiltonian(field, onsite, h_blocks, block_cols, block_counts):
    vcount, width = field.shape
    local_blocks = block_cols.shape[0]
    block = width // local_blocks
    nblocks = local_blocks * lax.axis_size("rows")
    first_row = lax.axis_index("rows") * local_blocks
    global_rows = first_row + jnp.arange(local_blocks, dtype=jnp.int32)
    widened = padded(field, (("rows", 1),), REACH * block)
    source = widened.reshape(vcount, local_blocks + 2 * REACH, block)
    where_cols = jnp.arange(local_blocks, dtype=jnp.int32)[:, None] + jnp.mod(
        block_cols - global_rows[:, None] + REACH, nblocks
    )
    slot_ids = jnp.arange(block_cols.shape[1], dtype=jnp.int32)
    weight = (slot_ids[None, :] < block_counts[:, None]).astype(jnp.float32)
    picked = source[:, where_cols, :] * weight[None, :, :, None]
    total = jnp.einsum("vrkj,rkij->vri", picked, h_blocks, precision=lax.Precision.HIGHEST)
    return total.reshape(vcount, width) + onsite[None, :] * field


def on_device(vectors, onsite, h_blocks, block_cols, block_counts):
    first = (
        apply_hamiltonian(vectors, onsite, h_blocks, block_cols, block_counts)
        - filter_center * vectors
    ) / filter_half
    second = (
        apply_hamiltonian(first, onsite, h_blocks, block_cols, block_counts) - filter_center * first
    )
    filtered = 2.0 * second / filter_half - vectors
    total_rows = filtered.shape[1] * lax.axis_size("rows")
    everyone = lax.all_gather(filtered, "cols", axis=0, tiled=True)
    partial_gram = (
        lax.dot_general(
            filtered,
            everyone,
            (((1,), (1,)), ((), ())),
            precision=lax.Precision.HIGHEST,
            preferred_element_type=jnp.float32,
        )
        / total_rows
    )
    correlation = lax.psum(partial_gram, "rows")
    return (filtered, correlation)


def solution(mesh):
    return jax.shard_map(
        on_device,
        mesh=mesh,
        in_specs=(
            P("cols", "rows"),
            P("rows"),
            P("rows", None, None, None),
            P("rows", None),
            P("rows"),
        ),
        out_specs=(P("cols", "rows"), P("cols", None)),
        check_vma=False,
    )
```

profile of v0, /device:TPU:1, one launch (start us, length us, event | category | flops | bytes accessed | tf_op | source)
XLA Modules:
  0.0 271.3 jit_solution(9548934557195821858)
XLA Ops:
  7.2 0.0 all-gather.2.cloned.1.call-start
  7.2 0.9 fusion.22
  8.1 2.8 %collective-permute-start = (f32[32,512]{1,0:T(8,128)S(1)}, f32[32,512]{1,0:T(8,128)S(1)}, u32[]{:S(2)}, u32[]{:S(2)}) collective-permute-start(f32[32,512]{1,0:T(8,128)S(1)} %get-tuple-element.4), channel_id=1, source_target_pairs={{0,8},{8,16},{16,24},{24,32},{32,40},{40,48},{48,56},{56,64},{64,7... | collective-permute-start | bytes 196616 | tf_op jit(solution)/shard_map/ppermute | solution.py:20
  10.9 0.6 collective-permute-start.1
  11.5 0.7 compare_select_fusion
  12.2 0.1 copy.12
  12.3 0.1 reshape.49
  12.4 0.7 fusion.18
  13.2 0.0 collective-permute-done
  13.2 1.4 collective-permute-done.1
  14.6 1.1 copy_bitcast_fusion.1
  15.7 3.3 %gather_fusion = f32[288,32,128]{2,1,0:T(8,128)} fusion(f32[32,40,128]{2,0,1:T(8,128)S(1)} %copy_bitcast_fusion.1, s32[1024]{0:T(1024)S(1)} %pad_clamp_fusion), kind=kCustom, calls=%fused_computation | custom fusion | bytes 9438336 | tf_op jit(solution)/shard_map/gather | solution.py:40
  19.0 0.0 copy-start
  19.0 0.0 copy-start.1
  19.0 22.8 %fusion.8 = f32[32,4,8,128]{3,2,1,0:T(8,128)S(1)} fusion(f32[32,9,128,128]{3,2,1,0:T(8,128)} %param.7, f32[32,9,32,128]{3,2,1,0:T(8,128)} %bitcast.55, f32[32,9]{1,0:T(8,128)S(1)} %fusion.18), kind=kOutput, calls=%fused_computation.10 | convolution fusion | flops 1813118976 | bytes 24118400 | tf_op jit(solution)/shard_map/vrkj,rkij->vri/dot_general | solution.py:41
  41.8 0.0 copy-done
  41.8 0.0 copy-done.1
  41.8 0.1 fusion.17
  41.9 0.1 collective-permute-start.2
  42.0 4.1 %collective-permute-start.3 = (f32[32,512]{1,0:T(8,128)S(1)}, f32[32,512]{1,0:T(8,128)S(1)}, u32[]{:S(2)}, u32[]{:S(2)}) collective-permute-start(f32[32,512]{1,0:T(8,128)S(1)} %get-tuple-element.3), channel_id=1, source_target_pairs={{8,0},{16,8},{24,16},{32,24},{40,32},{48,40},{56,48},{64,56},{72,6... | collective-permute-start | bytes 196616 | tf_op jit(solution)/shard_map/ppermute | solution.py:21
  46.1 0.5 collective-permute-done.2
  46.6 0.4 collective-permute-done.3
  47.0 0.1 copy_bitcast_fusion
  47.1 3.3 %gather_fusion.1 = f32[288,32,128]{2,1,0:T(8,128)} fusion(f32[32,40,128]{2,0,1:T(8,128)S(1)} %copy_bitcast_fusion, s32[1024]{0:T(1024)S(1)} %pad_clamp_fusion), kind=kCustom, calls=%fused_computation.1 | custom fusion | bytes 9438336 | tf_op jit(solution)/shard_map/gather | solution.py:40
  50.4 22.8 %fusion.11 = f32[32,4,8,128]{3,2,1,0:T(8,128)S(1)} fusion(f32[32,9,128,128]{3,2,1,0:T(8,128)} %param.7, f32[32,9,32,128]{3,2,1,0:T(8,128)} %bitcast.54, f32[32,9]{1,0:T(8,128)S(1)} %fusion.18), kind=kOutput, calls=%fused_computation.11 | convolution fusion | flops 1813118976 | bytes 24118400 | tf_op jit(solution)/shard_map/vrkj,rkij->vri/dot_general | solution.py:41
  73.2 1.0 fusion.15
  74.1 0.0 all-gather.2.cloned.1.call-update
  74.2 61.1 %all-gather.2.cloned.1.call-done = f32[256,4096]{1,0:T(8,128)} async-done(((f32[32,4096]{1,0:T(8,128)}), f32[256,4096]{1,0:T(8,128)}) %all-gather.2.cloned.1.call-update) | async-done | bytes 4194320 | tf_op jit(solution)/shard_map/all_gather | solution.py:55
  135.3 6.1 %convolution_multiply_fusion = f32[32,256]{1,0:T(8,128)S(1)} fusion(f32[32,4096]{1,0:T(8,128)} %fusion.15, f32[256,4096]{1,0:T(8,128)} %all-gather.2.cloned.1.call-done), kind=kOutput, calls=%fused_computation.12 | convolution fusion | flops 402661376 | bytes 4751360 | tf_op jit(solution)/shard_map/dot_general | solution.py:57
  141.4 123.1 %psum.7 = f32[32,256]{1,0:T(8,128)} all-reduce(f32[32,256]{1,0:T(8,128)S(1)} %convolution_multiply_fusion), channel_id=1, replica_groups=mesh['rows'=32,'cols'=8] {'rows'}, use_global_device_ids=true, to_apply=%region_0.1 | all-reduce | flops 8192 | bytes 65536 | tf_op jit(solution)/shard_map/psum | solution.py:66
  (4 shorter events, 0.0 us)
Async XLA Ops:
  7.2 128.1 %all-gather.2.cloned.1.call-start = ((), (), s32[]{:S(2)}) async-start(), calls=%async_computation | async-start | bytes 4718592 | tf_op jit(solution)/shard_map/all_gather | solution.py:55
  8.1 5.1 %collective-permute-start = (f32[32,512]{1,0:T(8,128)S(1)}, f32[32,512]{1,0:T(8,128)S(1)}, u32[]{:S(2)}, u32[]{:S(2)}) collective-permute-start(f32[32,512]{1,0:T(8,128)S(1)} %get-tuple-element.4), channel_id=1, source_target_pairs={{0,8},{8,16},{16,24},{24,32},{32,40},{40,48},{48,56},{56,64},{64,7... | collective-permute-start | bytes 196616 | tf_op jit(solution)/shard_map/ppermute | solution.py:20
  10.9 3.7 %collective-permute-start.1 = (f32[32,512]{1,0:T(8,128)S(1)}, f32[32,512]{1,0:T(8,128)S(1)}, u32[]{:S(2)}, u32[]{:S(2)}) collective-permute-start(f32[32,512]{1,0:T(8,128)S(1)} %get-tuple-element.5), channel_id=1, source_target_pairs={{8,0},{16,8},{24,16},{32,24},{40,32},{48,40},{56,48},{64,56},{72,6... | collective-permute-start | bytes 196616 | tf_op jit(solution)/shard_map/ppermute | solution.py:21
  19.0 22.8 %copy-start = (f32[32,4096]{1,0:T(8,128)S(1)}, f32[32,4096]{1,0:T(8,128)}, u32[]{:S(2)}) copy-start(f32[32,4096]{1,0:T(8,128)} %param.5) | copy-start | bytes 1572868
  19.0 22.8 %copy-start.1 = (f32[4096]{0:T(1024)S(1)}, f32[4096]{0:T(1024)}, u32[]{:S(2)}) copy-start(f32[4096]{0:T(1024)} %param.6) | copy-start | bytes 49156
  41.9 4.7 %collective-permute-start.2 = (f32[32,512]{1,0:T(8,128)S(1)}, f32[32,512]{1,0:T(8,128)S(1)}, u32[]{:S(2)}, u32[]{:S(2)}) collective-permute-start(f32[32,512]{1,0:T(8,128)S(1)} %get-tuple-element.2), channel_id=1, source_target_pairs={{0,8},{8,16},{16,24},{24,32},{32,40},{40,48},{48,56},{56,64},{64,7... | collective-permute-start | bytes 196616 | tf_op jit(solution)/shard_map/ppermute | solution.py:20
  42.0 5.0 %collective-permute-start.3 = (f32[32,512]{1,0:T(8,128)S(1)}, f32[32,512]{1,0:T(8,128)S(1)}, u32[]{:S(2)}, u32[]{:S(2)}) collective-permute-start(f32[32,512]{1,0:T(8,128)S(1)} %get-tuple-element.3), channel_id=1, source_target_pairs={{8,0},{16,8},{24,16},{32,24},{40,32},{48,40},{56,48},{64,56},{72,6... | collective-permute-start | bytes 196616 | tf_op jit(solution)/shard_map/ppermute | solution.py:21
Sparse Core Ops, SparseCore 0:
  74.3 60.9 all-gather.1
where the time goes:
time: 274 us; the launch traced here: 271 us
  blocking collectives  123 us (45%)
  waiting for transfers between devices  63.4 us (23%)
  matrix products  51.6 us (19%)
  between operations  14.1 us (5%)
  local copies, waits for them, and re-layouts  7.7 us (3%)
  starting transfers between devices  7.66 us (3%)
  other arithmetic  3.68 us (1%)
    psum x1, blocking collectives, on_device(): correlation = lax.psum(partial_gram, 'rows')  123 us
    all_gather x1, waiting for transfers between devices, on_device(): everyone = lax.all_gather(filtered, 'cols', axis=0, tiled=True)  61.1 us
    dot_general x2, matrix products, apply_hamiltonian(): jnp.einsum('vrkj,rkij->vri', picked, h_blocks, precision=lax.Precision.HI...  45.6 us
    gather x2, local copies, waits for them, and re-layouts, apply_hamiltonian(): picked = source[:, where_cols, :] * weight[None, :, :, None]  6.6 us
    dot_general x1, matrix products, on_device(): lax.dot_general(filtered, everyone, (((1,), (1,)), ((), ())), precision=l...  6.09 us
  transfers between devices with their start and end apart: 5, of which 4 were waited for; matrix products, arithmetic and copies ran while one was open for 1% of the time, Pallas kernels for 0%

commit v1 on v0

v1 whole, which is shorter than its diff:
```python
import functools

import jax
import jax.numpy as jnp
from jax import lax
from jax.experimental import pallas as pl
from jax.experimental.pallas import tpu as pltpu
from jax.sharding import PartitionSpec as P

REACH = 4
BLOCK = 128

filter_center = 1.0
filter_half = 2.0

f32, bf16 = jnp.float32, jnp.bfloat16
VMEM = pl.BlockSpec(memory_space=pltpu.VMEM)
SMEM = pl.BlockSpec(memory_space=pltpu.SMEM)
ANY = pl.BlockSpec(memory_space=pl.ANY)


def halves(x):
    high = x.astype(bf16)
    return high, (x - high.astype(f32)).astype(bf16)


def load_blocks(table, pieces):
    vcount = table.shape[1] // 2
    for ref, start, blocks in pieces:
        for b in range(blocks):
            high, low = halves(ref[:, b * BLOCK : (b + 1) * BLOCK])
            table[start + b, 0:vcount] = high
            table[start + b, vcount : 2 * vcount] = low
    table[table.shape[0] - 1] = jnp.zeros(table.shape[1:], bf16)


def apply_rows(count, unroll, row_of, cols, counts, nblocks, table, h_hbm, h_buf, sems, finish):
    slots = h_buf.shape[1]
    empty = table.shape[0] - 1

    def fetch(i):
        return pltpu.make_async_copy(h_hbm.at[row_of(i)], h_buf.at[i], sems.at[i])

    def product(i):
        row = row_of(i)
        here = cols[row, 0]
        used = counts[row]
        picked = []
        for k in range(slots):
            shift = lax.rem(cols[row, k] - here + (REACH + nblocks), nblocks)
            picked.append(table[jnp.where(k < used, row + shift, empty)])
        left = jnp.concatenate(picked, axis=1)
        split = [halves(h_buf[i, k]) for k in range(slots)]
        right = jnp.concatenate(
            [
                jnp.concatenate([high for high, _ in split], axis=1),
                jnp.concatenate([low for _, low in split], axis=1),
            ],
            axis=0,
        )
        both = lax.dot_general(left, right, (((1,), (1,)), ((), ())), preferred_element_type=f32)
        v = left.shape[0] // 2
        return (both[:v, :BLOCK] + both[:v, BLOCK:]) + (both[v:, :BLOCK] + both[v:, BLOCK:])

    def step(s, carry):
        for u in range(unroll):
            fetch(s * unroll + u).wait()
        for u in range(unroll):
            i = s * unroll + u
            finish(i, row_of(i), product(i))
        return carry

    return fetch, lambda: lax.fori_loop(0, count // unroll, step, 0)


def columns(ref, block, count=1):
    return ref[:, pl.ds(pl.multiple_of(block * BLOCK, BLOCK), count * BLOCK)]


def set_columns(ref, block, value):
    ref[:, pl.ds(pl.multiple_of(block * BLOCK, BLOCK), BLOCK)] = value


def run_all(count, fetch):
    def one(i, carry):
        fetch(i).start()
        return carry

    lax.fori_loop(0, count, one, 0)


def first_inner(nblocks, local, cols, counts, onsite, field, h_hbm, out, table, h_buf, sems):
    count = local - 2 * REACH

    def row_of(i):
        return i + REACH

    def finish(i, row, total):
        diag = onsite[pl.ds(row, 1), :] - filter_center
        set_columns(out, i, (total + diag * columns(field, row)) / filter_half)

    fetch, loop = apply_rows(
        count, 4, row_of, cols, counts, nblocks, table, h_hbm, h_buf, sems, finish
    )
    run_all(count, fetch)
    load_blocks(table, [(field, REACH, local)])
    loop()


def first_edge(
    nblocks, local, cols, counts, onsite, before, field, after, h_hbm, low, high, table, h_buf, sems
):
    count = 2 * REACH

    def row_of(i):
        return jnp.where(i < REACH, i, i + local - 2 * REACH)

    def finish(i, row, total):
        diag = onsite[pl.ds(row, 1), :] - filter_center
        value = (total + diag * columns(field, row)) / filter_half

        @pl.when(i < REACH)
        def _():
            set_columns(low, i, value)

        @pl.when(i >= REACH)
        def _():
            set_columns(high, i - REACH, value)

    fetch, loop = apply_rows(
        count, 4, row_of, cols, counts, nblocks, table, h_hbm, h_buf, sems, finish
    )
    run_all(count, fetch)
    pieces = [(before, 0, REACH), (after, local + REACH, REACH)]
    pieces.append((field.at[:, 0 : 2 * REACH * BLOCK], REACH, 2 * REACH))
    pieces.append((field.at[:, (local - 2 * REACH) * BLOCK :], local - REACH, 2 * REACH))
    load_blocks(table, pieces)
    loop()


def second_inner(
    nblocks, local, groups, where, cols, counts, onsite, inner, field, h_hbm, out, parts, table, h_buf, sems
):
    count = local - 4 * REACH
    each = count // groups

    def row_of(i):
        k = i // each
        return lax.rem(where[0] + k, groups) * each + (i - k * each) + 2 * REACH

    def finish(i, row, total):
        diag = onsite[pl.ds(row, 1), :] - filter_center
        second = total + diag * columns(inner, row - REACH)
        value = 2.0 * second / filter_half - columns(field, row)
        set_columns(out, row - 2 * REACH, value)
        k = i // each
        parts[k, :, pl.ds(pl.multiple_of((i - k * each) * BLOCK, BLOCK), BLOCK)] = value

    fetch, loop = apply_rows(
        count, 4, row_of, cols, counts, nblocks, table, h_hbm, h_buf, sems, finish
    )
    run_all(count, fetch)
    load_blocks(table, [(inner, 2 * REACH, local - 2 * REACH)])
    loop()


def second_edge(
    nblocks, local, groups, where, cols, counts, onsite, before, low, inner, high, after, field, h_hbm,
    out_low, out_high, parts, table, h_buf, sems, middle,
):
    half = 2 * REACH
    count = 2 * half
    each = count // groups

    def place_of(i):
        k = i // each
        return lax.rem(where[0] + k, groups) * each + (i - k * each)

    def row_of(i):
        m = place_of(i)
        return jnp.where(m < half, m, m + local - 2 * half)

    def finish(i, row, total):
        diag = onsite[pl.ds(row, 1), :] - filter_center
        m = place_of(i)
        second = total + diag * columns(middle, m)
        value = 2.0 * second / filter_half - columns(field, row)

        @pl.when(m < half)
        def _():
            set_columns(out_low, m, value)

        @pl.when(m >= half)
        def _():
            set_columns(out_high, m - half, value)

        k = i // each
        parts[k, :, pl.ds(pl.multiple_of((i - k * each) * BLOCK, BLOCK), BLOCK)] = value

    fetch, loop = apply_rows(
        count, 4, row_of, cols, counts, nblocks, table, h_hbm, h_buf, sems, finish
    )
    run_all(count, fetch)
    reach = REACH * BLOCK
    middle[:, 0:reach] = low[...]
    middle[:, reach : 2 * reach] = inner[:, 0:reach]
    middle[:, 2 * reach : 3 * reach] = inner[:, inner.shape[1] - reach :]
    middle[:, 3 * reach :] = high[...]
    load_blocks(
        table,
        [
            (before, 0, REACH),
            (low, REACH, REACH),
            (inner.at[:, 0 : 2 * reach], 2 * REACH, 2 * REACH),
            (inner.at[:, inner.shape[1] - 2 * reach :], local - 2 * REACH, 2 * REACH),
            (high, local, REACH),
            (after, local + REACH, REACH),
        ],
    )
    loop()


def gram(groups, scale, where, *refs):
    sent, out = refs[: 2 * groups], refs[2 * groups]
    high, low, both = refs[2 * groups + 1 :]
    vcount, width = sent[0].shape[-2:]
    for k in range(groups):
        place = pl.multiple_of(lax.rem(where[0] + (groups - k), groups) * vcount, vcount)
        for c in range(2):
            ref = sent[2 * k + c]
            block = ref[0] if k == 0 else ref[...]
            a, b = halves(block)
            high[pl.ds(place, vcount), c * width : (c + 1) * width] = a
            low[pl.ds(place, vcount), c * width : (c + 1) * width] = b
    nt = (((1,), (1,)), ((), ()))
    a, b = high[...], low[...]
    both[...] = (
        lax.dot_general(a, a, nt, preferred_element_type=f32)
        + lax.dot_general(a, b, nt, preferred_element_type=f32)
        + lax.dot_general(b, a, nt, preferred_element_type=f32)
    ) * scale
    for k in range(groups):
        place = pl.multiple_of(lax.rem(where[0] + (groups - k), groups) * vcount, vcount)
        out[k] = both[pl.ds(place, vcount), :]


def params():
    return pltpu.CompilerParams(vmem_limit_bytes=40 * 1024 * 1024)


def cost(rows, slots, vcount):
    return pl.CostEstimate(
        flops=rows * slots * BLOCK * BLOCK * vcount * 2 * 6,
        bytes_accessed=rows * slots * BLOCK * BLOCK * 4,
        transcendentals=0,
    )


def on_device(vectors, onsite, h_blocks, block_cols, block_counts):
    vcount, width = vectors.shape
    local, slots = block_cols.shape
    ranks = lax.axis_size("rows")
    groups = lax.axis_size("cols")
    nblocks = local * ranks
    reach = REACH * BLOCK
    where = lax.axis_index("cols").astype(jnp.int32).reshape(1)
    onsite2 = onsite.reshape(local, BLOCK)

    def shape(*dims):
        return jax.ShapeDtypeStruct(dims, f32)

    def scratch(rows):
        return [
            pltpu.VMEM((local + 2 * REACH + 1, 2 * vcount, BLOCK), bf16),
            pltpu.VMEM((rows, slots, BLOCK, BLOCK), f32),
            pltpu.SemaphoreType.DMA((rows,)),
        ]

    up = [(i, (i + 1) % ranks) for i in range(ranks)]
    down = [(j, i) for i, j in up]

    def around(low, high):
        return lax.ppermute(high, "rows", up), lax.ppermute(low, "rows", down)

    before, after = around(vectors[:, :reach], vectors[:, width - reach :])

    n = local - 2 * REACH
    inner = pl.pallas_call(
        functools.partial(first_inner, nblocks, local),
        in_specs=[SMEM, SMEM, VMEM, VMEM, ANY],
        out_specs=VMEM,
        out_shape=shape(vcount, n * BLOCK),
        scratch_shapes=scratch(n),
        compiler_params=params(),
        cost_estimate=cost(n, slots, vcount),
        name="first_inner",
    )(block_cols, block_counts, onsite2, vectors, h_blocks)

    n = 2 * REACH
    low, high = pl.pallas_call(
        functools.partial(first_edge, nblocks, local),
        in_specs=[SMEM, SMEM, VMEM, VMEM, VMEM, VMEM, ANY],
        out_specs=(VMEM, VMEM),
        out_shape=(shape(vcount, reach), shape(vcount, reach)),
        scratch_shapes=scratch(n),
        compiler_params=params(),
        cost_estimate=cost(n, slots, vcount),
        name="first_edge",
    )(block_cols, block_counts, onsite2, before, vectors, after, h_blocks)

    before, after = around(low, high)

    n = local - 4 * REACH
    out_inner, parts_inner = pl.pallas_call(
        functools.partial(second_inner, nblocks, local, groups),
        in_specs=[SMEM, SMEM, SMEM, VMEM, VMEM, VMEM, ANY],
        out_specs=(VMEM, VMEM),
        out_shape=(shape(vcount, n * BLOCK), shape(groups, vcount, n * BLOCK // groups)),
        scratch_shapes=scratch(n),
        compiler_params=params(),
        cost_estimate=cost(n, slots, vcount),
        name="second_inner",
    )(where, block_cols, block_counts, onsite2, inner, vectors, h_blocks)

    n = 4 * REACH
    out_low, out_high, parts_edge = pl.pallas_call(
        functools.partial(second_edge, nblocks, local, groups),
        in_specs=[SMEM, SMEM, SMEM, VMEM, VMEM, VMEM, VMEM, VMEM, VMEM, VMEM, ANY],
        out_specs=(VMEM, VMEM, VMEM),
        out_shape=(
            shape(vcount, 2 * reach),
            shape(vcount, 2 * reach),
            shape(groups, vcount, n * BLOCK // groups),
        ),
        scratch_shapes=scratch(n) + [pltpu.VMEM((vcount, n * BLOCK), f32)],
        compiler_params=params(),
        cost_estimate=cost(n, slots, vcount),
        name="second_edge",
    )(where, block_cols, block_counts, onsite2, before, low, inner, high, after, vectors, h_blocks)

    filtered = jnp.concatenate([out_low, out_inner, out_high], axis=1)

    def turn(x, k):
        return lax.ppermute(x, "cols", [(i, (i + k) % groups) for i in range(groups)])

    order = sorted(range(1, groups), key=lambda k: -min(k, groups - k))
    got = {0: (parts_inner, parts_edge)}
    first_got = {k: turn(parts_inner[k], k) for k in order}
    second_got = {k: turn(parts_edge[k], k) for k in order}
    for k in order:
        got[k] = (first_got[k], second_got[k])
    flat = [x for k in range(groups) for x in got[k]]
    total_v = vcount * groups
    total_w = width // groups
    terms = pl.pallas_call(
        functools.partial(gram, groups, 1.0 / (width * ranks)),
        in_specs=[SMEM] + [VMEM] * (2 * groups),
        out_specs=VMEM,
        out_shape=shape(groups, vcount, total_v),
        scratch_shapes=[
            pltpu.VMEM((total_v, total_w), bf16),
            pltpu.VMEM((total_v, total_w), bf16),
            pltpu.VMEM((total_v, total_v), f32),
        ],
        compiler_params=params(),
        name="gram",
    )(where, *flat)

    mine = terms[0]
    for x in [turn(terms[k], -k) for k in order]:
        mine = mine + x

    step = 1
    while step < ranks:
        mine = mine + lax.ppermute(mine, "rows", [(i, i ^ step) for i in range(ranks)])
        step *= 2
    return (filtered, mine)


def solution(mesh):
    return jax.shard_map(
        on_device,
        mesh=mesh,
        in_specs=(
            P("cols", "rows"),
            P("rows"),
            P("rows", None, None, None),
            P("rows", None),
            P("rows"),
        ),
        out_specs=(P("cols", "rows"), P("cols", None)),
        check_vma=False,
    )
```

time: 274 us -> 121 us (0.44)
  the two profiles are of different devices: /device:TPU:1 before, /device:TPU:32 now
where the time goes in v1:
time: 121 us
  starting transfers between devices  53 us (44%)
  waiting for transfers between devices  31.2 us (26%)
  Pallas kernels  30.2 us (25%)
  local copies, waits for them, and re-layouts  4.13 us (3%)
  other arithmetic  1.49 us (1%)
    ppermute x21, starting transfers between devices, turn(): lax.ppermute(x, 'cols', [(i, (i + k) % groups) for i in range(groups)])  43 us
    ppermute x5, waiting for transfers between devices, on_device(): lax.ppermute(mine, 'rows', [(i, i ^ step) for i in range(ranks)])  19 us
    ppermute x21, waiting for transfers between devices, turn(): lax.ppermute(x, 'cols', [(i, (i + k) % groups) for i in range(groups)])  12.2 us
    ppermute x4, starting transfers between devices, around(): return (lax.ppermute(high, 'rows', up), lax.ppermute(low, 'rows', down))  9.95 us
    pallas_call x1, Pallas kernels, on_device(): pl.pallas_call(functools.partial(second_edge, nblocks, local, groups), in...  9.85 us
    pallas_call x1, Pallas kernels, on_device(): pl.pallas_call(functools.partial(first_inner, nblocks, local), in_specs=[...  7.7 us
    pallas_call x1, Pallas kernels, on_device(): pl.pallas_call(functools.partial(first_edge, nblocks, local), in_specs=[S...  6.07 us
    pallas_call x1, Pallas kernels, on_device(): pl.pallas_call(functools.partial(second_inner, nblocks, local, groups), i...  6.04 us
  transfers between devices with their start and end apart: 30, of which 11 were waited for; matrix products, arithmetic and copies ran while one was open for 1% of the time, Pallas kernels for 20%

profile of v1, /device:TPU:32, one launch (start us, length us, event | category | flops | bytes accessed | tf_op | source)
XLA Modules:
  0.0 120.8 jit_solution(2582729704463735623)
XLA Ops:
  0.6 0.9 fusion.7
  1.5 4.7 %collective-permute-start.1 = (f32[32,512]{1,0:T(8,128)S(1)}, f32[32,512]{1,0:T(8,128)S(1)}, u32[]{:S(2)}, u32[]{:S(2)}) collective-permute-start(f32[32,512]{1,0:T(8,128)S(1)} %get-tuple-element.16), channel_id=1, source_target_pairs={{8,0},{16,8},{24,16},{32,24},{40,32},{48,40},{56,48},{64,56},{72,6... | collective-permute-start | bytes 196616 | tf_op jit(solution)/shard_map/ppermute | solution.py:283
  6.2 0.8 copy.9.cols
  7.0 1.0 copy-done
  8.1 0.7 copy-done.2
  8.8 0.7 copy-done.3
  9.4 7.7 %first_inner.1.inner = f32[32,3072]{1,0:T(8,128)S(1)} custom-call(s32[32,9]{1,0:T(8,128)S(1)} %copy.9.cols, s32[32]{0:T(128)S(1)} %copy-done.3, f32[32,128]{1,0:T(8,128)S(1)} %bitcast.60, f32[32,4096]{1,0:T(8,128)S(1)} %copy-done, f32[32,9,128,128]{3,2,1,0:T(8,128)} %h_hbm.7), custom_call_target="tpu_custom_call" | custom-call | flops 1358954496 | bytes 14155776 | tf_op jit(solution)/shard_map/first_inner/pallas_call | solution.py:288
  17.1 6.0 %second_inner.1 = (f32[32,2048]{1,0:T(8,128)S(1)}, f32[8,32,256]{2,1,0:T(8,128)S(1)}) custom-call(s32[1]{0:T(128)} %bitcast.where, s32[32,9]{1,0:T(8,128)S(1)} %copy.9.cols, s32[32]{0:T(128)S(1)} %copy-done.3, f32[32,128]{1,0:T(8,128)S(1)} %bitcast.61, f32[32,3072]{1,0:T(8,128)S(1)} %first_inner.1.inner, f32[32,4096]{1,0:T(8,128)S(1)} %copy-done, ...), custom_call_target="tpu_custom_call" | custom-call | flops 905969664 | bytes 9437184 | tf_op jit(solution)/shard_map/second_inner/pallas_call | solution.py:314
  23.2 0.0 collective-permute-done.before
  23.2 6.1 %first_edge.1 = (f32[32,512]{1,0:T(8,128)S(1)}, f32[32,512]{1,0:T(8,128)S(1)}) custom-call(s32[32,9]{1,0:T(8,128)S(1)} %copy.9.cols, s32[32]{0:T(128)S(1)} %copy-done.3, f32[32,128]{1,0:T(8,128)S(1)} %bitcast.62, f32[32,512]{1,0:T(8,128)S(1)} %collective-permute-done.before, f32[32,4096]{1,0:T(8,128)S(1)} %copy-done.1, ...), custom_call_target="tpu_custom_call" | custom-call | flops 452984832 | bytes 4718592 | tf_op jit(solution)/shard_map/first_edge/pallas_call | solution.py:300
  29.3 0.1 collective-permute-start.2
  29.4 5.1 %collective-permute-start.3 = (f32[32,512]{1,0:T(8,128)S(1)}, f32[32,512]{1,0:T(8,128)S(1)}, u32[]{:S(2)}, u32[]{:S(2)}) collective-permute-start(f32[32,512]{1,0:T(8,128)S(1)} %get-tuple-element.10.low), channel_id=1, source_target_pairs={{8,0},{16,8},{24,16},{32,24},{40,32},{48,40},{56,48},{64,56},{72,6... | collective-permute-start | bytes 196616 | tf_op jit(solution)/shard_map/ppermute | solution.py:283
  34.6 0.2 collective-permute-start.16
  34.8 6.3 %collective-permute-start.14 = (f32[32,256]{1,0:T(8,128)S(1)}, f32[32,256]{1,0:T(8,128)S(1)}, u32[]{:S(2)}, u32[]{:S(2)}) collective-permute-start(f32[32,256]{1,0:T(8,128)S(1)} %get-tuple-element.33), channel_id=1, source_target_pairs={{0,6},{1,7},{2,0},{3,1},{4,2},{5,3},{6,4},{7,5},{8,14},{9,15},{10,... | collective-permute-start | bytes 98312 | tf_op jit(solution)/shard_map/ppermute | solution.py:344
  41.1 1.0 collective-permute-start.12
  42.0 4.5 %collective-permute-start.10 = (f32[32,256]{1,0:T(8,128)S(1)}, f32[32,256]{1,0:T(8,128)S(1)}, u32[]{:S(2)}, u32[]{:S(2)}) collective-permute-start(f32[32,256]{1,0:T(8,128)S(1)} %get-tuple-element.35), channel_id=1, source_target_pairs={{0,4},{1,5},{2,6},{3,7},{4,0},{5,1},{6,2},{7,3},{8,12},{9,13},{10,... | collective-permute-start | bytes 98312 | tf_op jit(solution)/shard_map/ppermute | solution.py:344
  46.5 0.5 collective-permute-start.8
  47.0 9.8 %second_edge.1 = (f32[32,1024]{1,0:T(8,128)S(1)}, f32[32,1024]{1,0:T(8,128)S(1)}, f32[8,32,256]{2,1,0:T(8,128)S(1)}) custom-call(s32[1]{0:T(128)} %bitcast.where, s32[32,9]{1,0:T(8,128)S(1)} %copy.9.cols, s32[32]{0:T(128)S(1)} %copy-done.3, f32[32,128]{1,0:T(8,128)S(1)} %bitcast.63, f32[32,512]{1,0:T(8,128)S(1)} %collective-permute-done.2.before, ...), custom_call_target="tpu_custom_call" | custom-call | flops 905969664 | bytes 9437184 | tf_op jit(solution)/shard_map/second_edge/pallas_call | solution.py:326
  56.9 0.0 collective-permute-done.16.refs_14_
  56.9 3.0 %collective-permute-start.6 = (f32[32,256]{1,0:T(8,128)S(1)}, f32[32,256]{1,0:T(8,128)S(1)}, u32[]{:S(2)}, u32[]{:S(2)}) collective-permute-start(f32[32,256]{1,0:T(8,128)S(1)} %get-tuple-element.37), channel_id=1, source_target_pairs={{0,2},{1,3},{2,4},{3,5},{4,6},{5,7},{6,0},{7,1},{8,10},{9,11},{10,... | collective-permute-start | bytes 98312 | tf_op jit(solution)/shard_map/ppermute | solution.py:344
  59.9 1.0 collective-permute-start.4
  60.9 1.0 collective-permute-start.17
  61.9 1.2 %collective-permute-start.15 = (f32[32,256]{1,0:T(8,128)S(1)}, f32[32,256]{1,0:T(8,128)S(1)}, u32[]{:S(2)}, u32[]{:S(2)}) collective-permute-start(f32[32,256]{1,0:T(8,128)S(1)} %get-tuple-element.26), channel_id=1, source_target_pairs={{0,6},{1,7},{2,0},{3,1},{4,2},{5,3},{6,4},{7,5},{8,14},{9,15},{10,... | collective-permute-start | bytes 98312 | tf_op jit(solution)/shard_map/ppermute | solution.py:344
  63.1 4.6 %collective-permute-start.13 = (f32[32,256]{1,0:T(8,128)S(1)}, f32[32,256]{1,0:T(8,128)S(1)}, u32[]{:S(2)}, u32[]{:S(2)}) collective-permute-start(f32[32,256]{1,0:T(8,128)S(1)} %get-tuple-element.27), channel_id=1, source_target_pairs={{0,5},{1,6},{2,7},{3,0},{4,1},{5,2},{6,3},{7,4},{8,13},{9,14},{10,... | collective-permute-start | bytes 98312 | tf_op jit(solution)/shard_map/ppermute | solution.py:344
  67.7 1.4 %collective-permute-start.11 = (f32[32,256]{1,0:T(8,128)S(1)}, f32[32,256]{1,0:T(8,128)S(1)}, u32[]{:S(2)}, u32[]{:S(2)}) collective-permute-start(f32[32,256]{1,0:T(8,128)S(1)} %get-tuple-element.28), channel_id=1, source_target_pairs={{0,4},{1,5},{2,6},{3,7},{4,0},{5,1},{6,2},{7,3},{8,12},{9,13},{10,... | collective-permute-start | bytes 98312 | tf_op jit(solution)/shard_map/ppermute | solution.py:344
  69.2 4.1 %collective-permute-start.9 = (f32[32,256]{1,0:T(8,128)S(1)}, f32[32,256]{1,0:T(8,128)S(1)}, u32[]{:S(2)}, u32[]{:S(2)}) collective-permute-start(f32[32,256]{1,0:T(8,128)S(1)} %get-tuple-element.29), channel_id=1, source_target_pairs={{0,3},{1,4},{2,5},{3,6},{4,7},{5,0},{6,1},{7,2},{8,11},{9,12},{10,... | collective-permute-start | bytes 98312 | tf_op jit(solution)/shard_map/ppermute | solution.py:344
  73.2 1.1 collective-permute-start.5
  74.3 1.2 %collective-permute-done.11.refs_9_ = f32[32,256]{1,0:T(8,128)S(1)} collective-permute-done((f32[32,256]{1,0:T(8,128)S(1)}, f32[32,256]{1,0:T(8,128)S(1)}, u32[]{:S(2)}, u32[]{:S(2)}) %collective-permute-start.11) | collective-permute-done | bytes 32800 | tf_op jit(solution)/shard_map/ppermute | solution.py:344
  75.6 1.9 %collective-permute-done.9.refs_7_ = f32[32,256]{1,0:T(8,128)S(1)} collective-permute-done((f32[32,256]{1,0:T(8,128)S(1)}, f32[32,256]{1,0:T(8,128)S(1)}, u32[]{:S(2)}, u32[]{:S(2)}) %collective-permute-start.9) | collective-permute-done | bytes 32800 | tf_op jit(solution)/shard_map/ppermute | solution.py:344
  77.5 1.9 %collective-permute-done.7.refs_5_ = f32[32,256]{1,0:T(8,128)S(1)} collective-permute-done((f32[32,256]{1,0:T(8,128)S(1)}, f32[32,256]{1,0:T(8,128)S(1)}, u32[]{:S(2)}, u32[]{:S(2)}) %collective-permute-start.7) | collective-permute-done | bytes 32800 | tf_op jit(solution)/shard_map/ppermute | solution.py:344
  79.4 0.5 gram.1
  79.9 1.9 %collective-permute-start.18 = (f32[32,256]{1,0:T(8,128)S(1)}, f32[32,256]{1,0:T(8,128)S(1)}, u32[]{:S(2)}, u32[]{:S(2)}) collective-permute-start(f32[32,256]{1,0:T(8,128)S(1)} %get-tuple-element.18), channel_id=1, source_target_pairs={{0,4},{1,5},{2,6},{3,7},{4,0},{5,1},{6,2},{7,3},{8,12},{9,13},{10,... | collective-permute-start | bytes 98312 | tf_op jit(solution)/shard_map/ppermute | solution.py:344
  81.8 0.9 collective-permute-start.24
  82.7 1.1 collective-permute-start.23
  83.8 2.7 %collective-permute-start.22 = (f32[32,256]{1,0:T(8,128)S(1)}, f32[32,256]{1,0:T(8,128)S(1)}, u32[]{:S(2)}, u32[]{:S(2)}) collective-permute-start(f32[32,256]{1,0:T(8,128)S(1)} %get-tuple-element.21), channel_id=1, source_target_pairs={{0,2},{1,3},{2,4},{3,5},{4,6},{5,7},{6,0},{7,1},{8,10},{9,11},{10,... | collective-permute-start | bytes 98312 | tf_op jit(solution)/shard_map/ppermute | solution.py:344
  86.5 1.4 %collective-permute-start.21 = (f32[32,256]{1,0:T(8,128)S(1)}, f32[32,256]{1,0:T(8,128)S(1)}, u32[]{:S(2)}, u32[]{:S(2)}) collective-permute-start(f32[32,256]{1,0:T(8,128)S(1)} %get-tuple-element.22), channel_id=1, source_target_pairs={{0,6},{1,7},{2,0},{3,1},{4,2},{5,3},{6,4},{7,5},{8,14},{9,15},{10,... | collective-permute-start | bytes 98312 | tf_op jit(solution)/shard_map/ppermute | solution.py:344
  87.9 0.2 collective-permute-done.18
  88.2 5.1 %collective-permute-start.20 = (f32[32,256]{1,0:T(8,128)S(1)}, f32[32,256]{1,0:T(8,128)S(1)}, u32[]{:S(2)}, u32[]{:S(2)}) collective-permute-start(f32[32,256]{1,0:T(8,128)S(1)} %get-tuple-element.23), channel_id=1, source_target_pairs={{0,3},{1,4},{2,5},{3,6},{4,7},{5,0},{6,1},{7,2},{8,11},{9,12},{10,... | collective-permute-start | bytes 98312 | tf_op jit(solution)/shard_map/ppermute | solution.py:344
  93.3 1.8 %collective-permute-done.20 = f32[32,256]{1,0:T(8,128)S(1)} collective-permute-done((f32[32,256]{1,0:T(8,128)S(1)}, f32[32,256]{1,0:T(8,128)S(1)}, u32[]{:S(2)}, u32[]{:S(2)}) %collective-permute-start.20) | collective-permute-done | bytes 32800 | tf_op jit(solution)/shard_map/ppermute | solution.py:344
  95.1 5.1 %collective-permute-done.19 = f32[32,256]{1,0:T(8,128)S(1)} collective-permute-done((f32[32,256]{1,0:T(8,128)S(1)}, f32[32,256]{1,0:T(8,128)S(1)}, u32[]{:S(2)}, u32[]{:S(2)}) %collective-permute-start.19) | collective-permute-done | bytes 32800 | tf_op jit(solution)/shard_map/ppermute | solution.py:344
  100.2 0.1 collective-permute-start.25
  100.3 1.2 collective-permute-done.25
  101.6 3.9 %collective-permute-done.26 = f32[32,256]{1,0:T(8,128)S(1)} collective-permute-done((f32[32,256]{1,0:T(8,128)S(1)}, f32[32,256]{1,0:T(8,128)S(1)}, u32[]{:S(2)}, u32[]{:S(2)}) %collective-permute-start.26) | collective-permute-done | bytes 32800 | tf_op jit(solution)/shard_map/ppermute | solution.py:375
  105.5 5.4 %collective-permute-done.27 = f32[32,256]{1,0:T(8,128)S(1)} collective-permute-done((f32[32,256]{1,0:T(8,128)S(1)}, f32[32,256]{1,0:T(8,128)S(1)}, u32[]{:S(2)}, u32[]{:S(2)}) %collective-permute-start.27) | collective-permute-done | bytes 32800 | tf_op jit(solution)/shard_map/ppermute | solution.py:375
  110.9 3.9 %collective-permute-done.28 = f32[32,256]{1,0:T(8,128)S(1)} collective-permute-done((f32[32,256]{1,0:T(8,128)S(1)}, f32[32,256]{1,0:T(8,128)S(1)}, u32[]{:S(2)}, u32[]{:S(2)}) %collective-permute-start.28) | collective-permute-done | bytes 32800 | tf_op jit(solution)/shard_map/ppermute | solution.py:375
  114.8 0.8 pad_maximum_fusion
  115.6 4.6 %collective-permute-done.29 = f32[32,256]{1,0:T(8,128)S(1)} collective-permute-done((f32[32,256]{1,0:T(8,128)S(1)}, f32[32,256]{1,0:T(8,128)S(1)}, u32[]{:S(2)}, u32[]{:S(2)}) %collective-permute-start.29) | collective-permute-done | bytes 32800 | tf_op jit(solution)/shard_map/ppermute | solution.py:375
  120.2 0.6 add.47
  (37 shorter events, 0.2 us)
Async XLA Ops:
  1.5 21.7 %collective-permute-start.1 = (f32[32,512]{1,0:T(8,128)S(1)}, f32[32,512]{1,0:T(8,128)S(1)}, u32[]{:S(2)}, u32[]{:S(2)}) collective-permute-start(f32[32,512]{1,0:T(8,128)S(1)} %get-tuple-element.16), channel_id=1, source_target_pairs={{8,0},{16,8},{24,16},{32,24},{40,32},{48,40},{56,48},{64,56},{72,6... | collective-permute-start | bytes 196616 | tf_op jit(solution)/shard_map/ppermute | solution.py:283
  6.2 17.0 %collective-permute-start = (f32[32,512]{1,0:T(8,128)S(1)}, f32[32,512]{1,0:T(8,128)S(1)}, u32[]{:S(2)}, u32[]{:S(2)}) collective-permute-start(f32[32,512]{1,0:T(8,128)S(1)} %get-tuple-element.17), channel_id=1, source_target_pairs={{0,8},{8,16},{16,24},{24,32},{32,40},{40,48},{48,56},{56,64},{64,7... | collective-permute-start | bytes 196616 | tf_op jit(solution)/shard_map/ppermute | solution.py:283
  7.0 1.0 copy-start
  8.1 0.7 copy-start.2
  8.8 0.7 copy-start.3
  9.4 13.8 %copy-start.1 = (f32[32,4096]{1,0:T(8,128)S(1)}, f32[32,4096]{1,0:T(8,128)}, u32[]{:S(2)}) copy-start(f32[32,4096]{1,0:T(8,128)} %field.7) | copy-start | bytes 1572868
  29.3 12.7 %collective-permute-start.2 = (f32[32,512]{1,0:T(8,128)S(1)}, f32[32,512]{1,0:T(8,128)S(1)}, u32[]{:S(2)}, u32[]{:S(2)}) collective-permute-start(f32[32,512]{1,0:T(8,128)S(1)} %get-tuple-element.9.high), channel_id=1, source_target_pairs={{0,8},{8,16},{16,24},{24,32},{32,40},{40,48},{48,56},{56,64},{64,7... | collective-permute-start | bytes 196616 | tf_op jit(solution)/shard_map/ppermute | solution.py:283
  29.4 17.1 %collective-permute-start.3 = (f32[32,512]{1,0:T(8,128)S(1)}, f32[32,512]{1,0:T(8,128)S(1)}, u32[]{:S(2)}, u32[]{:S(2)}) collective-permute-start(f32[32,512]{1,0:T(8,128)S(1)} %get-tuple-element.10.low), channel_id=1, source_target_pairs={{8,0},{16,8},{24,16},{32,24},{40,32},{48,40},{56,48},{64,56},{72,6... | collective-permute-start | bytes 196616 | tf_op jit(solution)/shard_map/ppermute | solution.py:283
  34.6 22.3 %collective-permute-start.16 = (f32[32,256]{1,0:T(8,128)S(1)}, f32[32,256]{1,0:T(8,128)S(1)}, u32[]{:S(2)}, u32[]{:S(2)}) collective-permute-start(f32[32,256]{1,0:T(8,128)S(1)} %get-tuple-element.32), channel_id=1, source_target_pairs={{0,7},{1,0},{2,1},{3,2},{4,3},{5,4},{6,5},{7,6},{8,15},{9,8},{10,9... | collective-permute-start | bytes 98312 | tf_op jit(solution)/shard_map/ppermute | solution.py:344
  34.8 25.1 %collective-permute-start.14 = (f32[32,256]{1,0:T(8,128)S(1)}, f32[32,256]{1,0:T(8,128)S(1)}, u32[]{:S(2)}, u32[]{:S(2)}) collective-permute-start(f32[32,256]{1,0:T(8,128)S(1)} %get-tuple-element.33), channel_id=1, source_target_pairs={{0,6},{1,7},{2,0},{3,1},{4,2},{5,3},{6,4},{7,5},{8,14},{9,15},{10,... | collective-permute-start | bytes 98312 | tf_op jit(solution)/shard_map/ppermute | solution.py:344
  41.1 19.8 %collective-permute-start.12 = (f32[32,256]{1,0:T(8,128)S(1)}, f32[32,256]{1,0:T(8,128)S(1)}, u32[]{:S(2)}, u32[]{:S(2)}) collective-permute-start(f32[32,256]{1,0:T(8,128)S(1)} %get-tuple-element.34), channel_id=1, source_target_pairs={{0,5},{1,6},{2,7},{3,0},{4,1},{5,2},{6,3},{7,4},{8,13},{9,14},{10,... | collective-permute-start | bytes 98312 | tf_op jit(solution)/shard_map/ppermute | solution.py:344
  42.0 19.9 %collective-permute-start.10 = (f32[32,256]{1,0:T(8,128)S(1)}, f32[32,256]{1,0:T(8,128)S(1)}, u32[]{:S(2)}, u32[]{:S(2)}) collective-permute-start(f32[32,256]{1,0:T(8,128)S(1)} %get-tuple-element.35), channel_id=1, source_target_pairs={{0,4},{1,5},{2,6},{3,7},{4,0},{5,1},{6,2},{7,3},{8,12},{9,13},{10,... | collective-permute-start | bytes 98312 | tf_op jit(solution)/shard_map/ppermute | solution.py:344
  46.5 16.6 %collective-permute-start.8 = (f32[32,256]{1,0:T(8,128)S(1)}, f32[32,256]{1,0:T(8,128)S(1)}, u32[]{:S(2)}, u32[]{:S(2)}) collective-permute-start(f32[32,256]{1,0:T(8,128)S(1)} %get-tuple-element.36), channel_id=1, source_target_pairs={{0,3},{1,4},{2,5},{3,6},{4,7},{5,0},{6,1},{7,2},{8,11},{9,12},{10,... | collective-permute-start | bytes 98312 | tf_op jit(solution)/shard_map/ppermute | solution.py:344
  56.9 10.8 %collective-permute-start.6 = (f32[32,256]{1,0:T(8,128)S(1)}, f32[32,256]{1,0:T(8,128)S(1)}, u32[]{:S(2)}, u32[]{:S(2)}) collective-permute-start(f32[32,256]{1,0:T(8,128)S(1)} %get-tuple-element.37), channel_id=1, source_target_pairs={{0,2},{1,3},{2,4},{3,5},{4,6},{5,7},{6,0},{7,1},{8,10},{9,11},{10,... | collective-permute-start | bytes 98312 | tf_op jit(solution)/shard_map/ppermute | solution.py:344
  59.9 9.3 %collective-permute-start.4 = (f32[32,256]{1,0:T(8,128)S(1)}, f32[32,256]{1,0:T(8,128)S(1)}, u32[]{:S(2)}, u32[]{:S(2)}) collective-permute-start(f32[32,256]{1,0:T(8,128)S(1)} %get-tuple-element.38), channel_id=1, source_target_pairs={{0,1},{1,2},{2,3},{3,4},{4,5},{5,6},{6,7},{7,0},{8,9},{9,10},{10,1... | collective-permute-start | bytes 98312 | tf_op jit(solution)/shard_map/ppermute | solution.py:344
  60.9 12.3 %collective-permute-start.17 = (f32[32,256]{1,0:T(8,128)S(1)}, f32[32,256]{1,0:T(8,128)S(1)}, u32[]{:S(2)}, u32[]{:S(2)}) collective-permute-start(f32[32,256]{1,0:T(8,128)S(1)} %get-tuple-element.25), channel_id=1, source_target_pairs={{0,7},{1,0},{2,1},{3,2},{4,3},{5,4},{6,5},{7,6},{8,15},{9,8},{10,9... | collective-permute-start | bytes 98312 | tf_op jit(solution)/shard_map/ppermute | solution.py:344
  61.9 11.3 %collective-permute-start.15 = (f32[32,256]{1,0:T(8,128)S(1)}, f32[32,256]{1,0:T(8,128)S(1)}, u32[]{:S(2)}, u32[]{:S(2)}) collective-permute-start(f32[32,256]{1,0:T(8,128)S(1)} %get-tuple-element.26), channel_id=1, source_target_pairs={{0,6},{1,7},{2,0},{3,1},{4,2},{5,3},{6,4},{7,5},{8,14},{9,15},{10,... | collective-permute-start | bytes 98312 | tf_op jit(solution)/shard_map/ppermute | solution.py:344
  63.1 11.2 %collective-permute-start.13 = (f32[32,256]{1,0:T(8,128)S(1)}, f32[32,256]{1,0:T(8,128)S(1)}, u32[]{:S(2)}, u32[]{:S(2)}) collective-permute-start(f32[32,256]{1,0:T(8,128)S(1)} %get-tuple-element.27), channel_id=1, source_target_pairs={{0,5},{1,6},{2,7},{3,0},{4,1},{5,2},{6,3},{7,4},{8,13},{9,14},{10,... | collective-permute-start | bytes 98312 | tf_op jit(solution)/shard_map/ppermute | solution.py:344
  67.7 7.8 %collective-permute-start.11 = (f32[32,256]{1,0:T(8,128)S(1)}, f32[32,256]{1,0:T(8,128)S(1)}, u32[]{:S(2)}, u32[]{:S(2)}) collective-permute-start(f32[32,256]{1,0:T(8,128)S(1)} %get-tuple-element.28), channel_id=1, source_target_pairs={{0,4},{1,5},{2,6},{3,7},{4,0},{5,1},{6,2},{7,3},{8,12},{9,13},{10,... | collective-permute-start | bytes 98312 | tf_op jit(solution)/shard_map/ppermute | solution.py:344
  69.2 8.3 %collective-permute-start.9 = (f32[32,256]{1,0:T(8,128)S(1)}, f32[32,256]{1,0:T(8,128)S(1)}, u32[]{:S(2)}, u32[]{:S(2)}) collective-permute-start(f32[32,256]{1,0:T(8,128)S(1)} %get-tuple-element.29), channel_id=1, source_target_pairs={{0,3},{1,4},{2,5},{3,6},{4,7},{5,0},{6,1},{7,2},{8,11},{9,12},{10,... | collective-permute-start | bytes 98312 | tf_op jit(solution)/shard_map/ppermute | solution.py:344
  73.2 6.1 %collective-permute-start.7 = (f32[32,256]{1,0:T(8,128)S(1)}, f32[32,256]{1,0:T(8,128)S(1)}, u32[]{:S(2)}, u32[]{:S(2)}) collective-permute-start(f32[32,256]{1,0:T(8,128)S(1)} %get-tuple-element.30), channel_id=1, source_target_pairs={{0,2},{1,3},{2,4},{3,5},{4,6},{5,7},{6,0},{7,1},{8,10},{9,11},{10,... | collective-permute-start | bytes 98312 | tf_op jit(solution)/shard_map/ppermute | solution.py:344
  73.2 6.1 %collective-permute-start.5 = (f32[32,256]{1,0:T(8,128)S(1)}, f32[32,256]{1,0:T(8,128)S(1)}, u32[]{:S(2)}, u32[]{:S(2)}) collective-permute-start(f32[32,256]{1,0:T(8,128)S(1)} %get-tuple-element.31), channel_id=1, source_target_pairs={{0,1},{1,2},{2,3},{3,4},{4,5},{5,6},{6,7},{7,0},{8,9},{9,10},{10,1... | collective-permute-start | bytes 98312 | tf_op jit(solution)/shard_map/ppermute | solution.py:344
  79.9 8.3 %collective-permute-start.18 = (f32[32,256]{1,0:T(8,128)S(1)}, f32[32,256]{1,0:T(8,128)S(1)}, u32[]{:S(2)}, u32[]{:S(2)}) collective-permute-start(f32[32,256]{1,0:T(8,128)S(1)} %get-tuple-element.18), channel_id=1, source_target_pairs={{0,4},{1,5},{2,6},{3,7},{4,0},{5,1},{6,2},{7,3},{8,12},{9,13},{10,... | collective-permute-start | bytes 98312 | tf_op jit(solution)/shard_map/ppermute | solution.py:344
  81.8 11.5 %collective-permute-start.24 = (f32[32,256]{1,0:T(8,128)S(1)}, f32[32,256]{1,0:T(8,128)S(1)}, u32[]{:S(2)}, u32[]{:S(2)}) collective-permute-start(f32[32,256]{1,0:T(8,128)S(1)} %get-tuple-element.19), channel_id=1, source_target_pairs={{0,1},{1,2},{2,3},{3,4},{4,5},{5,6},{6,7},{7,0},{8,9},{9,10},{10,1... | collective-permute-start | bytes 98312 | tf_op jit(solution)/shard_map/ppermute | solution.py:344
  82.7 10.6 %collective-permute-start.23 = (f32[32,256]{1,0:T(8,128)S(1)}, f32[32,256]{1,0:T(8,128)S(1)}, u32[]{:S(2)}, u32[]{:S(2)}) collective-permute-start(f32[32,256]{1,0:T(8,128)S(1)} %get-tuple-element.20), channel_id=1, source_target_pairs={{0,7},{1,0},{2,1},{3,2},{4,3},{5,4},{6,5},{7,6},{8,15},{9,8},{10,9... | collective-permute-start | bytes 98312 | tf_op jit(solution)/shard_map/ppermute | solution.py:344
  83.8 9.5 %collective-permute-start.22 = (f32[32,256]{1,0:T(8,128)S(1)}, f32[32,256]{1,0:T(8,128)S(1)}, u32[]{:S(2)}, u32[]{:S(2)}) collective-permute-start(f32[32,256]{1,0:T(8,128)S(1)} %get-tuple-element.21), channel_id=1, source_target_pairs={{0,2},{1,3},{2,4},{3,5},{4,6},{5,7},{6,0},{7,1},{8,10},{9,11},{10,... | collective-permute-start | bytes 98312 | tf_op jit(solution)/shard_map/ppermute | solution.py:344
  86.5 6.8 %collective-permute-start.21 = (f32[32,256]{1,0:T(8,128)S(1)}, f32[32,256]{1,0:T(8,128)S(1)}, u32[]{:S(2)}, u32[]{:S(2)}) collective-permute-start(f32[32,256]{1,0:T(8,128)S(1)} %get-tuple-element.22), channel_id=1, source_target_pairs={{0,6},{1,7},{2,0},{3,1},{4,2},{5,3},{6,4},{7,5},{8,14},{9,15},{10,... | collective-permute-start | bytes 98312 | tf_op jit(solution)/shard_map/ppermute | solution.py:344
  88.2 7.0 %collective-permute-start.20 = (f32[32,256]{1,0:T(8,128)S(1)}, f32[32,256]{1,0:T(8,128)S(1)}, u32[]{:S(2)}, u32[]{:S(2)}) collective-permute-start(f32[32,256]{1,0:T(8,128)S(1)} %get-tuple-element.23), channel_id=1, source_target_pairs={{0,3},{1,4},{2,5},{3,6},{4,7},{5,0},{6,1},{7,2},{8,11},{9,12},{10,... | collective-permute-start | bytes 98312 | tf_op jit(solution)/shard_map/ppermute | solution.py:344
  93.3 6.9 %collective-permute-start.19 = (f32[32,256]{1,0:T(8,128)S(1)}, f32[32,256]{1,0:T(8,128)S(1)}, u32[]{:S(2)}, u32[]{:S(2)}) collective-permute-start(f32[32,256]{1,0:T(8,128)S(1)} %get-tuple-element.24), channel_id=1, source_target_pairs={{0,5},{1,6},{2,7},{3,0},{4,1},{5,2},{6,3},{7,4},{8,13},{9,14},{10,... | collective-permute-start | bytes 98312 | tf_op jit(solution)/shard_map/ppermute | solution.py:344
  100.2 1.3 %collective-permute-start.25 = (f32[32,256]{1,0:T(8,128)S(1)}, f32[32,256]{1,0:T(8,128)S(1)}, u32[]{:S(2)}, u32[]{:S(2)}) collective-permute-start(f32[32,256]{1,0:T(8,128)S(1)} %fusion.6), channel_id=1, source_target_pairs={{0,8},{8,0},{16,24},{24,16},{32,40},{40,32},{48,56},{56,48},{64,72... | collective-permute-start | bytes 98312 | tf_op jit(solution)/shard_map/ppermute | solution.py:375
  101.5 3.9 %collective-permute-start.26 = (f32[32,256]{1,0:T(8,128)S(1)}, f32[32,256]{1,0:T(8,128)S(1)}, u32[]{:S(2)}, u32[]{:S(2)}) collective-permute-start(f32[32,256]{1,0:T(8,128)S(1)} %add.43), channel_id=1, source_target_pairs={{0,16},{8,24},{16,0},{24,8},{32,48},{40,56},{48,32},{56,40},{64,80... | collective-permute-start | bytes 98312 | tf_op jit(solution)/shard_map/ppermute | solution.py:375
  105.5 5.4 %collective-permute-start.27 = (f32[32,256]{1,0:T(8,128)S(1)}, f32[32,256]{1,0:T(8,128)S(1)}, u32[]{:S(2)}, u32[]{:S(2)}) collective-permute-start(f32[32,256]{1,0:T(8,128)S(1)} %add.44), channel_id=1, source_target_pairs={{0,32},{8,40},{16,48},{24,56},{32,0},{40,8},{48,16},{56,24},{64,96... | collective-permute-start | bytes 98312 | tf_op jit(solution)/shard_map/ppermute | solution.py:375
  110.9 3.9 %collective-permute-start.28 = (f32[32,256]{1,0:T(8,128)S(1)}, f32[32,256]{1,0:T(8,128)S(1)}, u32[]{:S(2)}, u32[]{:S(2)}) collective-permute-start(f32[32,256]{1,0:T(8,128)S(1)} %add.45), channel_id=1, source_target_pairs={{0,64},{8,72},{16,80},{24,88},{32,96},{40,104},{48,112},{56,120},{... | collective-permute-start | bytes 98312 | tf_op jit(solution)/shard_map/ppermute | solution.py:375
  114.8 5.4 %collective-permute-start.29 = (f32[32,256]{1,0:T(8,128)S(1)}, f32[32,256]{1,0:T(8,128)S(1)}, u32[]{:S(2)}, u32[]{:S(2)}) collective-permute-start(f32[32,256]{1,0:T(8,128)S(1)} %add.46), channel_id=1, source_target_pairs={{0,128},{8,136},{16,144},{24,152},{32,160},{40,168},{48,176},{56,1... | collective-permute-start | bytes 98312 | tf_op jit(solution)/shard_map/ppermute | solution.py:375

commit v2 on v0

v2 whole, which is shorter than its diff:
```python
import functools

import jax
import jax.numpy as jnp
from jax import lax
from jax.experimental import pallas as pl
from jax.experimental.pallas import tpu as pltpu
from jax.sharding import PartitionSpec as P

REACH = 4
BLOCK = 128

filter_center = 1.0
filter_half = 2.0

f32, bf16 = jnp.float32, jnp.bfloat16
VMEM = pl.BlockSpec(memory_space=pltpu.VMEM)
SMEM = pl.BlockSpec(memory_space=pltpu.SMEM)
HBM = pl.BlockSpec(memory_space=pltpu.HBM)
NT = (((1,), (1,)), ((), ()))


def halves(x):
    high = x.astype(bf16)
    return high, (x - high.astype(f32)).astype(bf16)


def load_blocks(table, pieces):
    vcount = table.shape[1] // 2
    for ref, block, slot, blocks in pieces:
        for b in range(blocks):
            high, low = halves(ref[:, (block + b) * BLOCK : (block + b + 1) * BLOCK])
            table[slot + b, 0:vcount] = high
            table[slot + b, vcount : 2 * vcount] = low
    table[table.shape[0] - 1] = jnp.zeros(table.shape[1:], bf16)


def columns(ref, block):
    return ref[:, pl.ds(pl.multiple_of(block * BLOCK, BLOCK), BLOCK)]


def set_columns(ref, block, value):
    ref[:, pl.ds(pl.multiple_of(block * BLOCK, BLOCK), BLOCK)] = value


def row_product(row, nblocks, cols, counts, table, h):
    slots = h.shape[1]
    here = cols[0, row]
    used = counts[row]
    picked = []
    for k in range(slots):
        shift = cols[k, row] - here
        shift = jnp.where(shift > REACH, shift - nblocks, shift)
        shift = jnp.where(shift < -REACH, shift + nblocks, shift)
        picked.append(table[jnp.where(k < used, row + shift + REACH, table.shape[0] - 1)])
    left = jnp.concatenate(picked, axis=1)
    split = [halves(h[row, k]) for k in range(slots)]
    right = jnp.concatenate(
        [
            jnp.concatenate([high for high, _ in split], axis=1),
            jnp.concatenate([low for _, low in split], axis=1),
        ],
        axis=0,
    )
    both = lax.dot_general(left, right, NT, preferred_element_type=f32)
    v = left.shape[0] // 2
    return (both[:v, :BLOCK] + both[:v, BLOCK:]) + (both[v:, :BLOCK] + both[v:, BLOCK:])


def first_value(row, total, onsite, field):
    diag = onsite[pl.ds(row, 1), :] - filter_center
    return (total + diag * columns(field, row)) / filter_half


def first_inner(
    nblocks, local, cols_hbm, counts_hbm, onsite_hbm, field_hbm, h_hbm,
    cols, counts, h, field, onsite, out, table, sems, small,
):
    count = local - 2 * REACH
    unroll = 4

    def fetch(row):
        return pltpu.make_async_copy(h_hbm.at[row], h.at[row], sems.at[row])

    copies = [
        pltpu.make_async_copy(a, b, small.at[n])
        for n, (a, b) in enumerate(
            [(field_hbm, field), (cols_hbm, cols), (counts_hbm, counts), (onsite_hbm, onsite)]
        )
    ]
    for copy in copies:
        copy.start()

    def begin(i, carry):
        fetch(lax.rem(i + REACH, local)).start()
        return carry

    lax.fori_loop(0, local, begin, 0)
    for copy in copies:
        copy.wait()
    load_blocks(table, [(field, 0, REACH, local)])

    def step(s, carry):
        for u in range(unroll):
            fetch(s * unroll + u + REACH).wait()
        for u in range(unroll):
            i = s * unroll + u
            row = i + REACH
            total = row_product(row, nblocks, cols, counts, table, h)
            set_columns(out, i, first_value(row, total, onsite, field))
        return carry

    lax.fori_loop(0, count // unroll, step, 0)

    def rest(i, carry):
        fetch(lax.rem(i + local - REACH, local)).wait()
        return carry

    lax.fori_loop(0, 2 * REACH, rest, 0)


def first_edge(nblocks, local, cols, counts, onsite, before, field, after, h, out, table):
    load_blocks(
        table,
        [
            (before, 0, 0, REACH),
            (field, 0, REACH, 2 * REACH),
            (field, local - 2 * REACH, local - REACH, 2 * REACH),
            (after, 0, local + REACH, REACH),
        ],
    )
    unroll = 4

    def step(s, carry):
        for u in range(unroll):
            i = s * unroll + u
            row = jnp.where(i < REACH, i, i + local - 2 * REACH)
            total = row_product(row, nblocks, cols, counts, table, h)
            set_columns(out, i, first_value(row, total, onsite, field))
        return carry

    lax.fori_loop(0, 2 * REACH // unroll, step, 0)


def second_value(row, total, onsite, first, field):
    diag = onsite[pl.ds(row, 1), :] - filter_center
    return 2.0 * (total + diag * first) / filter_half - columns(field, row)


def second_inner(nblocks, local, cols, counts, onsite, edge, inner, field, h, out, table):
    load_blocks(
        table,
        [
            (edge, 0, REACH, REACH),
            (inner, 0, 2 * REACH, local - 2 * REACH),
            (edge, REACH, local, REACH),
        ],
    )
    unroll = 4

    def step(s, carry):
        for u in range(unroll):
            i = s * unroll + u
            row = i + REACH
            total = row_product(row, nblocks, cols, counts, table, h)
            set_columns(out, i, second_value(row, total, onsite, columns(inner, i), field))
        return carry

    lax.fori_loop(0, (local - 2 * REACH) // unroll, step, 0)


def second_edge(
    nblocks, local, groups, cols, counts, onsite, before, edge, inner, after, field, done, h,
    out, parts, table,
):
    load_blocks(
        table,
        [
            (before, 0, 0, REACH),
            (edge, 0, REACH, REACH),
            (inner, 0, 2 * REACH, REACH),
            (inner, local - 3 * REACH, local - REACH, REACH),
            (edge, REACH, local, REACH),
            (after, 0, local + REACH, REACH),
        ],
    )
    out[:, REACH * BLOCK : (local - REACH) * BLOCK] = done[...]
    unroll = 4

    def step(s, carry):
        for u in range(unroll):
            i = s * unroll + u
            row = jnp.where(i < REACH, i, i + local - 2 * REACH)
            total = row_product(row, nblocks, cols, counts, table, h)
            set_columns(out, row, second_value(row, total, onsite, columns(edge, i), field))
        return carry

    lax.fori_loop(0, 2 * REACH // unroll, step, 0)
    where = lax.axis_index("cols")
    width = parts.shape[2]
    for k in range(groups):
        place = lax.rem(where + k, groups) * width
        parts[k] = out[:, pl.ds(pl.multiple_of(place, width), width)]


def gram(groups, scale, own, *refs):
    got = refs[: groups - 1]
    keep, give, high, low, both = refs[groups - 1 :]
    vcount = own.shape[1]
    where = lax.axis_index("cols")
    core = lax.rem(lax.axis_index("rows"), 2)

    def place(k):
        return pl.multiple_of(lax.rem(where + k, groups) * vcount, vcount)

    for k in range(groups):
        a, b = halves(own[0] if k == 0 else got[k - 1][...])
        at = place(groups - k)
        high[pl.ds(at, vcount), :] = a
        low[pl.ds(at, vcount), :] = b
    a, b = high[...], low[...]
    both[...] = (
        lax.dot_general(a, a, NT, preferred_element_type=f32)
        + lax.dot_general(a, b, NT, preferred_element_type=f32)
        + lax.dot_general(b, a, NT, preferred_element_type=f32)
    ) * scale
    half = groups // 2
    for j in range(half):
        even, odd = (half, 0) if j == 0 else (j, groups - j)
        keep[j] = both[pl.ds(place(jnp.where(core == 0, even, odd)), vcount), :]
        give[j] = both[pl.ds(place(jnp.where(core == 0, odd, even)), vcount), :]


def params(mebibytes):
    return pltpu.CompilerParams(vmem_limit_bytes=mebibytes * 1024 * 1024)


def cost(rows, slots, vcount):
    return pl.CostEstimate(
        flops=rows * slots * BLOCK * BLOCK * vcount * 2 * 4,
        bytes_accessed=rows * slots * BLOCK * BLOCK * 4,
        transcendentals=0,
    )


def on_device(vectors, onsite, h_blocks, block_cols, block_counts):
    vcount, width = vectors.shape
    local, slots = block_cols.shape
    ranks = lax.axis_size("rows")
    groups = lax.axis_size("cols")
    nblocks = local * ranks
    reach = REACH * BLOCK
    edge_rows, inner_rows = 2 * REACH, local - 2 * REACH
    cols = block_cols.T
    onsite = onsite.reshape(local, BLOCK)

    def shape(*dims):
        return jax.ShapeDtypeStruct(dims, f32)

    table = pltpu.VMEM((local + 2 * REACH + 1, 2 * vcount, BLOCK), bf16)
    up = [(i, (i + 1) % ranks) for i in range(ranks)]
    down = [(j, i) for i, j in up]

    def around(low, high):
        return lax.ppermute(high, "rows", up), lax.ppermute(low, "rows", down)

    before, after = around(vectors[:, :reach], vectors[:, width - reach :])

    cols, counts, h, field, onsite, inner = pl.pallas_call(
        functools.partial(first_inner, nblocks, local),
        in_specs=[HBM] * 5,
        out_specs=(SMEM,) * 2 + (VMEM,) * 4,
        out_shape=(
            pltpu.SMEM(cols.shape, jnp.int32),
            pltpu.SMEM(block_counts.shape, jnp.int32),
            pltpu.VMEM(h_blocks.shape, f32),
            pltpu.VMEM(vectors.shape, f32),
            pltpu.VMEM(onsite.shape, f32),
            pltpu.VMEM((vcount, inner_rows * BLOCK), f32),
        ),
        scratch_shapes=[
            table,
            pltpu.SemaphoreType.DMA((local,)),
            pltpu.SemaphoreType.DMA((4,)),
        ],
        compiler_params=params(8),
        cost_estimate=cost(local, slots, vcount),
        name="first_inner",
    )(*[pltpu.with_memory_space_constraint(x, pltpu.HBM) for x in (cols, block_counts, onsite, vectors, h_blocks)])

    edge = pl.pallas_call(
        functools.partial(first_edge, nblocks, local),
        in_specs=[SMEM, SMEM] + [VMEM] * 5,
        out_specs=VMEM,
        out_shape=shape(vcount, edge_rows * BLOCK),
        scratch_shapes=[table],
        compiler_params=params(8),
        cost_estimate=cost(edge_rows, slots, vcount),
        name="first_edge",
    )(cols, counts, onsite, before, field, after, h)

    before, after = around(edge[:, :reach], edge[:, reach:])

    done = pl.pallas_call(
        functools.partial(second_inner, nblocks, local),
        in_specs=[SMEM, SMEM] + [VMEM] * 5,
        out_specs=VMEM,
        out_shape=shape(vcount, inner_rows * BLOCK),
        scratch_shapes=[table],
        compiler_params=params(8),
        cost_estimate=cost(inner_rows, slots, vcount),
        name="second_inner",
    )(cols, counts, onsite, edge, inner, field, h)

    filtered, parts = pl.pallas_call(
        functools.partial(second_edge, nblocks, local, groups),
        in_specs=[SMEM, SMEM] + [VMEM] * 8,
        out_specs=(VMEM, VMEM),
        out_shape=(shape(vcount, width), shape(groups, vcount, width // groups)),
        scratch_shapes=[table],
        compiler_params=params(8),
        cost_estimate=cost(edge_rows, slots, vcount),
        name="second_edge",
    )(cols, counts, onsite, before, edge, inner, after, field, done, h)

    order = sorted(range(1, groups), key=lambda k: -min(k, groups - k))
    got = {}
    for k in order:
        pairs = [(i, (i + k) % groups) for i in range(groups)]
        got[k] = lax.ppermute(parts[k], "cols", pairs)
    total = vcount * groups
    half = groups // 2
    keep, give = pl.pallas_call(
        functools.partial(gram, groups, 1.0 / (width * ranks)),
        in_specs=[VMEM] * groups,
        out_specs=(VMEM, VMEM),
        out_shape=(shape(half, vcount, total), shape(half, vcount, total)),
        scratch_shapes=[
            pltpu.VMEM((total, width // groups), bf16),
            pltpu.VMEM((total, width // groups), bf16),
            pltpu.VMEM((total, total), f32),
        ],
        compiler_params=params(8),
        name="gram",
    )(parts, *[got[k] for k in range(1, groups)])

    keep = keep + lax.ppermute(give, "rows", [(i, i ^ 1) for i in range(ranks)])
    terms = []
    for j in range(half):
        pairs = []
        for r in range(ranks):
            shift = (half if j == 0 else j) if r % 2 == 0 else -j
            pairs += [(r * groups + z, r * groups + (z + shift) % groups) for z in range(groups)]
        terms.append(lax.ppermute(keep[j], ("rows", "cols"), pairs))
    mine = sum(terms[1:], terms[0])

    side = 4
    for stride in (2, 2 * side):
        terms = []
        for k in range(1, side):
            pairs = []
            for r in range(ranks):
                at = r // stride % side
                pairs.append((r, r + ((at + k) % side - at) * stride))
            terms.append(lax.ppermute(mine, "rows", pairs))
        mine = sum(terms, mine)
    mine = mine + lax.ppermute(mine, "rows", [(i, i ^ 1) for i in range(ranks)])
    return (filtered, mine)


def solution(mesh):
    return jax.shard_map(
        on_device,
        mesh=mesh,
        in_specs=(
            P("cols", "rows"),
            P("rows"),
            P("rows", None, None, None),
            P("rows", None),
            P("rows"),
        ),
        out_specs=(P("cols", "rows"), P("cols", None)),
        check_vma=False,
    )
```

time: 274 us -> 87.1 us (0.32)
  blocking collectives: 123 us -> 0 us
  matrix products: 51.6 us -> 0 us
  waiting for transfers between devices: 63.4 us -> 17.9 us
  starting transfers between devices: 7.66 us -> 49.4 us
  Pallas kernels: 0 us -> 17.2 us
  between operations: 14.1 us -> 0.78 us
  local copies, waits for them, and re-layouts: 7.7 us -> 0.94 us
  other arithmetic: 3.68 us -> 0.67 us
    psum x1 -> x0, blocking collectives: 123 us -> none  [on_device(): correlation = lax.psum(partial_gram, 'rows')]
    all_gather x1 -> x0, waiting for transfers between devices: 61.1 us -> none  [on_device(): everyone = lax.all_gather(filtered, 'cols', axis=0, tiled=True)]
    dot_general x3 -> x0, matrix products: 51.6 us -> none  [the longest x2 45.6 us: apply_hamiltonian(): jnp.einsum('vrkj,rkij->vri', picked, h_blocks, precision=lax.Precision.HI...]
    ppermute x4 -> x23, starting transfers between devices: 7.62 us -> 49.4 us  [the longest x7 15.3 us: on_device(): got[k] = lax.ppermute(parts[k], 'cols', pairs)]
    pallas_call x0 -> x5, Pallas kernels: none -> 17.2 us  [the longest x1 7.3 us: on_device(): pl.pallas_call(functools.partial(first_inner, nblocks, local), in_specs=[...]
    ppermute x4 -> x23, waiting for transfers between devices: 2.29 us -> 17.9 us  [the longest x6 7.87 us: on_device(): terms.append(lax.ppermute(mine, 'rows', pairs))]
    gather x2 -> x0, local copies, waits for them, and re-layouts: 6.6 us -> none  [apply_hamiltonian(): picked = source[:, where_cols, :] * weight[None, :, :, None]]
  transfers between devices with their start and end apart: 5 -> 23, of which waited for: 4 -> 12; matrix products, arithmetic and copies ran while one was open for 1% -> 0% of each run, Pallas kernels for 0% -> 14%
where the time goes in v2:
time: 87.1 us; the launch traced here: 87 us
  starting transfers between devices  49.4 us (57%)
  waiting for transfers between devices  17.9 us (21%)
  Pallas kernels  17.2 us (20%)
  local copies, waits for them, and re-layouts  0.94 us (1%)
    ppermute x7, starting transfers between devices, on_device(): got[k] = lax.ppermute(parts[k], 'cols', pairs)  15.3 us
    ppermute x1, starting transfers between devices, on_device(): mine = mine + lax.ppermute(mine, 'rows', [(i, i ^ 1) for i in range(ranks)])  9.95 us
    ppermute x1, starting transfers between devices, on_device(): keep = keep + lax.ppermute(give, 'rows', [(i, i ^ 1) for i in range(ranks)])  8.62 us
    ppermute x6, waiting for transfers between devices, on_device(): terms.append(lax.ppermute(mine, 'rows', pairs))  7.87 us
    pallas_call x1, Pallas kernels, on_device(): pl.pallas_call(functools.partial(first_inner, nblocks, local), in_specs=[...  7.3 us
    ppermute x4, starting transfers between devices, around(): return (lax.ppermute(high, 'rows', up), lax.ppermute(low, 'rows', down))  6.31 us
    pallas_call x1, Pallas kernels, on_device(): pl.pallas_call(functools.partial(second_inner, nblocks, local), in_specs=...  5.14 us
    ppermute x4, starting transfers between devices, on_device(): terms.append(lax.ppermute(keep[j], ('rows', 'cols'), pairs))  4.95 us
  transfers between devices with their start and end apart: 23, of which 12 were waited for; matrix products, arithmetic and copies ran while one was open for 0% of the time, Pallas kernels for 14%

profile of v2, /device:TPU:1, one launch (start us, length us, event | category | flops | bytes accessed | tf_op | source)
XLA Modules:
  0.0 87.0 jit_solution(13578316586626817508)
XLA Ops:
  0.6 0.9 %fusion = (f32[32,512]{1,0:T(8,128)S(1)}, f32[32,512]{1,0:T(8,128)S(1)}) fusion(f32[32,4096]{1,0:T(8,128)} %field_hbm.1), kind=kLoop, calls=%fused_computation.14 | loop fusion | bytes 262144 | tf_op jit(solution)/shard_map/slice | solution.py:267
  1.5 3.3 %collective-permute-start.1 = (f32[32,512]{1,0:T(8,128)S(1)}, f32[32,512]{1,0:T(8,128)S(1)}, u32[]{:S(2)}, u32[]{:S(2)}) collective-permute-start(f32[32,512]{1,0:T(8,128)S(1)} %get-tuple-element.29), channel_id=1, source_target_pairs={{8,0},{16,8},{24,16},{32,24},{40,32},{48,40},{56,48},{64,56},{72,6... | collective-permute-start | bytes 196616 | tf_op jit(solution)/shard_map/ppermute | solution.py:265
  4.8 7.3 %first_inner.1 = (s32[9,32]{1,0:T(8,128)S(4)}, s32[32]{0:T(128)S(4)}, f32[32,9,128,128]{3,2,1,0:T(8,128)S(1)}, f32[32,4096]{1,0:T(8,128)S(1)}, f32[32,128]{1,0:T(8,128)S(1)}, /*index=5*/f32[32,3072]{1,0:T(8,128)S(1)}) custom-call(s32[9,32]{1,0:T(8,128)} %bitcast.25, s32[32]{0:T(128)} %counts_hbm.1, f32[32,128]{1,0:T(8,128)} %bitcast.24, ...), custom_call_target="tpu_custom_call" | custom-call | flops 1207959552 | bytes 18874368 | tf_op jit(solution)/shard_map/first_inner/pallas_call | solution.py:269
  12.1 0.0 collective-permute-done.1.after
  12.2 0.0 collective-permute-done.before
  12.2 1.7 %first_edge.1.edge = f32[32,1024]{1,0:T(8,128)S(1)} custom-call(s32[9,32]{1,0:T(8,128)S(4)} %get-tuple-element.12.cols, s32[32]{0:T(128)S(4)} %get-tuple-element.13.counts, f32[32,128]{1,0:T(8,128)S(1)} %get-tuple-element.14.onsite, f32[32,512]{1,0:T(8,128)S(1)} %collective-permute-done.before, f32[32,4096]{1,0:T(8,128)S(1)} %get-tuple-element.15.field, ...), custom_call_target="tpu_custom_call" | custom-call | flops 301989888 | bytes 4718592 | tf_op jit(solution)/shard_map/first_edge/pallas_call | solution.py:291
  13.9 3.0 %collective-permute-start.3 = (f32[32,512]{1,0:T(8,128)S(1)}, f32[32,512]{1,0:T(8,128)S(1)}, u32[]{:S(2)}, u32[]{:S(2)}) collective-permute-start(f32[32,512]{1,0:T(8,128)S(1)} %get-tuple-element.35), channel_id=1, source_target_pairs={{8,0},{16,8},{24,16},{32,24},{40,32},{48,40},{56,48},{64,56},{72,6... | collective-permute-start | bytes 196616 | tf_op jit(solution)/shard_map/ppermute | solution.py:265
  16.9 0.0 collective-permute-start.2
  16.9 5.1 %second_inner.1.done = f32[32,3072]{1,0:T(8,128)S(1)} custom-call(s32[9,32]{1,0:T(8,128)S(4)} %get-tuple-element.12.cols, s32[32]{0:T(128)S(4)} %get-tuple-element.13.counts, f32[32,128]{1,0:T(8,128)S(1)} %get-tuple-element.14.onsite, f32[32,1024]{1,0:T(8,128)S(1)} %first_edge.1.edge, f32[32,3072]{1,0:T(8,128)S(1)} %get-tuple-element.17.inner, ...), custom_call_target="tpu_custom_call" | custom-call | flops 905969664 | bytes 14155776 | tf_op jit(solution)/shard_map/second_inner/pallas_call | solution.py:304
  22.1 0.6 collective-permute-done.2.before
  22.7 2.6 %second_edge.1 = (f32[32,4096]{1,0:T(8,128)}, f32[8,32,512]{2,1,0:T(8,128)S(1)}) custom-call(s32[9,32]{1,0:T(8,128)S(4)} %get-tuple-element.12.cols, s32[32]{0:T(128)S(4)} %get-tuple-element.13.counts, f32[32,128]{1,0:T(8,128)S(1)} %get-tuple-element.14.onsite, f32[32,512]{1,0:T(8,128)S(1)} %collective-permute-done.2.before, f32[32,1024]{1,0:T(8,128)S(1)} %first_edge.1.edge, ...), custom_call_target="tpu_custom_call" | custom-call | flops 301989888 | bytes 4718592 | tf_op jit(solution)/shard_map/second_edge/pallas_call | solution.py:315
  25.3 5.7 %collective-permute-start.10 = (f32[32,512]{1,0:T(8,128)S(1)}, f32[32,512]{1,0:T(8,128)S(1)}, u32[]{:S(2)}, u32[]{:S(2)}) collective-permute-start(f32[32,512]{1,0:T(8,128)S(1)} %get-tuple-element.22), channel_id=1, source_target_pairs={{0,7},{1,0},{2,1},{3,2},{4,3},{5,4},{6,5},{7,6},{8,15},{9,8},{10,9... | collective-permute-start | bytes 196616 | tf_op jit(solution)/shard_map/ppermute | solution.py:330
  31.0 1.2 %collective-permute-start.9 = (f32[32,512]{1,0:T(8,128)S(1)}, f32[32,512]{1,0:T(8,128)S(1)}, u32[]{:S(2)}, u32[]{:S(2)}) collective-permute-start(f32[32,512]{1,0:T(8,128)S(1)} %get-tuple-element.23), channel_id=1, source_target_pairs={{0,6},{1,7},{2,0},{3,1},{4,2},{5,3},{6,4},{7,5},{8,14},{9,15},{10,... | collective-permute-start | bytes 196616 | tf_op jit(solution)/shard_map/ppermute | solution.py:330
  32.1 0.4 collective-permute-start.8
  32.6 4.5 %collective-permute-start.7 = (f32[32,512]{1,0:T(8,128)S(1)}, f32[32,512]{1,0:T(8,128)S(1)}, u32[]{:S(2)}, u32[]{:S(2)}) collective-permute-start(f32[32,512]{1,0:T(8,128)S(1)} %get-tuple-element.25), channel_id=1, source_target_pairs={{0,4},{1,5},{2,6},{3,7},{4,0},{5,1},{6,2},{7,3},{8,12},{9,13},{10,... | collective-permute-start | bytes 196616 | tf_op jit(solution)/shard_map/ppermute | solution.py:330
  37.1 0.0 collective-permute-start.6
  37.1 0.0 collective-permute-done.10.refs_6_
  37.1 2.2 %collective-permute-start.5 = (f32[32,512]{1,0:T(8,128)S(1)}, f32[32,512]{1,0:T(8,128)S(1)}, u32[]{:S(2)}, u32[]{:S(2)}) collective-permute-start(f32[32,512]{1,0:T(8,128)S(1)} %get-tuple-element.27), channel_id=1, source_target_pairs={{0,2},{1,3},{2,4},{3,5},{4,6},{5,7},{6,0},{7,1},{8,10},{9,11},{10,... | collective-permute-start | bytes 196616 | tf_op jit(solution)/shard_map/ppermute | solution.py:330
  39.2 1.4 %collective-permute-start.4 = (f32[32,512]{1,0:T(8,128)S(1)}, f32[32,512]{1,0:T(8,128)S(1)}, u32[]{:S(2)}, u32[]{:S(2)}) collective-permute-start(f32[32,512]{1,0:T(8,128)S(1)} %get-tuple-element.28), channel_id=1, source_target_pairs={{0,1},{1,2},{2,3},{3,4},{4,5},{5,6},{6,7},{7,0},{8,9},{9,10},{10,1... | collective-permute-start | bytes 196616 | tf_op jit(solution)/shard_map/ppermute | solution.py:330
  40.6 0.0 collective-permute-done.8.refs_4_
  40.6 0.0 collective-permute-done.7.refs_3_
  40.6 2.6 %collective-permute-done.6.refs_2_ = f32[32,512]{1,0:T(8,128)S(1)} collective-permute-done((f32[32,512]{1,0:T(8,128)S(1)}, f32[32,512]{1,0:T(8,128)S(1)}, u32[]{:S(2)}, u32[]{:S(2)}) %collective-permute-start.6) | collective-permute-done | bytes 65568 | tf_op jit(solution)/shard_map/ppermute | solution.py:330
  43.3 2.0 %collective-permute-done.5.refs_1_ = f32[32,512]{1,0:T(8,128)S(1)} collective-permute-done((f32[32,512]{1,0:T(8,128)S(1)}, f32[32,512]{1,0:T(8,128)S(1)}, u32[]{:S(2)}, u32[]{:S(2)}) %collective-permute-start.5) | collective-permute-done | bytes 65568 | tf_op jit(solution)/shard_map/ppermute | solution.py:330
  45.2 0.0 collective-permute-done.4.refs_0_
  45.2 0.5 gram.1
  45.7 8.6 %collective-permute-start.11 = (f32[4,32,256]{2,1,0:T(8,128)S(1)}, f32[4,32,256]{2,1,0:T(8,128)S(1)}, u32[]{:S(2)}, u32[]{:S(2)}) collective-permute-start(f32[4,32,256]{2,1,0:T(8,128)S(1)} %get-tuple-element.21), channel_id=1, source_target_pairs={{0,8},{8,0},{16,24},{24,16},{32,40},{40,32},{48,56},{56,48},{64,72... | collective-permute-start | bytes 393224 | tf_op jit(solution)/shard_map/ppermute | solution.py:347
  54.4 1.0 %collective-permute-done.11 = f32[4,32,256]{2,1,0:T(8,128)S(1)} collective-permute-done((f32[4,32,256]{2,1,0:T(8,128)S(1)}, f32[4,32,256]{2,1,0:T(8,128)S(1)}, u32[]{:S(2)}, u32[]{:S(2)}) %collective-permute-start.11) | collective-permute-done | bytes 131104 | tf_op jit(solution)/shard_map/ppermute | solution.py:347
  55.4 1.2 %collective-permute-start.13 = (f32[32,256]{1,0:T(8,128)S(1)}, f32[32,256]{1,0:T(8,128)S(1)}, u32[]{:S(2)}, u32[]{:S(2)}) collective-permute-start(f32[32,256]{1,0:T(8,128)S(1)} %get-tuple-element.31), channel_id=1, source_target_pairs={{0,1},{1,2},{2,3},{3,4},{4,5},{5,6},{6,7},{7,0},{8,15},{9,8},{10,9... | collective-permute-start | bytes 98312 | tf_op jit(solution)/shard_map/ppermute | solution.py:354
  56.6 2.8 %collective-permute-start.15 = (f32[32,256]{1,0:T(8,128)S(1)}, f32[32,256]{1,0:T(8,128)S(1)}, u32[]{:S(2)}, u32[]{:S(2)}) collective-permute-start(f32[32,256]{1,0:T(8,128)S(1)} %get-tuple-element.32), channel_id=1, source_target_pairs={{0,3},{1,4},{2,5},{3,6},{4,7},{5,0},{6,1},{7,2},{8,13},{9,14},{10,... | collective-permute-start | bytes 98312 | tf_op jit(solution)/shard_map/ppermute | solution.py:354
  59.4 0.3 collective-permute-start.14
  59.7 0.7 collective-permute-start.12
  60.4 0.0 collective-permute-done.13
  60.4 0.9 %collective-permute-done.15 = f32[32,256]{1,0:T(8,128)S(1)} collective-permute-done((f32[32,256]{1,0:T(8,128)S(1)}, f32[32,256]{1,0:T(8,128)S(1)}, u32[]{:S(2)}, u32[]{:S(2)}) %collective-permute-start.15) | collective-permute-done | bytes 32800 | tf_op jit(solution)/shard_map/ppermute | solution.py:354
  61.3 2.0 %collective-permute-done.14 = f32[32,256]{1,0:T(8,128)S(1)} collective-permute-done((f32[32,256]{1,0:T(8,128)S(1)}, f32[32,256]{1,0:T(8,128)S(1)}, u32[]{:S(2)}, u32[]{:S(2)}) %collective-permute-start.14) | collective-permute-done | bytes 32800 | tf_op jit(solution)/shard_map/ppermute | solution.py:354
  63.3 0.0 collective-permute-done.12
  63.3 0.1 collective-permute-start.18
  63.4 0.1 collective-permute-start.17
  63.5 1.4 %collective-permute-start.16 = (f32[32,256]{1,0:T(8,128)S(1)}, f32[32,256]{1,0:T(8,128)S(1)}, u32[]{:S(2)}, u32[]{:S(2)}) collective-permute-start(f32[32,256]{1,0:T(8,128)S(1)} %add_add_fusion.2), channel_id=1, source_target_pairs={{0,16},{8,24},{16,32},{24,40},{32,48},{40,56},{48,0},{56,8},{64,80... | collective-permute-start | bytes 98312 | tf_op jit(solution)/shard_map/ppermute | solution.py:365
  64.9 1.3 %collective-permute-done.18 = f32[32,256]{1,0:T(8,128)S(1)} collective-permute-done((f32[32,256]{1,0:T(8,128)S(1)}, f32[32,256]{1,0:T(8,128)S(1)}, u32[]{:S(2)}, u32[]{:S(2)}) %collective-permute-start.18) | collective-permute-done | bytes 32800 | tf_op jit(solution)/shard_map/ppermute | solution.py:365
  66.2 1.6 %collective-permute-done.17 = f32[32,256]{1,0:T(8,128)S(1)} collective-permute-done((f32[32,256]{1,0:T(8,128)S(1)}, f32[32,256]{1,0:T(8,128)S(1)}, u32[]{:S(2)}, u32[]{:S(2)}) %collective-permute-start.17) | collective-permute-done | bytes 32800 | tf_op jit(solution)/shard_map/ppermute | solution.py:365
  67.8 1.1 %collective-permute-done.16 = f32[32,256]{1,0:T(8,128)S(1)} collective-permute-done((f32[32,256]{1,0:T(8,128)S(1)}, f32[32,256]{1,0:T(8,128)S(1)}, u32[]{:S(2)}, u32[]{:S(2)}) %collective-permute-start.16) | collective-permute-done | bytes 32800 | tf_op jit(solution)/shard_map/ppermute | solution.py:365
  68.9 2.1 %collective-permute-start.21 = (f32[32,256]{1,0:T(8,128)S(1)}, f32[32,256]{1,0:T(8,128)S(1)}, u32[]{:S(2)}, u32[]{:S(2)}) collective-permute-start(f32[32,256]{1,0:T(8,128)S(1)} %add_add_fusion.1), channel_id=1, source_target_pairs={{0,192},{8,200},{16,208},{24,216},{32,224},{40,232},{48,240},{56,2... | collective-permute-start | bytes 98312 | tf_op jit(solution)/shard_map/ppermute | solution.py:365
  70.9 0.7 collective-permute-start.19
  71.6 0.3 collective-permute-done.21
  72.0 3.5 %collective-permute-done.20 = f32[32,256]{1,0:T(8,128)S(1)} collective-permute-done((f32[32,256]{1,0:T(8,128)S(1)}, f32[32,256]{1,0:T(8,128)S(1)}, u32[]{:S(2)}, u32[]{:S(2)}) %collective-permute-start.20) | collective-permute-done | bytes 32800 | tf_op jit(solution)/shard_map/ppermute | solution.py:365
  75.5 10.0 %collective-permute-start.22 = (f32[32,256]{1,0:T(8,128)S(1)}, f32[32,256]{1,0:T(8,128)S(1)}, u32[]{:S(2)}, u32[]{:S(2)}) collective-permute-start(f32[32,256]{1,0:T(8,128)S(1)} %add_add_fusion), channel_id=1, source_target_pairs={{0,8},{8,0},{16,24},{24,16},{32,40},{40,32},{48,56},{56,48},{64,72... | collective-permute-start | bytes 98312 | tf_op jit(solution)/shard_map/ppermute | solution.py:367
  85.5 0.9 collective-permute-done.22
  86.3 0.6 add.43
  (12 shorter events, 0.1 us)
Async XLA Ops:
  1.5 10.6 %collective-permute-start.1 = (f32[32,512]{1,0:T(8,128)S(1)}, f32[32,512]{1,0:T(8,128)S(1)}, u32[]{:S(2)}, u32[]{:S(2)}) collective-permute-start(f32[32,512]{1,0:T(8,128)S(1)} %get-tuple-element.29), channel_id=1, source_target_pairs={{8,0},{16,8},{24,16},{32,24},{40,32},{48,40},{56,48},{64,56},{72,6... | collective-permute-start | bytes 196616 | tf_op jit(solution)/shard_map/ppermute | solution.py:265
  4.8 7.3 %collective-permute-start = (f32[32,512]{1,0:T(8,128)S(1)}, f32[32,512]{1,0:T(8,128)S(1)}, u32[]{:S(2)}, u32[]{:S(2)}) collective-permute-start(f32[32,512]{1,0:T(8,128)S(1)} %get-tuple-element.30), channel_id=1, source_target_pairs={{0,8},{8,16},{16,24},{24,32},{32,40},{40,48},{48,56},{56,64},{64,7... | collective-permute-start | bytes 196616 | tf_op jit(solution)/shard_map/ppermute | solution.py:265
  13.9 8.1 %collective-permute-start.3 = (f32[32,512]{1,0:T(8,128)S(1)}, f32[32,512]{1,0:T(8,128)S(1)}, u32[]{:S(2)}, u32[]{:S(2)}) collective-permute-start(f32[32,512]{1,0:T(8,128)S(1)} %get-tuple-element.35), channel_id=1, source_target_pairs={{8,0},{16,8},{24,16},{32,24},{40,32},{48,40},{56,48},{64,56},{72,6... | collective-permute-start | bytes 196616 | tf_op jit(solution)/shard_map/ppermute | solution.py:265
  16.9 5.8 %collective-permute-start.2 = (f32[32,512]{1,0:T(8,128)S(1)}, f32[32,512]{1,0:T(8,128)S(1)}, u32[]{:S(2)}, u32[]{:S(2)}) collective-permute-start(f32[32,512]{1,0:T(8,128)S(1)} %get-tuple-element.36), channel_id=1, source_target_pairs={{0,8},{8,16},{16,24},{24,32},{32,40},{40,48},{48,56},{56,64},{64,7... | collective-permute-start | bytes 196616 | tf_op jit(solution)/shard_map/ppermute | solution.py:265
  25.3 11.8 %collective-permute-start.10 = (f32[32,512]{1,0:T(8,128)S(1)}, f32[32,512]{1,0:T(8,128)S(1)}, u32[]{:S(2)}, u32[]{:S(2)}) collective-permute-start(f32[32,512]{1,0:T(8,128)S(1)} %get-tuple-element.22), channel_id=1, source_target_pairs={{0,7},{1,0},{2,1},{3,2},{4,3},{5,4},{6,5},{7,6},{8,15},{9,8},{10,9... | collective-permute-start | bytes 196616 | tf_op jit(solution)/shard_map/ppermute | solution.py:330
  31.0 8.3 %collective-permute-start.9 = (f32[32,512]{1,0:T(8,128)S(1)}, f32[32,512]{1,0:T(8,128)S(1)}, u32[]{:S(2)}, u32[]{:S(2)}) collective-permute-start(f32[32,512]{1,0:T(8,128)S(1)} %get-tuple-element.23), channel_id=1, source_target_pairs={{0,6},{1,7},{2,0},{3,1},{4,2},{5,3},{6,4},{7,5},{8,14},{9,15},{10,... | collective-permute-start | bytes 196616 | tf_op jit(solution)/shard_map/ppermute | solution.py:330
  32.1 8.5 %collective-permute-start.8 = (f32[32,512]{1,0:T(8,128)S(1)}, f32[32,512]{1,0:T(8,128)S(1)}, u32[]{:S(2)}, u32[]{:S(2)}) collective-permute-start(f32[32,512]{1,0:T(8,128)S(1)} %get-tuple-element.24), channel_id=1, source_target_pairs={{0,5},{1,6},{2,7},{3,0},{4,1},{5,2},{6,3},{7,4},{8,13},{9,14},{10,... | collective-permute-start | bytes 196616 | tf_op jit(solution)/shard_map/ppermute | solution.py:330
  32.6 8.0 %collective-permute-start.7 = (f32[32,512]{1,0:T(8,128)S(1)}, f32[32,512]{1,0:T(8,128)S(1)}, u32[]{:S(2)}, u32[]{:S(2)}) collective-permute-start(f32[32,512]{1,0:T(8,128)S(1)} %get-tuple-element.25), channel_id=1, source_target_pairs={{0,4},{1,5},{2,6},{3,7},{4,0},{5,1},{6,2},{7,3},{8,12},{9,13},{10,... | collective-permute-start | bytes 196616 | tf_op jit(solution)/shard_map/ppermute | solution.py:330
  37.1 6.2 %collective-permute-start.6 = (f32[32,512]{1,0:T(8,128)S(1)}, f32[32,512]{1,0:T(8,128)S(1)}, u32[]{:S(2)}, u32[]{:S(2)}) collective-permute-start(f32[32,512]{1,0:T(8,128)S(1)} %get-tuple-element.26), channel_id=1, source_target_pairs={{0,3},{1,4},{2,5},{3,6},{4,7},{5,0},{6,1},{7,2},{8,11},{9,12},{10,... | collective-permute-start | bytes 196616 | tf_op jit(solution)/shard_map/ppermute | solution.py:330
  37.1 8.2 %collective-permute-start.5 = (f32[32,512]{1,0:T(8,128)S(1)}, f32[32,512]{1,0:T(8,128)S(1)}, u32[]{:S(2)}, u32[]{:S(2)}) collective-permute-start(f32[32,512]{1,0:T(8,128)S(1)} %get-tuple-element.27), channel_id=1, source_target_pairs={{0,2},{1,3},{2,4},{3,5},{4,6},{5,7},{6,0},{7,1},{8,10},{9,11},{10,... | collective-permute-start | bytes 196616 | tf_op jit(solution)/shard_map/ppermute | solution.py:330
  39.2 6.0 %collective-permute-start.4 = (f32[32,512]{1,0:T(8,128)S(1)}, f32[32,512]{1,0:T(8,128)S(1)}, u32[]{:S(2)}, u32[]{:S(2)}) collective-permute-start(f32[32,512]{1,0:T(8,128)S(1)} %get-tuple-element.28), channel_id=1, source_target_pairs={{0,1},{1,2},{2,3},{3,4},{4,5},{5,6},{6,7},{7,0},{8,9},{9,10},{10,1... | collective-permute-start | bytes 196616 | tf_op jit(solution)/shard_map/ppermute | solution.py:330
  45.7 9.6 %collective-permute-start.11 = (f32[4,32,256]{2,1,0:T(8,128)S(1)}, f32[4,32,256]{2,1,0:T(8,128)S(1)}, u32[]{:S(2)}, u32[]{:S(2)}) collective-permute-start(f32[4,32,256]{2,1,0:T(8,128)S(1)} %get-tuple-element.21), channel_id=1, source_target_pairs={{0,8},{8,0},{16,24},{24,16},{32,40},{40,32},{48,56},{56,48},{64,72... | collective-permute-start | bytes 393224 | tf_op jit(solution)/shard_map/ppermute | solution.py:347
  55.4 5.0 %collective-permute-start.13 = (f32[32,256]{1,0:T(8,128)S(1)}, f32[32,256]{1,0:T(8,128)S(1)}, u32[]{:S(2)}, u32[]{:S(2)}) collective-permute-start(f32[32,256]{1,0:T(8,128)S(1)} %get-tuple-element.31), channel_id=1, source_target_pairs={{0,1},{1,2},{2,3},{3,4},{4,5},{5,6},{6,7},{7,0},{8,15},{9,8},{10,9... | collective-permute-start | bytes 98312 | tf_op jit(solution)/shard_map/ppermute | solution.py:354
  56.6 4.7 %collective-permute-start.15 = (f32[32,256]{1,0:T(8,128)S(1)}, f32[32,256]{1,0:T(8,128)S(1)}, u32[]{:S(2)}, u32[]{:S(2)}) collective-permute-start(f32[32,256]{1,0:T(8,128)S(1)} %get-tuple-element.32), channel_id=1, source_target_pairs={{0,3},{1,4},{2,5},{3,6},{4,7},{5,0},{6,1},{7,2},{8,13},{9,14},{10,... | collective-permute-start | bytes 98312 | tf_op jit(solution)/shard_map/ppermute | solution.py:354
  59.4 3.9 %collective-permute-start.14 = (f32[32,256]{1,0:T(8,128)S(1)}, f32[32,256]{1,0:T(8,128)S(1)}, u32[]{:S(2)}, u32[]{:S(2)}) collective-permute-start(f32[32,256]{1,0:T(8,128)S(1)} %get-tuple-element.33), channel_id=1, source_target_pairs={{0,2},{1,3},{2,4},{3,5},{4,6},{5,7},{6,0},{7,1},{8,14},{9,15},{10,... | collective-permute-start | bytes 98312 | tf_op jit(solution)/shard_map/ppermute | solution.py:354
  59.7 3.6 %collective-permute-start.12 = (f32[32,256]{1,0:T(8,128)S(1)}, f32[32,256]{1,0:T(8,128)S(1)}, u32[]{:S(2)}, u32[]{:S(2)}) collective-permute-start(f32[32,256]{1,0:T(8,128)S(1)} %get-tuple-element.34), channel_id=1, source_target_pairs={{0,4},{1,5},{2,6},{3,7},{4,0},{5,1},{6,2},{7,3},{8,8},{9,9},{10,10... | collective-permute-start | bytes 98312 | tf_op jit(solution)/shard_map/ppermute | solution.py:354
  63.3 2.8 %collective-permute-start.18 = (f32[32,256]{1,0:T(8,128)S(1)}, f32[32,256]{1,0:T(8,128)S(1)}, u32[]{:S(2)}, u32[]{:S(2)}) collective-permute-start(f32[32,256]{1,0:T(8,128)S(1)} %add_add_fusion.2), channel_id=1, source_target_pairs={{0,48},{8,56},{16,0},{24,8},{32,16},{40,24},{48,32},{56,40},{64,11... | collective-permute-start | bytes 98312 | tf_op jit(solution)/shard_map/ppermute | solution.py:365
  63.4 4.4 %collective-permute-start.17 = (f32[32,256]{1,0:T(8,128)S(1)}, f32[32,256]{1,0:T(8,128)S(1)}, u32[]{:S(2)}, u32[]{:S(2)}) collective-permute-start(f32[32,256]{1,0:T(8,128)S(1)} %add_add_fusion.2), channel_id=1, source_target_pairs={{0,32},{8,40},{16,48},{24,56},{32,0},{40,8},{48,16},{56,24},{64,96... | collective-permute-start | bytes 98312 | tf_op jit(solution)/shard_map/ppermute | solution.py:365
  63.5 5.3 %collective-permute-start.16 = (f32[32,256]{1,0:T(8,128)S(1)}, f32[32,256]{1,0:T(8,128)S(1)}, u32[]{:S(2)}, u32[]{:S(2)}) collective-permute-start(f32[32,256]{1,0:T(8,128)S(1)} %add_add_fusion.2), channel_id=1, source_target_pairs={{0,16},{8,24},{16,32},{24,40},{32,48},{40,56},{48,0},{56,8},{64,80... | collective-permute-start | bytes 98312 | tf_op jit(solution)/shard_map/ppermute | solution.py:365
  68.9 3.1 %collective-permute-start.21 = (f32[32,256]{1,0:T(8,128)S(1)}, f32[32,256]{1,0:T(8,128)S(1)}, u32[]{:S(2)}, u32[]{:S(2)}) collective-permute-start(f32[32,256]{1,0:T(8,128)S(1)} %add_add_fusion.1), channel_id=1, source_target_pairs={{0,192},{8,200},{16,208},{24,216},{32,224},{40,232},{48,240},{56,2... | collective-permute-start | bytes 98312 | tf_op jit(solution)/shard_map/ppermute | solution.py:365
  70.9 4.6 %collective-permute-start.20 = (f32[32,256]{1,0:T(8,128)S(1)}, f32[32,256]{1,0:T(8,128)S(1)}, u32[]{:S(2)}, u32[]{:S(2)}) collective-permute-start(f32[32,256]{1,0:T(8,128)S(1)} %add_add_fusion.1), channel_id=1, source_target_pairs={{0,128},{8,136},{16,144},{24,152},{32,160},{40,168},{48,176},{56,1... | collective-permute-start | bytes 98312 | tf_op jit(solution)/shard_map/ppermute | solution.py:365
  70.9 4.6 %collective-permute-start.19 = (f32[32,256]{1,0:T(8,128)S(1)}, f32[32,256]{1,0:T(8,128)S(1)}, u32[]{:S(2)}, u32[]{:S(2)}) collective-permute-start(f32[32,256]{1,0:T(8,128)S(1)} %add_add_fusion.1), channel_id=1, source_target_pairs={{0,64},{8,72},{16,80},{24,88},{32,96},{40,104},{48,112},{56,120},{... | collective-permute-start | bytes 98312 | tf_op jit(solution)/shard_map/ppermute | solution.py:365
  75.5 10.8 %collective-permute-start.22 = (f32[32,256]{1,0:T(8,128)S(1)}, f32[32,256]{1,0:T(8,128)S(1)}, u32[]{:S(2)}, u32[]{:S(2)}) collective-permute-start(f32[32,256]{1,0:T(8,128)S(1)} %add_add_fusion), channel_id=1, source_target_pairs={{0,8},{8,0},{16,24},{24,16},{32,40},{40,32},{48,56},{56,48},{64,72... | collective-permute-start | bytes 98312 | tf_op jit(solution)/shard_map/ppermute | solution.py:367

commit v3 on v2

--- a/solution.py
+++ b/solution.py
@@ -33,6 +33,23 @@
             table[slot + b, 0:vcount] = high
             table[slot + b, vcount : 2 * vcount] = low
     table[table.shape[0] - 1] = jnp.zeros(table.shape[1:], bf16)
+
+
+def is_first_core():
+    return lax.rem(lax.axis_index("rows"), 2) == 0
+
+
+def outer_slots(local):
+    first = is_first_core()
+    return jnp.where(first, local + REACH, 0), jnp.where(first, 0, local + REACH)
+
+
+def split_ends(ref, near, far, count):
+    width = count * BLOCK
+    first = is_first_core()
+    high = ref.shape[1] - width
+    near[...] = ref[:, pl.ds(pl.multiple_of(jnp.where(first, high, 0), BLOCK), width)]
+    far[...] = ref[:, pl.ds(pl.multiple_of(jnp.where(first, 0, high), BLOCK), width)]
 
 
 def columns(ref, block):
@@ -72,6 +89,22 @@
     return (total + diag * columns(field, row)) / filter_half
 
 
+def ends(field_hbm, near, far, sems):
+    width = near.shape[1]
+    high = field_hbm.shape[1] - width
+    first = is_first_core()
+    copies = []
+    for n, (start, ref) in enumerate(
+        [(jnp.where(first, 0, high), far), (jnp.where(first, high, 0), near)]
+    ):
+        part = field_hbm.at[:, pl.ds(pl.multiple_of(start, BLOCK), width)]
+        copies.append(pltpu.make_async_copy(part, ref, sems.at[n]))
+    for copy in copies:
+        copy.start()
+    for copy in copies:
+        copy.wait()
+
+
 def first_inner(
     nblocks, local, cols_hbm, counts_hbm, onsite_hbm, field_hbm, h_hbm,
     cols, counts, h, field, onsite, out, table, sems, small,
@@ -119,14 +152,17 @@
     lax.fori_loop(0, 2 * REACH, rest, 0)
 
 
-def first_edge(nblocks, local, cols, counts, onsite, before, field, after, h, out, table):
+def first_edge(
+    nblocks, local, cols, counts, onsite, near, far, field, h, out, near_out, far_out, table
+):
+    near_slot, far_slot = outer_slots(local)
     load_blocks(
         table,
         [
-            (before, 0, 0, REACH),
+            (near, 0, near_slot, REACH),
+            (far, 0, far_slot, REACH),
             (field, 0, REACH, 2 * REACH),
             (field, local - 2 * REACH, local - REACH, 2 * REACH),
-            (after, 0, local + REACH, REACH),
         ],
     )
     unroll = 4
@@ -140,6 +176,7 @@
         return carry
 
     lax.fori_loop(0, 2 * REACH // unroll, step, 0)
+    split_ends(out, near_out, far_out, REACH)
 
 
 def second_value(row, total, onsite, first, field):
@@ -170,18 +207,18 @@
 
 
 def second_edge(
-    nblocks, local, groups, cols, counts, onsite, before, edge, inner, after, field, done, h,
-    out, parts, table,
+    nblocks, local, cols, counts, onsite, near, far, edge, inner, field, done, h, out, parts, table
 ):
+    near_slot, far_slot = outer_slots(local)
     load_blocks(
         table,
         [
-            (before, 0, 0, REACH),
+            (near, 0, near_slot, REACH),
+            (far, 0, far_slot, REACH),
             (edge, 0, REACH, REACH),
             (inner, 0, 2 * REACH, REACH),
             (inner, local - 3 * REACH, local - REACH, REACH),
             (edge, REACH, local, REACH),
-            (after, 0, local + REACH, REACH),
         ],
     )
     out[:, REACH * BLOCK : (local - REACH) * BLOCK] = done[...]
@@ -196,39 +233,32 @@
         return carry
 
     lax.fori_loop(0, 2 * REACH // unroll, step, 0)
-    where = lax.axis_index("cols")
     width = parts.shape[2]
-    for k in range(groups):
-        place = lax.rem(where + k, groups) * width
-        parts[k] = out[:, pl.ds(pl.multiple_of(place, width), width)]
-
-
-def gram(groups, scale, own, *refs):
-    got = refs[: groups - 1]
-    keep, give, high, low, both = refs[groups - 1 :]
-    vcount = own.shape[1]
-    where = lax.axis_index("cols")
-    core = lax.rem(lax.axis_index("rows"), 2)
-
-    def place(k):
-        return pl.multiple_of(lax.rem(where + k, groups) * vcount, vcount)
-
-    for k in range(groups):
-        a, b = halves(own[0] if k == 0 else got[k - 1][...])
-        at = place(groups - k)
-        high[pl.ds(at, vcount), :] = a
-        low[pl.ds(at, vcount), :] = b
-    a, b = high[...], low[...]
-    both[...] = (
+    for k in range(parts.shape[0]):
+        parts[k] = out[:, k * width : (k + 1) * width]
+
+
+def gram(scale, parts, keep, give):
+    groups, vcount, width = parts.shape
+    total = groups * vcount
+    a, b = halves(parts[...].reshape(total, width))
+    both = (
         lax.dot_general(a, a, NT, preferred_element_type=f32)
         + lax.dot_general(a, b, NT, preferred_element_type=f32)
         + lax.dot_general(b, a, NT, preferred_element_type=f32)
     ) * scale
-    half = groups // 2
-    for j in range(half):
-        even, odd = (half, 0) if j == 0 else (j, groups - j)
-        keep[j] = both[pl.ds(place(jnp.where(core == 0, even, odd)), vcount), :]
-        give[j] = both[pl.ds(place(jnp.where(core == 0, odd, even)), vcount), :]
+    low = both[:, : total // 2].reshape(groups, vcount, total // 2)
+    high = both[:, total // 2 :].reshape(groups, vcount, total // 2)
+    first = is_first_core()
+    keep[...] = jnp.where(first, low, high)
+    give[...] = jnp.where(first, high, low)
+
+
+def join(mine, other, out):
+    first = is_first_core()
+    half = mine.shape[1]
+    out[:, :half] = jnp.where(first, mine[...], other[...])
+    out[:, half:] = jnp.where(first, other[...], mine[...])
 
 
 def params(mebibytes):
@@ -258,13 +288,26 @@
         return jax.ShapeDtypeStruct(dims, f32)
 
     table = pltpu.VMEM((local + 2 * REACH + 1, 2 * vcount, BLOCK), bf16)
-    up = [(i, (i + 1) % ranks) for i in range(ranks)]
-    down = [(j, i) for i, j in up]
-
-    def around(low, high):
-        return lax.ppermute(high, "rows", up), lax.ppermute(low, "rows", down)
-
-    before, after = around(vectors[:, :reach], vectors[:, width - reach :])
+    mate = [(i, i ^ 1) for i in range(ranks)]
+    beyond = [(i, (i + 1 if i % 2 else i - 1) % ranks) for i in range(ranks)]
+
+    def around(near, far):
+        far = lax.ppermute(far, "rows", beyond)
+        return lax.ppermute(near, "rows", mate), far
+
+    def in_hbm(*arrays):
+        return [pltpu.with_memory_space_constraint(x, pltpu.HBM) for x in arrays]
+
+    near, far = pl.pallas_call(
+        ends,
+        in_specs=[HBM],
+        out_specs=(VMEM, VMEM),
+        out_shape=(pltpu.VMEM((vcount, reach), f32), pltpu.VMEM((vcount, reach), f32)),
+        scratch_shapes=[pltpu.SemaphoreType.DMA((2,))],
+        compiler_params=params(8),
+        name="ends",
+    )(*in_hbm(vectors))
+    near, far = around(near, far)
 
     cols, counts, h, field, onsite, inner = pl.pallas_call(
         functools.partial(first_inner, nblocks, local),
@@ -286,20 +329,19 @@
         compiler_params=params(8),
         cost_estimate=cost(local, slots, vcount),
         name="first_inner",
-    )(*[pltpu.with_memory_space_constraint(x, pltpu.HBM) for x in (cols, block_counts, onsite, vectors, h_blocks)])
-
-    edge = pl.pallas_call(
+    )(*in_hbm(cols, block_counts, onsite, vectors, h_blocks))
+
+    edge, near, far = pl.pallas_call(
         functools.partial(first_edge, nblocks, local),
         in_specs=[SMEM, SMEM] + [VMEM] * 5,
-        out_specs=VMEM,
-        out_shape=shape(vcount, edge_rows * BLOCK),
+        out_specs=(VMEM,) * 3,
+        out_shape=(shape(vcount, 2 * reach), shape(vcount, reach), shape(vcount, reach)),
         scratch_shapes=[table],
         compiler_params=params(8),
         cost_estimate=cost(edge_rows, slots, vcount),
         name="first_edge",
-    )(cols, counts, onsite, before, field, after, h)
-
-    before, after = around(edge[:, :reach], edge[:, reach:])
+    )(cols, counts, onsite, near, far, field, h)
+    near, far = around(near, far)
 
     done = pl.pallas_call(
         functools.partial(second_inner, nblocks, local),
@@ -313,7 +355,7 @@
     )(cols, counts, onsite, edge, inner, field, h)
 
     filtered, parts = pl.pallas_call(
-        functools.partial(second_edge, nblocks, local, groups),
+        functools.partial(second_edge, nblocks, local),
         in_specs=[SMEM, SMEM] + [VMEM] * 8,
         out_specs=(VMEM, VMEM),
         out_shape=(shape(vcount, width), shape(groups, vcount, width // groups)),
@@ -321,51 +363,36 @@
         compiler_params=params(8),
         cost_estimate=cost(edge_rows, slots, vcount),
         name="second_edge",
-    )(cols, counts, onsite, before, edge, inner, after, field, done, h)
-
-    order = sorted(range(1, groups), key=lambda k: -min(k, groups - k))
-    got = {}
-    for k in order:
-        pairs = [(i, (i + k) % groups) for i in range(groups)]
-        got[k] = lax.ppermute(parts[k], "cols", pairs)
+    )(cols, counts, onsite, near, far, edge, inner, field, done, h)
+
+    parts = lax.all_to_all(parts, "cols", 0, 0)
     total = vcount * groups
-    half = groups // 2
     keep, give = pl.pallas_call(
-        functools.partial(gram, groups, 1.0 / (width * ranks)),
-        in_specs=[VMEM] * groups,
+        functools.partial(gram, 1.0 / (width * ranks)),
+        in_specs=[VMEM],
         out_specs=(VMEM, VMEM),
-        out_shape=(shape(half, vcount, total), shape(half, vcount, total)),
-        scratch_shapes=[
-            pltpu.VMEM((total, width // groups), bf16),
-            pltpu.VMEM((total, width // groups), bf16),
-            pltpu.VMEM((total, total), f32),
-        ],
+        out_shape=(shape(groups, vcount, total // 2), shape(groups, vcount, total // 2)),
         compiler_params=params(8),
         name="gram",
-    )(parts, *[got[k] for k in range(1, groups)])
-
-    keep = keep + lax.ppermute(give, "rows", [(i, i ^ 1) for i in range(ranks)])
-    terms = []
-    for j in range(half):
-        pairs = []
-        for r in range(ranks):
-            shift = (half if j == 0 else j) if r % 2 == 0 else -j
-            pairs += [(r * groups + z, r * groups + (z + shift) % groups) for z in range(groups)]
-        terms.append(lax.ppermute(keep[j], ("rows", "cols"), pairs))
-    mine = sum(terms[1:], terms[0])
-
-    side = 4
-    for stride in (2, 2 * side):
-        terms = []
-        for k in range(1, side):
-            pairs = []
-            for r in range(ranks):
-                at = r // stride % side
-                pairs.append((r, r + ((at + k) % side - at) * stride))
-            terms.append(lax.ppermute(mine, "rows", pairs))
-        mine = sum(terms, mine)
-    mine = mine + lax.ppermute(mine, "rows", [(i, i ^ 1) for i in range(ranks)])
-    return (filtered, mine)
+    )(parts)
+    terms = lax.all_to_all(keep + lax.ppermute(give, "rows", mate), "cols", 0, 0)
+    mine = jnp.sum(terms, axis=0)
+
+    peers = ranks // 2
+    same = [[2 * i + core for i in range(peers)] for core in range(2)]
+    terms = jnp.broadcast_to(mine[None], (peers, *mine.shape))
+    terms = lax.all_to_all(terms, "rows", 0, 0, axis_index_groups=same)
+    mine = jnp.sum(terms, axis=0)
+    other = lax.ppermute(mine, "rows", mate)
+    correlation = pl.pallas_call(
+        join,
+        in_specs=[VMEM, VMEM],
+        out_specs=VMEM,
+        out_shape=shape(vcount, total),
+        compiler_params=params(8),
+        name="join",
+    )(mine, other)
+    return (filtered, correlation)
 
 
 def solution(mesh):

time: 87.1 us -> 79.7 us (0.915)
  blocking collectives: 0 us -> 44.2 us
  starting transfers between devices: 49.4 us -> 14 us
  waiting for transfers between devices: 17.9 us -> 1.84 us
  Pallas kernels: 17.2 us -> 18.7 us
  local copies, waits for them, and re-layouts: 0.94 us -> 0.02 us
    all_to_all x0 -> x3, blocking collectives: none -> 44.2 us  [the longest x1 22.4 us: on_device(): parts = lax.all_to_all(parts, 'cols', 0, 0)]
    ppermute x23 -> x6, starting transfers between devices: 49.4 us -> 14 us  [the longest x2 7 us: around(): return (lax.ppermute(near, 'rows', mate), far)]
    ppermute x23 -> x6, waiting for transfers between devices: 17.9 us -> 1.84 us  [the longest x1 0.99 us: on_device(): lax.ppermute(give, 'rows', mate)]
    pallas_call x2 -> x4, Pallas kernels: 3.05 us -> 4.5 us  [the longest x1 2.57 us: on_device(): pl.pallas_call(functools.partial(second_edge, nblocks, local), in_specs=[...]
    slice x2 -> x0, local copies, waits for them, and re-layouts: 0.89 us -> none  [the longest x1 0.88 us: on_device(): before, after = around(vectors[:, :reach], vectors[:, width - reach:])]
  transfers between devices with their start and end apart: 23 -> 6, of which waited for: 12 -> 2; matrix products, arithmetic and copies ran while one was open for 0% -> 0% of each run, Pallas kernels for 14% -> 16%
where the time goes in v3:
time: 79.7 us; the launch traced here: 79.5 us
  blocking collectives  44.2 us (55%)
  Pallas kernels  18.7 us (23%)
  starting transfers between devices  14 us (18%)
  waiting for transfers between devices  1.84 us (2%)
    all_to_all x1, blocking collectives, on_device(): parts = lax.all_to_all(parts, 'cols', 0, 0)  22.4 us
    all_to_all x1, blocking collectives, on_device(): terms = lax.all_to_all(terms, 'rows', 0, 0, axis_index_groups=same)  10.9 us
    all_to_all x1, blocking collectives, on_device(): lax.all_to_all(keep + lax.ppermute(give, 'rows', mate), 'cols', 0, 0)  10.8 us
    pallas_call x1, Pallas kernels, on_device(): pl.pallas_call(functools.partial(first_inner, nblocks, local), in_specs=[...  7.3 us
    ppermute x2, starting transfers between devices, around(): return (lax.ppermute(near, 'rows', mate), far)  7 us
    pallas_call x1, Pallas kernels, on_device(): pl.pallas_call(functools.partial(second_inner, nblocks, local), in_specs=...  5.14 us
    ppermute x1, starting transfers between devices, on_device(): lax.ppermute(give, 'rows', mate)  4.06 us
    ppermute x1, starting transfers between devices, on_device(): other = lax.ppermute(mine, 'rows', mate)  2.91 us
  transfers between devices with their start and end apart: 6, of which 2 were waited for; matrix products, arithmetic and copies ran while one was open for 0% of the time, Pallas kernels for 16%

profile of v3, /device:TPU:1, one launch (start us, length us, event | category | flops | bytes accessed | tf_op | source)
XLA Modules:
  0.0 79.5 jit_solution(12227163981953472932)
XLA Ops:
  0.6 0.9 %ends.1 = (f32[32,512]{1,0:T(8,128)S(1)}, f32[32,512]{1,0:T(8,128)S(1)}) custom-call(f32[32,4096]{1,0:T(8,128)} %field_hbm.3), custom_call_target="tpu_custom_call" | custom-call | tf_op jit(solution)/shard_map/ends/pallas_call | solution.py:301
  1.5 3.3 %collective-permute-start = (f32[32,512]{1,0:T(8,128)S(1)}, f32[32,512]{1,0:T(8,128)S(1)}, u32[]{:S(2)}, u32[]{:S(2)}) collective-permute-start(f32[32,512]{1,0:T(8,128)S(1)} %get-tuple-element.20), channel_id=1, source_target_pairs={{0,8},{8,0},{16,24},{24,16},{32,40},{40,32},{48,56},{56,48},{64,72... | collective-permute-start | bytes 196616 | tf_op jit(solution)/shard_map/ppermute | solution.py:296
  4.9 0.0 collective-permute-start.1
  4.9 7.3 %first_inner.1 = (s32[9,32]{1,0:T(8,128)S(4)}, s32[32]{0:T(128)S(4)}, f32[32,9,128,128]{3,2,1,0:T(8,128)S(1)}, f32[32,4096]{1,0:T(8,128)S(1)}, f32[32,128]{1,0:T(8,128)S(1)}, /*index=5*/f32[32,3072]{1,0:T(8,128)S(1)}) custom-call(s32[9,32]{1,0:T(8,128)} %bitcast.3, s32[32]{0:T(128)} %counts_hbm.1, f32[32,128]{1,0:T(8,128)} %bitcast.2, f32[32,4096]{1,0:T(8,128)} %field_hbm.3, ...), custom_call_target="tpu_custom_call" | custom-call | flops 1207959552 | bytes 18874368 | tf_op jit(solution)/shard_map/first_inner/pallas_call | solution.py:312
  12.2 0.0 collective-permute-done.near
  12.2 0.0 collective-permute-done.1.far
  12.2 1.7 %first_edge.1 = (f32[32,1024]{1,0:T(8,128)S(1)}, f32[32,512]{1,0:T(8,128)S(1)}, f32[32,512]{1,0:T(8,128)S(1)}) custom-call(s32[9,32]{1,0:T(8,128)S(4)} %get-tuple-element.17.cols, s32[32]{0:T(128)S(4)} %get-tuple-element.18.counts, f32[32,128]{1,0:T(8,128)S(1)} %get-tuple-element.19.onsite, f32[32,512]{1,0:T(8,128)S(1)} %collective-permute-done.near, ...), custom_call_target="tpu_custom_call" | custom-call | flops 301989888 | bytes 4718592 | tf_op jit(solution)/shard_map/first_edge/pallas_call | solution.py:334
  14.0 3.7 %collective-permute-start.2 = (f32[32,512]{1,0:T(8,128)S(1)}, f32[32,512]{1,0:T(8,128)S(1)}, u32[]{:S(2)}, u32[]{:S(2)}) collective-permute-start(f32[32,512]{1,0:T(8,128)S(1)} %get-tuple-element.24), channel_id=1, source_target_pairs={{0,8},{8,0},{16,24},{24,16},{32,40},{40,32},{48,56},{56,48},{64,72... | collective-permute-start | bytes 196616 | tf_op jit(solution)/shard_map/ppermute | solution.py:296
  17.6 0.0 collective-permute-start.3
  17.6 5.1 %second_inner.1.done = f32[32,3072]{1,0:T(8,128)S(1)} custom-call(s32[9,32]{1,0:T(8,128)S(4)} %get-tuple-element.17.cols, s32[32]{0:T(128)S(4)} %get-tuple-element.18.counts, f32[32,128]{1,0:T(8,128)S(1)} %get-tuple-element.19.onsite, f32[32,1024]{1,0:T(8,128)S(1)} %get-tuple-element.26.edge, f32[32,3072]{1,0:T(8,128)S(1)} %get-tuple-element.27.inner, ...), custom_call_target="tpu_custom_call" | custom-call | flops 905969664 | bytes 14155776 | tf_op jit(solution)/shard_map/second_inner/pallas_call | solution.py:346
  22.8 0.0 collective-permute-done.2.near
  22.8 0.0 collective-permute-done.3.far
  22.8 2.6 %second_edge.1 = (f32[32,4096]{1,0:T(8,128)}, f32[8,32,512]{2,1,0:T(8,128)S(1)}) custom-call(s32[9,32]{1,0:T(8,128)S(4)} %get-tuple-element.17.cols, s32[32]{0:T(128)S(4)} %get-tuple-element.18.counts, f32[32,128]{1,0:T(8,128)S(1)} %get-tuple-element.19.onsite, f32[32,512]{1,0:T(8,128)S(1)} %collective-permute-done.2.near, ...), custom_call_target="tpu_custom_call" | custom-call | flops 301989888 | bytes 4718592 | tf_op jit(solution)/shard_map/second_edge/pallas_call | solution.py:357
  25.4 22.4 %all_to_all.15.parts = f32[8,32,512]{2,1,0:T(8,128)S(1)} all-to-all(f32[8,32,512]{2,1,0:T(8,128)S(1)} %get-tuple-element.29), channel_id=1, replica_groups=mesh['rows'=32,'cols'=8] {'cols'}, dimensions={0} | all-to-all | bytes 1048576 | tf_op jit(solution)/shard_map/all_to_all | solution.py:368
  47.8 0.4 gram.1
  48.2 4.1 %collective-permute-start.4 = (f32[8,32,128]{2,1,0:T(8,128)S(1)}, f32[8,32,128]{2,1,0:T(8,128)S(1)}, u32[]{:S(2)}, u32[]{:S(2)}) collective-permute-start(f32[8,32,128]{2,1,0:T(8,128)S(1)} %get-tuple-element.31), channel_id=1, source_target_pairs={{0,8},{8,0},{16,24},{24,16},{32,40},{40,32},{48,56},{56,48},{64,72... | collective-permute-start | bytes 393224 | tf_op jit(solution)/shard_map/ppermute | solution.py:378
  52.3 1.0 %collective-permute-done.4 = f32[8,32,128]{2,1,0:T(8,128)S(1)} collective-permute-done((f32[8,32,128]{2,1,0:T(8,128)S(1)}, f32[8,32,128]{2,1,0:T(8,128)S(1)}, u32[]{:S(2)}, u32[]{:S(2)}) %collective-permute-start.4) | collective-permute-done | bytes 131104 | tf_op jit(solution)/shard_map/ppermute | solution.py:378
  53.3 10.8 %all_to_all.16 = f32[8,32,128]{2,1,0:T(8,128)S(1)} all-to-all(f32[8,32,128]{2,1,0:T(8,128)S(1)} %add.3), channel_id=1, replica_groups=mesh['rows'=32,'cols'=8] {'cols'}, dimensions={0} | all-to-all | bytes 262144 | tf_op jit(solution)/shard_map/all_to_all | solution.py:378
  64.1 10.9 %all_to_all.17 = f32[16,32,128]{2,1,0:T(8,128)S(1)} all-to-all(f32[16,32,128]{2,1,0:T(8,128)S(1)} %broadcast_in_dim.2), channel_id=1, replica_groups={{0,16,32,48,64,80,96,112,128,144,160,176,192,208,224,240},{8,24,40,56,7..., dimensions={0} | all-to-all | bytes 524288 | tf_op jit(solution)/shard_map/all_to_all | solution.py:384
  75.1 2.9 %collective-permute-start.5 = (f32[32,128]{1,0:T(8,128)S(1)}, f32[32,128]{1,0:T(8,128)S(1)}, u32[]{:S(2)}, u32[]{:S(2)}) collective-permute-start(f32[32,128]{1,0:T(8,128)S(1)} %reduce_sum.19.mine), channel_id=1, source_target_pairs={{0,8},{8,0},{16,24},{24,16},{32,40},{40,32},{48,56},{56,48},{64,72... | collective-permute-start | bytes 49160 | tf_op jit(solution)/shard_map/ppermute | solution.py:386
  78.0 0.8 %collective-permute-done.5.other = f32[32,128]{1,0:T(8,128)S(1)} collective-permute-done((f32[32,128]{1,0:T(8,128)S(1)}, f32[32,128]{1,0:T(8,128)S(1)}, u32[]{:S(2)}, u32[]{:S(2)}) %collective-permute-start.5) | collective-permute-done | bytes 16416 | tf_op jit(solution)/shard_map/ppermute | solution.py:386
  78.9 0.6 join.1
  (4 shorter events, 0.1 us)
Async XLA Ops:
  1.5 10.6 %collective-permute-start = (f32[32,512]{1,0:T(8,128)S(1)}, f32[32,512]{1,0:T(8,128)S(1)}, u32[]{:S(2)}, u32[]{:S(2)}) collective-permute-start(f32[32,512]{1,0:T(8,128)S(1)} %get-tuple-element.20), channel_id=1, source_target_pairs={{0,8},{8,0},{16,24},{24,16},{32,40},{40,32},{48,56},{56,48},{64,72... | collective-permute-start | bytes 196616 | tf_op jit(solution)/shard_map/ppermute | solution.py:296
  4.9 7.3 %collective-permute-start.1 = (f32[32,512]{1,0:T(8,128)S(1)}, f32[32,512]{1,0:T(8,128)S(1)}, u32[]{:S(2)}, u32[]{:S(2)}) collective-permute-start(f32[32,512]{1,0:T(8,128)S(1)} %get-tuple-element.21), channel_id=1, source_target_pairs={{0,248},{8,16},{16,8},{24,32},{32,24},{40,48},{48,40},{56,64},{64,... | collective-permute-start | bytes 196616 | tf_op jit(solution)/shard_map/ppermute | solution.py:295
  14.0 8.8 %collective-permute-start.2 = (f32[32,512]{1,0:T(8,128)S(1)}, f32[32,512]{1,0:T(8,128)S(1)}, u32[]{:S(2)}, u32[]{:S(2)}) collective-permute-start(f32[32,512]{1,0:T(8,128)S(1)} %get-tuple-element.24), channel_id=1, source_target_pairs={{0,8},{8,0},{16,24},{24,16},{32,40},{40,32},{48,56},{56,48},{64,72... | collective-permute-start | bytes 196616 | tf_op jit(solution)/shard_map/ppermute | solution.py:296
  17.6 5.2 %collective-permute-start.3 = (f32[32,512]{1,0:T(8,128)S(1)}, f32[32,512]{1,0:T(8,128)S(1)}, u32[]{:S(2)}, u32[]{:S(2)}) collective-permute-start(f32[32,512]{1,0:T(8,128)S(1)} %get-tuple-element.25), channel_id=1, source_target_pairs={{0,248},{8,16},{16,8},{24,32},{32,24},{40,48},{48,40},{56,64},{64,... | collective-permute-start | bytes 196616 | tf_op jit(solution)/shard_map/ppermute | solution.py:295
  48.2 5.0 %collective-permute-start.4 = (f32[8,32,128]{2,1,0:T(8,128)S(1)}, f32[8,32,128]{2,1,0:T(8,128)S(1)}, u32[]{:S(2)}, u32[]{:S(2)}) collective-permute-start(f32[8,32,128]{2,1,0:T(8,128)S(1)} %get-tuple-element.31), channel_id=1, source_target_pairs={{0,8},{8,0},{16,24},{24,16},{32,40},{40,32},{48,56},{56,48},{64,72... | collective-permute-start | bytes 393224 | tf_op jit(solution)/shard_map/ppermute | solution.py:378
  75.1 3.7 %collective-permute-start.5 = (f32[32,128]{1,0:T(8,128)S(1)}, f32[32,128]{1,0:T(8,128)S(1)}, u32[]{:S(2)}, u32[]{:S(2)}) collective-permute-start(f32[32,128]{1,0:T(8,128)S(1)} %reduce_sum.19.mine), channel_id=1, source_target_pairs={{0,8},{8,0},{16,24},{24,16},{32,40},{40,32},{48,56},{56,48},{64,72... | collective-permute-start | bytes 49160 | tf_op jit(solution)/shard_map/ppermute | solution.py:386

commit v4 on v3

--- a/solution.py
+++ b/solution.py
@@ -110,7 +110,7 @@
     cols, counts, h, field, onsite, out, table, sems, small,
 ):
     count = local - 2 * REACH
-    unroll = 4
+    unroll = 8
 
     def fetch(row):
         return pltpu.make_async_copy(h_hbm.at[row], h.at[row], sems.at[row])
@@ -165,7 +165,7 @@
             (field, local - 2 * REACH, local - REACH, 2 * REACH),
         ],
     )
-    unroll = 4
+    unroll = 8
 
     def step(s, carry):
         for u in range(unroll):
@@ -193,7 +193,7 @@
             (edge, REACH, local, REACH),
         ],
     )
-    unroll = 4
+    unroll = 8
 
     def step(s, carry):
         for u in range(unroll):
@@ -222,7 +222,7 @@
         ],
     )
     out[:, REACH * BLOCK : (local - REACH) * BLOCK] = done[...]
-    unroll = 4
+    unroll = 8
 
     def step(s, carry):
         for u in range(unroll):
@@ -254,11 +254,15 @@
     give[...] = jnp.where(first, high, low)
 
 
-def join(mine, other, out):
-    first = is_first_core()
-    half = mine.shape[1]
-    out[:, :half] = jnp.where(first, mine[...], other[...])
-    out[:, half:] = jnp.where(first, other[...], mine[...])
+def join(side, terms, out):
+    count, width = terms.shape[1:]
+    for x in range(side):
+        for core in range(2):
+            total = None
+            for y in range(side):
+                one = terms[(x * side + y) * 2 + core]
+                total = one if total is None else total + one
+            out[x * count : (x + 1) * count, core * width : (core + 1) * width] = total
 
 
 def params(mebibytes):
@@ -375,23 +379,27 @@
         compiler_params=params(8),
         name="gram",
     )(parts)
-    terms = lax.all_to_all(keep + lax.ppermute(give, "rows", mate), "cols", 0, 0)
+    keep = keep + lax.ppermute(give, "rows", mate)
+
+    side = 4
+    share = vcount // side
+    same = []
+    for y in range(side):
+        for core in range(2):
+            at = [((x * side + y) * 2 + core) * groups for x in range(side)]
+            same.append([r + z for z in range(groups) for r in at])
+    terms = keep.reshape(groups * side, share, total // 2)
+    terms = lax.all_to_all(terms, ("rows", "cols"), 0, 0, axis_index_groups=same)
     mine = jnp.sum(terms, axis=0)
-
-    peers = ranks // 2
-    same = [[2 * i + core for i in range(peers)] for core in range(2)]
-    terms = jnp.broadcast_to(mine[None], (peers, *mine.shape))
-    terms = lax.all_to_all(terms, "rows", 0, 0, axis_index_groups=same)
-    mine = jnp.sum(terms, axis=0)
-    other = lax.ppermute(mine, "rows", mate)
+    terms = lax.all_to_all(jnp.broadcast_to(mine[None], (ranks, *mine.shape)), "rows", 0, 0)
     correlation = pl.pallas_call(
-        join,
-        in_specs=[VMEM, VMEM],
+        functools.partial(join, side),
+        in_specs=[VMEM],
         out_specs=VMEM,
         out_shape=shape(vcount, total),
         compiler_params=params(8),
         name="join",
-    )(mine, other)
+    )(terms)
     return (filtered, correlation)
 
 

time: 79.7 us -> 79.1 us (level)
  blocking collectives: 44.2 us -> 47.8 us
  starting transfers between devices: 14 us -> 11.1 us
  waiting for transfers between devices: 1.84 us -> 1 us
    all_to_all x2, blocking collectives: 21.7 us -> 25.4 us  [the longest x1 12.8 us: on_device(): lax.all_to_all(terms, ('rows', 'cols'), 0, 0, axis_index_groups=same)]
    ppermute x2 -> x1, starting transfers between devices: 6.97 us -> 4.13 us  [on_device(): keep = keep + lax.ppermute(give, 'rows', mate)]
    ppermute x2 -> x1, waiting for transfers between devices: 1.83 us -> 0.99 us  [on_device(): keep = keep + lax.ppermute(give, 'rows', mate)]
  transfers between devices with their start and end apart: 6 -> 5, of which waited for: 2 -> 1; matrix products, arithmetic and copies ran while one was open for 0% -> 0% of each run, Pallas kernels for 16% -> 16%
where the time goes in v4:
time: 79.1 us; the launch traced here: 78.9 us
  blocking collectives  47.8 us (60%)
  Pallas kernels  18.2 us (23%)
  starting transfers between devices  11.1 us (14%)
  waiting for transfers between devices  1 us (1%)
    all_to_all x1, blocking collectives, on_device(): parts = lax.all_to_all(parts, 'cols', 0, 0)  22.4 us
    all_to_all x1, blocking collectives, on_device(): lax.all_to_all(terms, ('rows', 'cols'), 0, 0, axis_index_groups=same)  12.8 us
    all_to_all x1, blocking collectives, on_device(): lax.all_to_all(jnp.broadcast_to(mine[None], (ranks, *mine.shape)), 'rows'...  12.6 us
    pallas_call x1, Pallas kernels, on_device(): pl.pallas_call(functools.partial(first_inner, nblocks, local), in_specs=[...  7.6 us
    ppermute x2, starting transfers between devices, around(): return (lax.ppermute(near, 'rows', mate), far)  7 us
    pallas_call x1, Pallas kernels, on_device(): pl.pallas_call(functools.partial(second_inner, nblocks, local), in_specs=...  4.76 us
    ppermute x1, starting transfers between devices, on_device(): keep = keep + lax.ppermute(give, 'rows', mate)  4.13 us
    pallas_call x1, Pallas kernels, on_device(): pl.pallas_call(functools.partial(second_edge, nblocks, local), in_specs=[...  2.36 us
  transfers between devices with their start and end apart: 5, of which 1 were waited for; matrix products, arithmetic and copies ran while one was open for 0% of the time, Pallas kernels for 16%

profile of v4, /device:TPU:1, one launch (start us, length us, event | category | flops | bytes accessed | tf_op | source)
XLA Modules:
  0.0 78.9 jit_solution(18072629329446505739)
XLA Ops:
  0.6 0.9 %ends.1 = (f32[32,512]{1,0:T(8,128)S(1)}, f32[32,512]{1,0:T(8,128)S(1)}) custom-call(f32[32,4096]{1,0:T(8,128)} %field_hbm.3), custom_call_target="tpu_custom_call" | custom-call | tf_op jit(solution)/shard_map/ends/pallas_call | solution.py:305
  1.5 3.3 %collective-permute-start = (f32[32,512]{1,0:T(8,128)S(1)}, f32[32,512]{1,0:T(8,128)S(1)}, u32[]{:S(2)}, u32[]{:S(2)}) collective-permute-start(f32[32,512]{1,0:T(8,128)S(1)} %get-tuple-element.20), channel_id=1, source_target_pairs={{0,8},{8,0},{16,24},{24,16},{32,40},{40,32},{48,56},{56,48},{64,72... | collective-permute-start | bytes 196616 | tf_op jit(solution)/shard_map/ppermute | solution.py:300
  4.9 0.0 collective-permute-start.1
  4.9 7.6 %first_inner.1 = (s32[9,32]{1,0:T(8,128)S(4)}, s32[32]{0:T(128)S(4)}, f32[32,9,128,128]{3,2,1,0:T(8,128)S(1)}, f32[32,4096]{1,0:T(8,128)S(1)}, f32[32,128]{1,0:T(8,128)S(1)}, /*index=5*/f32[32,3072]{1,0:T(8,128)S(1)}) custom-call(s32[9,32]{1,0:T(8,128)} %bitcast.5, s32[32]{0:T(128)} %counts_hbm.1, f32[32,128]{1,0:T(8,128)} %bitcast.4, f32[32,4096]{1,0:T(8,128)} %field_hbm.3, ...), custom_call_target="tpu_custom_call" | custom-call | flops 1207959552 | bytes 18874368 | tf_op jit(solution)/shard_map/first_inner/pallas_call | solution.py:316
  12.5 0.0 collective-permute-done.near
  12.5 0.0 collective-permute-done.1.far
  12.5 1.6 %first_edge.1 = (f32[32,1024]{1,0:T(8,128)S(1)}, f32[32,512]{1,0:T(8,128)S(1)}, f32[32,512]{1,0:T(8,128)S(1)}) custom-call(s32[9,32]{1,0:T(8,128)S(4)} %get-tuple-element.17.cols, s32[32]{0:T(128)S(4)} %get-tuple-element.18.counts, f32[32,128]{1,0:T(8,128)S(1)} %get-tuple-element.19.onsite, f32[32,512]{1,0:T(8,128)S(1)} %collective-permute-done.near, ...), custom_call_target="tpu_custom_call" | custom-call | flops 301989888 | bytes 4718592 | tf_op jit(solution)/shard_map/first_edge/pallas_call | solution.py:338
  14.1 3.7 %collective-permute-start.2 = (f32[32,512]{1,0:T(8,128)S(1)}, f32[32,512]{1,0:T(8,128)S(1)}, u32[]{:S(2)}, u32[]{:S(2)}) collective-permute-start(f32[32,512]{1,0:T(8,128)S(1)} %get-tuple-element.24), channel_id=1, source_target_pairs={{0,8},{8,0},{16,24},{24,16},{32,40},{40,32},{48,56},{56,48},{64,72... | collective-permute-start | bytes 196616 | tf_op jit(solution)/shard_map/ppermute | solution.py:300
  17.8 0.0 collective-permute-start.3
  17.8 4.8 %second_inner.1.done = f32[32,3072]{1,0:T(8,128)S(1)} custom-call(s32[9,32]{1,0:T(8,128)S(4)} %get-tuple-element.17.cols, s32[32]{0:T(128)S(4)} %get-tuple-element.18.counts, f32[32,128]{1,0:T(8,128)S(1)} %get-tuple-element.19.onsite, f32[32,1024]{1,0:T(8,128)S(1)} %get-tuple-element.26.edge, f32[32,3072]{1,0:T(8,128)S(1)} %get-tuple-element.27.inner, ...), custom_call_target="tpu_custom_call" | custom-call | flops 905969664 | bytes 14155776 | tf_op jit(solution)/shard_map/second_inner/pallas_call | solution.py:350
  22.5 0.0 collective-permute-done.2.near
  22.5 0.0 collective-permute-done.3.far
  22.5 2.4 %second_edge.1 = (f32[32,4096]{1,0:T(8,128)}, f32[8,32,512]{2,1,0:T(8,128)S(1)}) custom-call(s32[9,32]{1,0:T(8,128)S(4)} %get-tuple-element.17.cols, s32[32]{0:T(128)S(4)} %get-tuple-element.18.counts, f32[32,128]{1,0:T(8,128)S(1)} %get-tuple-element.19.onsite, f32[32,512]{1,0:T(8,128)S(1)} %collective-permute-done.2.near, ...), custom_call_target="tpu_custom_call" | custom-call | flops 301989888 | bytes 4718592 | tf_op jit(solution)/shard_map/second_edge/pallas_call | solution.py:361
  24.9 22.4 %all_to_all.15.parts = f32[8,32,512]{2,1,0:T(8,128)S(1)} all-to-all(f32[8,32,512]{2,1,0:T(8,128)S(1)} %get-tuple-element.29), channel_id=1, replica_groups=mesh['rows'=32,'cols'=8] {'cols'}, dimensions={0} | all-to-all | bytes 1048576 | tf_op jit(solution)/shard_map/all_to_all | solution.py:372
  47.3 0.4 gram.1
  47.7 4.1 %collective-permute-start.4 = (f32[8,32,128]{2,1,0:T(8,128)S(1)}, f32[8,32,128]{2,1,0:T(8,128)S(1)}, u32[]{:S(2)}, u32[]{:S(2)}) collective-permute-start(f32[8,32,128]{2,1,0:T(8,128)S(1)} %get-tuple-element.31), channel_id=1, source_target_pairs={{0,8},{8,0},{16,24},{24,16},{32,40},{40,32},{48,56},{56,48},{64,72... | collective-permute-start | bytes 393224 | tf_op jit(solution)/shard_map/ppermute | solution.py:382
  51.8 1.0 %collective-permute-done.4 = f32[8,32,128]{2,1,0:T(8,128)S(1)} collective-permute-done((f32[8,32,128]{2,1,0:T(8,128)S(1)}, f32[8,32,128]{2,1,0:T(8,128)S(1)}, u32[]{:S(2)}, u32[]{:S(2)}) %collective-permute-start.4) | collective-permute-done | bytes 131104 | tf_op jit(solution)/shard_map/ppermute | solution.py:382
  52.8 12.8 %all_to_all.16 = f32[32,8,128]{2,1,0:T(8,128)S(1)} all-to-all(f32[32,8,128]{2,1,0:T(8,128)S(1)} %bitcast.3), channel_id=1, replica_groups={{0,64,128,192,1,65,129,193,2,66,130,194,3,67,131,195,4,68,132,196,5,69,..., dimensions={0} | all-to-all | bytes 262144 | tf_op jit(solution)/shard_map/all_to_all | solution.py:392
  65.7 12.6 %all_to_all.17.terms = f32[32,8,128]{2,1,0:T(8,128)S(1)} all-to-all(f32[32,8,128]{2,1,0:T(8,128)S(1)} %broadcast_in_dim.2), channel_id=1, replica_groups=mesh['rows'=32,'cols'=8] {'rows'}, dimensions={0} | all-to-all | bytes 262144 | tf_op jit(solution)/shard_map/all_to_all | solution.py:394
  78.3 0.6 join.1
  (3 shorter events, 0.1 us)
Async XLA Ops:
  1.5 10.9 %collective-permute-start = (f32[32,512]{1,0:T(8,128)S(1)}, f32[32,512]{1,0:T(8,128)S(1)}, u32[]{:S(2)}, u32[]{:S(2)}) collective-permute-start(f32[32,512]{1,0:T(8,128)S(1)} %get-tuple-element.20), channel_id=1, source_target_pairs={{0,8},{8,0},{16,24},{24,16},{32,40},{40,32},{48,56},{56,48},{64,72... | collective-permute-start | bytes 196616 | tf_op jit(solution)/shard_map/ppermute | solution.py:300
  4.9 7.6 %collective-permute-start.1 = (f32[32,512]{1,0:T(8,128)S(1)}, f32[32,512]{1,0:T(8,128)S(1)}, u32[]{:S(2)}, u32[]{:S(2)}) collective-permute-start(f32[32,512]{1,0:T(8,128)S(1)} %get-tuple-element.21), channel_id=1, source_target_pairs={{0,248},{8,16},{16,8},{24,32},{32,24},{40,48},{48,40},{56,64},{64,... | collective-permute-start | bytes 196616 | tf_op jit(solution)/shard_map/ppermute | solution.py:299
  14.1 8.4 %collective-permute-start.2 = (f32[32,512]{1,0:T(8,128)S(1)}, f32[32,512]{1,0:T(8,128)S(1)}, u32[]{:S(2)}, u32[]{:S(2)}) collective-permute-start(f32[32,512]{1,0:T(8,128)S(1)} %get-tuple-element.24), channel_id=1, source_target_pairs={{0,8},{8,0},{16,24},{24,16},{32,40},{40,32},{48,56},{56,48},{64,72... | collective-permute-start | bytes 196616 | tf_op jit(solution)/shard_map/ppermute | solution.py:300
  17.8 4.8 %collective-permute-start.3 = (f32[32,512]{1,0:T(8,128)S(1)}, f32[32,512]{1,0:T(8,128)S(1)}, u32[]{:S(2)}, u32[]{:S(2)}) collective-permute-start(f32[32,512]{1,0:T(8,128)S(1)} %get-tuple-element.25), channel_id=1, source_target_pairs={{0,248},{8,16},{16,8},{24,32},{32,24},{40,48},{48,40},{56,64},{64,... | collective-permute-start | bytes 196616 | tf_op jit(solution)/shard_map/ppermute | solution.py:299
  47.7 5.1 %collective-permute-start.4 = (f32[8,32,128]{2,1,0:T(8,128)S(1)}, f32[8,32,128]{2,1,0:T(8,128)S(1)}, u32[]{:S(2)}, u32[]{:S(2)}) collective-permute-start(f32[8,32,128]{2,1,0:T(8,128)S(1)} %get-tuple-element.31), channel_id=1, source_target_pairs={{0,8},{8,0},{16,24},{24,16},{32,40},{40,32},{48,56},{56,48},{64,72... | collective-permute-start | bytes 393224 | tf_op jit(solution)/shard_map/ppermute | solution.py:382

commit v5 on v4

--- a/solution.py
+++ b/solution.py
@@ -44,12 +44,11 @@
     return jnp.where(first, local + REACH, 0), jnp.where(first, 0, local + REACH)
 
 
-def split_ends(ref, near, far, count):
-    width = count * BLOCK
-    first = is_first_core()
+def outer_end(ref, near):
+    width = REACH * BLOCK
     high = ref.shape[1] - width
-    near[...] = ref[:, pl.ds(pl.multiple_of(jnp.where(first, high, 0), BLOCK), width)]
-    far[...] = ref[:, pl.ds(pl.multiple_of(jnp.where(first, 0, high), BLOCK), width)]
+    start = jnp.where(is_first_core(), high, 0) if near else jnp.where(is_first_core(), 0, high)
+    return ref.at[:, pl.ds(pl.multiple_of(start, BLOCK), width)]
 
 
 def columns(ref, block):
@@ -89,28 +88,18 @@
     return (total + diag * columns(field, row)) / filter_half
 
 
-def ends(field_hbm, near, far, sems):
-    width = near.shape[1]
-    high = field_hbm.shape[1] - width
-    first = is_first_core()
-    copies = []
-    for n, (start, ref) in enumerate(
-        [(jnp.where(first, 0, high), far), (jnp.where(first, high, 0), near)]
-    ):
-        part = field_hbm.at[:, pl.ds(pl.multiple_of(start, BLOCK), width)]
-        copies.append(pltpu.make_async_copy(part, ref, sems.at[n]))
-    for copy in copies:
-        copy.start()
-    for copy in copies:
-        copy.wait()
+def far_end(field_hbm, far, sem):
+    copy = pltpu.make_async_copy(outer_end(field_hbm, False), far, sem.at[0])
+    copy.start()
+    copy.wait()
 
 
 def first_inner(
     nblocks, local, cols_hbm, counts_hbm, onsite_hbm, field_hbm, h_hbm,
-    cols, counts, h, field, onsite, out, table, sems, small,
+    cols, counts, h, field, onsite, out, near_out, table, sems, small,
 ):
     count = local - 2 * REACH
-    unroll = 8
+    unroll = 4
 
     def fetch(row):
         return pltpu.make_async_copy(h_hbm.at[row], h.at[row], sems.at[row])
@@ -131,6 +120,7 @@
     lax.fori_loop(0, local, begin, 0)
     for copy in copies:
         copy.wait()
+    near_out[...] = outer_end(field, True)[...]
     load_blocks(table, [(field, 0, REACH, local)])
 
     def step(s, carry):
@@ -153,7 +143,7 @@
 
 
 def first_edge(
-    nblocks, local, cols, counts, onsite, near, far, field, h, out, near_out, far_out, table
+    nblocks, local, cols, counts, onsite, near, far, field, h, out, far_out, table
 ):
     near_slot, far_slot = outer_slots(local)
     load_blocks(
@@ -176,7 +166,7 @@
         return carry
 
     lax.fori_loop(0, 2 * REACH // unroll, step, 0)
-    split_ends(out, near_out, far_out, REACH)
+    far_out[...] = outer_end(out, False)[...]
 
 
 def second_value(row, total, onsite, first, field):
@@ -184,7 +174,10 @@
     return 2.0 * (total + diag * first) / filter_half - columns(field, row)
 
 
-def second_inner(nblocks, local, cols, counts, onsite, edge, inner, field, h, out, table):
+def second_inner(
+    nblocks, local, cols, counts, onsite, edge, inner, field, h, out, near_out, table
+):
+    near_out[...] = outer_end(edge, True)[...]
     load_blocks(
         table,
         [
@@ -295,28 +288,24 @@
     mate = [(i, i ^ 1) for i in range(ranks)]
     beyond = [(i, (i + 1 if i % 2 else i - 1) % ranks) for i in range(ranks)]
 
-    def around(near, far):
-        far = lax.ppermute(far, "rows", beyond)
-        return lax.ppermute(near, "rows", mate), far
-
     def in_hbm(*arrays):
         return [pltpu.with_memory_space_constraint(x, pltpu.HBM) for x in arrays]
 
-    near, far = pl.pallas_call(
-        ends,
+    far = pl.pallas_call(
+        far_end,
         in_specs=[HBM],
-        out_specs=(VMEM, VMEM),
-        out_shape=(pltpu.VMEM((vcount, reach), f32), pltpu.VMEM((vcount, reach), f32)),
-        scratch_shapes=[pltpu.SemaphoreType.DMA((2,))],
-        compiler_params=params(8),
-        name="ends",
+        out_specs=VMEM,
+        out_shape=pltpu.VMEM((vcount, reach), f32),
+        scratch_shapes=[pltpu.SemaphoreType.DMA((1,))],
+        compiler_params=params(8),
+        name="far_end",
     )(*in_hbm(vectors))
-    near, far = around(near, far)
-
-    cols, counts, h, field, onsite, inner = pl.pallas_call(
+    far = lax.ppermute(far, "rows", beyond)
+
+    cols, counts, h, field, onsite, inner, near = pl.pallas_call(
         functools.partial(first_inner, nblocks, local),
         in_specs=[HBM] * 5,
-        out_specs=(SMEM,) * 2 + (VMEM,) * 4,
+        out_specs=(SMEM,) * 2 + (VMEM,) * 5,
         out_shape=(
             pltpu.SMEM(cols.shape, jnp.int32),
             pltpu.SMEM(block_counts.shape, jnp.int32),
@@ -324,6 +313,7 @@
             pltpu.VMEM(vectors.shape, f32),
             pltpu.VMEM(onsite.shape, f32),
             pltpu.VMEM((vcount, inner_rows * BLOCK), f32),
+            pltpu.VMEM((vcount, reach), f32),
         ),
         scratch_shapes=[
             table,
@@ -335,28 +325,32 @@
         name="first_inner",
     )(*in_hbm(cols, block_counts, onsite, vectors, h_blocks))
 
-    edge, near, far = pl.pallas_call(
+    near = lax.ppermute(near, "rows", mate)
+
+    edge, far = pl.pallas_call(
         functools.partial(first_edge, nblocks, local),
         in_specs=[SMEM, SMEM] + [VMEM] * 5,
-        out_specs=(VMEM,) * 3,
-        out_shape=(shape(vcount, 2 * reach), shape(vcount, reach), shape(vcount, reach)),
+        out_specs=(VMEM,) * 2,
+        out_shape=(shape(vcount, 2 * reach), shape(vcount, reach)),
         scratch_shapes=[table],
         compiler_params=params(8),
         cost_estimate=cost(edge_rows, slots, vcount),
         name="first_edge",
     )(cols, counts, onsite, near, far, field, h)
-    near, far = around(near, far)
-
-    done = pl.pallas_call(
+    far = lax.ppermute(far, "rows", beyond)
+
+    done, near = pl.pallas_call(
         functools.partial(second_inner, nblocks, local),
         in_specs=[SMEM, SMEM] + [VMEM] * 5,
-        out_specs=VMEM,
-        out_shape=shape(vcount, inner_rows * BLOCK),
+        out_specs=(VMEM, VMEM),
+        out_shape=(shape(vcount, inner_rows * BLOCK), shape(vcount, reach)),
         scratch_shapes=[table],
         compiler_params=params(8),
         cost_estimate=cost(inner_rows, slots, vcount),
         name="second_inner",
     )(cols, counts, onsite, edge, inner, field, h)
+
+    near = lax.ppermute(near, "rows", mate)
 
     filtered, parts = pl.pallas_call(
         functools.partial(second_edge, nblocks, local),

time: 79.1 us -> 83.1 us (1.051)
  blocking collectives: 47.8 us -> 49.7 us
  waiting for transfers between devices: 1 us -> 2.79 us
    all_to_all x1, blocking collectives: 12.6 us -> 15.2 us  [on_device(): lax.all_to_all(jnp.broadcast_to(mine[None], (ranks, *mine.shape)), 'rows'...]
    ppermute x4, starting transfers between devices: 7 us -> 8.99 us  [the longest x2 6.12 us: on_device(): near = lax.ppermute(near, 'rows', mate)]
    ppermute x4, waiting for transfers between devices: 0.01 us -> 1.8 us  [the longest x2 1.8 us: on_device(): near = lax.ppermute(near, 'rows', mate)]
    ppermute x1, starting transfers between devices: 4.13 us -> 2.71 us  [on_device(): keep = keep + lax.ppermute(give, 'rows', mate)]
  transfers between devices with their start and end apart: 5 -> 5, of which waited for: 1 -> 3; matrix products, arithmetic and copies ran while one was open for 0% -> 0% of each run, Pallas kernels for 16% -> 15%
where the time goes in v5:
time: 83.1 us; the launch traced here: 82.9 us
  blocking collectives  49.7 us (60%)
  Pallas kernels  17.9 us (22%)
  starting transfers between devices  11.7 us (14%)
  waiting for transfers between devices  2.79 us (3%)
    all_to_all x1, blocking collectives, on_device(): parts = lax.all_to_all(parts, 'cols', 0, 0)  22.1 us
    all_to_all x1, blocking collectives, on_device(): lax.all_to_all(jnp.broadcast_to(mine[None], (ranks, *mine.shape)), 'rows'...  15.2 us
    all_to_all x1, blocking collectives, on_device(): lax.all_to_all(terms, ('rows', 'cols'), 0, 0, axis_index_groups=same)  12.4 us
    pallas_call x1, Pallas kernels, on_device(): pl.pallas_call(functools.partial(first_inner, nblocks, local), in_specs=[...  7.3 us
    ppermute x2, starting transfers between devices, on_device(): near = lax.ppermute(near, 'rows', mate)  6.12 us
    pallas_call x1, Pallas kernels, on_device(): pl.pallas_call(functools.partial(second_inner, nblocks, local), in_specs=...  4.77 us
    ppermute x2, starting transfers between devices, on_device(): far = lax.ppermute(far, 'rows', beyond)  2.87 us
    ppermute x1, starting transfers between devices, on_device(): keep = keep + lax.ppermute(give, 'rows', mate)  2.71 us
  transfers between devices with their start and end apart: 5, of which 3 were waited for; matrix products, arithmetic and copies ran while one was open for 0% of the time, Pallas kernels for 15%

profile of v5, /device:TPU:1, one launch (start us, length us, event | category | flops | bytes accessed | tf_op | source)
XLA Modules:
  0.0 82.9 jit_solution(2810853450107807320)
XLA Ops:
  0.6 0.9 %far_end.1 = f32[32,512]{1,0:T(8,128)S(1)} custom-call(f32[32,4096]{1,0:T(8,128)} %field_hbm.3), custom_call_target="tpu_custom_call" | custom-call | tf_op jit(solution)/shard_map/far_end/pallas_call | solution.py:294
  1.5 2.8 %collective-permute-start.1 = (f32[32,512]{1,0:T(8,128)S(1)}, f32[32,512]{1,0:T(8,128)S(1)}, u32[]{:S(2)}, u32[]{:S(2)}) collective-permute-start(f32[32,512]{1,0:T(8,128)S(1)} %far_end.1), channel_id=1, source_target_pairs={{0,248},{8,16},{16,8},{24,32},{32,24},{40,48},{48,40},{56,64},{64,... | collective-permute-start | bytes 196616 | tf_op jit(solution)/shard_map/ppermute | solution.py:303
  4.3 7.3 %first_inner.1 = (s32[9,32]{1,0:T(8,128)S(4)}, s32[32]{0:T(128)S(4)}, f32[32,9,128,128]{3,2,1,0:T(8,128)S(1)}, f32[32,4096]{1,0:T(8,128)S(1)}, f32[32,128]{1,0:T...) custom-call(s32[9,32]{1,0:T(8,128)} %bitcast.5, s32[32]{0:T(128)} %counts_hbm.1, f32[32,128]{1,0:T(8,128)} %bitcast.4, ...), custom_call_target="tpu_custom_call" | custom-call | flops 1207959552 | bytes 18874368 | tf_op jit(solution)/shard_map/first_inner/pallas_call | solution.py:305
  11.6 3.6 %collective-permute-start = (f32[32,512]{1,0:T(8,128)S(1)}, f32[32,512]{1,0:T(8,128)S(1)}, u32[]{:S(2)}, u32[]{:S(2)}) collective-permute-start(f32[32,512]{1,0:T(8,128)S(1)} %get-tuple-element.20), channel_id=1, source_target_pairs={{0,8},{8,0},{16,24},{24,16},{32,40},{40,32},{48,56},{56,48},{64,72... | collective-permute-start | bytes 196616 | tf_op jit(solution)/shard_map/ppermute | solution.py:328
  15.1 0.0 collective-permute-done.1.far
  15.1 0.9 %collective-permute-done.near = f32[32,512]{1,0:T(8,128)S(1)} collective-permute-done((f32[32,512]{1,0:T(8,128)S(1)}, f32[32,512]{1,0:T(8,128)S(1)}, u32[]{:S(2)}, u32[]{:S(2)}) %collective-permute-start) | collective-permute-done | bytes 65568 | tf_op jit(solution)/shard_map/ppermute | solution.py:328
  16.0 1.6 %first_edge.1 = (f32[32,1024]{1,0:T(8,128)S(1)}, f32[32,512]{1,0:T(8,128)S(1)}) custom-call(s32[9,32]{1,0:T(8,128)S(4)} %get-tuple-element.17.cols, s32[32]{0:T(128)S(4)} %get-tuple-element.18.counts, f32[32,128]{1,0:T(8,128)S(1)} %get-tuple-element.19.onsite, f32[32,512]{1,0:T(8,128)S(1)} %collective-permute-done.near, ...), custom_call_target="tpu_custom_call" | custom-call | flops 301989888 | bytes 4718592 | tf_op jit(solution)/shard_map/first_edge/pallas_call | solution.py:330
  17.6 0.1 collective-permute-start.3
  17.7 4.8 %second_inner.1 = (f32[32,3072]{1,0:T(8,128)S(1)}, f32[32,512]{1,0:T(8,128)S(1)}) custom-call(s32[9,32]{1,0:T(8,128)S(4)} %get-tuple-element.17.cols, s32[32]{0:T(128)S(4)} %get-tuple-element.18.counts, f32[32,128]{1,0:T(8,128)S(1)} %get-tuple-element.19.onsite, f32[32,1024]{1,0:T(8,128)S(1)} %get-tuple-element.23.edge, ...), custom_call_target="tpu_custom_call" | custom-call | flops 905969664 | bytes 14155776 | tf_op jit(solution)/shard_map/second_inner/pallas_call | solution.py:342
  22.5 2.6 %collective-permute-start.2 = (f32[32,512]{1,0:T(8,128)S(1)}, f32[32,512]{1,0:T(8,128)S(1)}, u32[]{:S(2)}, u32[]{:S(2)}) collective-permute-start(f32[32,512]{1,0:T(8,128)S(1)} %get-tuple-element.25), channel_id=1, source_target_pairs={{0,8},{8,0},{16,24},{24,16},{32,40},{40,32},{48,56},{56,48},{64,72... | collective-permute-start | bytes 196616 | tf_op jit(solution)/shard_map/ppermute | solution.py:353
  25.1 0.0 collective-permute-done.3.far
  25.1 0.9 %collective-permute-done.2.near = f32[32,512]{1,0:T(8,128)S(1)} collective-permute-done((f32[32,512]{1,0:T(8,128)S(1)}, f32[32,512]{1,0:T(8,128)S(1)}, u32[]{:S(2)}, u32[]{:S(2)}) %collective-permute-start.2) | collective-permute-done | bytes 65568 | tf_op jit(solution)/shard_map/ppermute | solution.py:353
  26.0 2.4 %second_edge.1 = (f32[32,4096]{1,0:T(8,128)}, f32[8,32,512]{2,1,0:T(8,128)S(1)}) custom-call(s32[9,32]{1,0:T(8,128)S(4)} %get-tuple-element.17.cols, s32[32]{0:T(128)S(4)} %get-tuple-element.18.counts, f32[32,128]{1,0:T(8,128)S(1)} %get-tuple-element.19.onsite, f32[32,512]{1,0:T(8,128)S(1)} %collective-permute-done.2.near, ...), custom_call_target="tpu_custom_call" | custom-call | flops 301989888 | bytes 4718592 | tf_op jit(solution)/shard_map/second_edge/pallas_call | solution.py:355
  28.3 22.1 %all_to_all.15.parts = f32[8,32,512]{2,1,0:T(8,128)S(1)} all-to-all(f32[8,32,512]{2,1,0:T(8,128)S(1)} %get-tuple-element.29), channel_id=1, replica_groups=mesh['rows'=32,'cols'=8] {'cols'}, dimensions={0} | all-to-all | bytes 1048576 | tf_op jit(solution)/shard_map/all_to_all | solution.py:366
  50.5 0.4 gram.1
  50.9 2.7 %collective-permute-start.4 = (f32[8,32,128]{2,1,0:T(8,128)S(1)}, f32[8,32,128]{2,1,0:T(8,128)S(1)}, u32[]{:S(2)}, u32[]{:S(2)}) collective-permute-start(f32[8,32,128]{2,1,0:T(8,128)S(1)} %get-tuple-element.31), channel_id=1, source_target_pairs={{0,8},{8,0},{16,24},{24,16},{32,40},{40,32},{48,56},{56,48},{64,72... | collective-permute-start | bytes 393224 | tf_op jit(solution)/shard_map/ppermute | solution.py:376
  53.6 1.0 %collective-permute-done.4 = f32[8,32,128]{2,1,0:T(8,128)S(1)} collective-permute-done((f32[8,32,128]{2,1,0:T(8,128)S(1)}, f32[8,32,128]{2,1,0:T(8,128)S(1)}, u32[]{:S(2)}, u32[]{:S(2)}) %collective-permute-start.4) | collective-permute-done | bytes 131104 | tf_op jit(solution)/shard_map/ppermute | solution.py:376
  54.6 12.4 %all_to_all.16 = f32[32,8,128]{2,1,0:T(8,128)S(1)} all-to-all(f32[32,8,128]{2,1,0:T(8,128)S(1)} %bitcast.3), channel_id=1, replica_groups={{0,64,128,192,1,65,129,193,2,66,130,194,3,67,131,195,4,68,132,196,5,69,..., dimensions={0} | all-to-all | bytes 262144 | tf_op jit(solution)/shard_map/all_to_all | solution.py:386
  67.1 15.2 %all_to_all.17.terms = f32[32,8,128]{2,1,0:T(8,128)S(1)} all-to-all(f32[32,8,128]{2,1,0:T(8,128)S(1)} %broadcast_in_dim.2), channel_id=1, replica_groups=mesh['rows'=32,'cols'=8] {'rows'}, dimensions={0} | all-to-all | bytes 262144 | tf_op jit(solution)/shard_map/all_to_all | solution.py:388
  82.3 0.6 join.1
  (3 shorter events, 0.1 us)
Async XLA Ops:
  1.5 13.6 %collective-permute-start.1 = (f32[32,512]{1,0:T(8,128)S(1)}, f32[32,512]{1,0:T(8,128)S(1)}, u32[]{:S(2)}, u32[]{:S(2)}) collective-permute-start(f32[32,512]{1,0:T(8,128)S(1)} %far_end.1), channel_id=1, source_target_pairs={{0,248},{8,16},{16,8},{24,32},{32,24},{40,48},{48,40},{56,64},{64,... | collective-permute-start | bytes 196616 | tf_op jit(solution)/shard_map/ppermute | solution.py:303
  11.6 4.5 %collective-permute-start = (f32[32,512]{1,0:T(8,128)S(1)}, f32[32,512]{1,0:T(8,128)S(1)}, u32[]{:S(2)}, u32[]{:S(2)}) collective-permute-start(f32[32,512]{1,0:T(8,128)S(1)} %get-tuple-element.20), channel_id=1, source_target_pairs={{0,8},{8,0},{16,24},{24,16},{32,40},{40,32},{48,56},{56,48},{64,72... | collective-permute-start | bytes 196616 | tf_op jit(solution)/shard_map/ppermute | solution.py:328
  17.6 7.5 %collective-permute-start.3 = (f32[32,512]{1,0:T(8,128)S(1)}, f32[32,512]{1,0:T(8,128)S(1)}, u32[]{:S(2)}, u32[]{:S(2)}) collective-permute-start(f32[32,512]{1,0:T(8,128)S(1)} %get-tuple-element.26), channel_id=1, source_target_pairs={{0,248},{8,16},{16,8},{24,32},{32,24},{40,48},{48,40},{56,64},{64,... | collective-permute-start | bytes 196616 | tf_op jit(solution)/shard_map/ppermute | solution.py:340
  22.5 3.5 %collective-permute-start.2 = (f32[32,512]{1,0:T(8,128)S(1)}, f32[32,512]{1,0:T(8,128)S(1)}, u32[]{:S(2)}, u32[]{:S(2)}) collective-permute-start(f32[32,512]{1,0:T(8,128)S(1)} %get-tuple-element.25), channel_id=1, source_target_pairs={{0,8},{8,0},{16,24},{24,16},{32,40},{40,32},{48,56},{56,48},{64,72... | collective-permute-start | bytes 196616 | tf_op jit(solution)/shard_map/ppermute | solution.py:353
  50.9 3.7 %collective-permute-start.4 = (f32[8,32,128]{2,1,0:T(8,128)S(1)}, f32[8,32,128]{2,1,0:T(8,128)S(1)}, u32[]{:S(2)}, u32[]{:S(2)}) collective-permute-start(f32[8,32,128]{2,1,0:T(8,128)S(1)} %get-tuple-element.31), channel_id=1, source_target_pairs={{0,8},{8,0},{16,24},{24,16},{32,40},{40,32},{48,56},{56,48},{64,72... | collective-permute-start | bytes 393224 | tf_op jit(solution)/shard_map/ppermute | solution.py:376

commit v6 on v4

--- a/solution.py
+++ b/solution.py
@@ -110,7 +110,7 @@
     cols, counts, h, field, onsite, out, table, sems, small,
 ):
     count = local - 2 * REACH
-    unroll = 8
+    unroll = 4
 
     def fetch(row):
         return pltpu.make_async_copy(h_hbm.at[row], h.at[row], sems.at[row])
@@ -254,7 +254,9 @@
     give[...] = jnp.where(first, high, low)
 
 
-def join(side, terms, out):
+def join(side, terms, filtered, filtered_hbm, out_hbm, out, sems):
+    write = pltpu.make_async_copy(filtered, filtered_hbm, sems.at[0])
+    write.start()
     count, width = terms.shape[1:]
     for x in range(side):
         for core in range(2):
@@ -263,6 +265,10 @@
                 one = terms[(x * side + y) * 2 + core]
                 total = one if total is None else total + one
             out[x * count : (x + 1) * count, core * width : (core + 1) * width] = total
+    last = pltpu.make_async_copy(out, out_hbm, sems.at[1])
+    last.start()
+    write.wait()
+    last.wait()
 
 
 def params(mebibytes):
@@ -362,7 +368,10 @@
         functools.partial(second_edge, nblocks, local),
         in_specs=[SMEM, SMEM] + [VMEM] * 8,
         out_specs=(VMEM, VMEM),
-        out_shape=(shape(vcount, width), shape(groups, vcount, width // groups)),
+        out_shape=(
+            pltpu.VMEM((vcount, width), f32),
+            shape(groups, vcount, width // groups),
+        ),
         scratch_shapes=[table],
         compiler_params=params(8),
         cost_estimate=cost(edge_rows, slots, vcount),
@@ -392,14 +401,15 @@
     terms = lax.all_to_all(terms, ("rows", "cols"), 0, 0, axis_index_groups=same)
     mine = jnp.sum(terms, axis=0)
     terms = lax.all_to_all(jnp.broadcast_to(mine[None], (ranks, *mine.shape)), "rows", 0, 0)
-    correlation = pl.pallas_call(
+    filtered, correlation = pl.pallas_call(
         functools.partial(join, side),
-        in_specs=[VMEM],
-        out_specs=VMEM,
-        out_shape=shape(vcount, total),
+        in_specs=[VMEM, VMEM],
+        out_specs=(HBM, HBM),
+        out_shape=(shape(vcount, width), shape(vcount, total)),
+        scratch_shapes=[pltpu.VMEM((vcount, total), f32), pltpu.SemaphoreType.DMA((2,))],
         compiler_params=params(8),
         name="join",
-    )(terms)
+    )(terms, filtered)
     return (filtered, correlation)
 
 

time: 79.1 us -> 78.3 us (0.990)
  Pallas kernels: 18.2 us -> 17.3 us
  transfers between devices with their start and end apart: 5 -> 5, of which waited for: 1 -> 1; matrix products, arithmetic and copies ran while one was open for 0% -> 0% of each run, Pallas kernels for 16% -> 15%
where the time goes in v6:
time: 78.3 us; the launch traced here: 78 us
  blocking collectives  47.8 us (61%)
  Pallas kernels  17.3 us (22%)
  starting transfers between devices  11.1 us (14%)
  waiting for transfers between devices  1 us (1%)
    all_to_all x1, blocking collectives, on_device(): parts = lax.all_to_all(parts, 'cols', 0, 0)  22.4 us
    all_to_all x1, blocking collectives, on_device(): lax.all_to_all(terms, ('rows', 'cols'), 0, 0, axis_index_groups=same)  12.8 us
    all_to_all x1, blocking collectives, on_device(): lax.all_to_all(jnp.broadcast_to(mine[None], (ranks, *mine.shape)), 'rows'...  12.6 us
    pallas_call x1, Pallas kernels, on_device(): pl.pallas_call(functools.partial(first_inner, nblocks, local), in_specs=[...  7.3 us
    ppermute x2, starting transfers between devices, around(): return (lax.ppermute(near, 'rows', mate), far)  7 us
    pallas_call x1, Pallas kernels, on_device(): pl.pallas_call(functools.partial(second_inner, nblocks, local), in_specs=...  4.76 us
    ppermute x1, starting transfers between devices, on_device(): keep = keep + lax.ppermute(give, 'rows', mate)  4.13 us
    pallas_call x1, Pallas kernels, on_device(): pl.pallas_call(functools.partial(second_edge, nblocks, local), in_specs=[...  1.59 us
  transfers between devices with their start and end apart: 5, of which 1 were waited for; matrix products, arithmetic and copies ran while one was open for 0% of the time, Pallas kernels for 15%

profile of v6, /device:TPU:1, one launch (start us, length us, event | category | flops | bytes accessed | tf_op | source)
XLA Modules:
  0.0 78.0 jit_solution(14150141778898673679)
XLA Ops:
  0.6 0.9 %ends.1 = (f32[32,512]{1,0:T(8,128)S(1)}, f32[32,512]{1,0:T(8,128)S(1)}) custom-call(f32[32,4096]{1,0:T(8,128)} %field_hbm.3), custom_call_target="tpu_custom_call" | custom-call | tf_op jit(solution)/shard_map/ends/pallas_call | solution.py:311
  1.5 3.3 %collective-permute-start = (f32[32,512]{1,0:T(8,128)S(1)}, f32[32,512]{1,0:T(8,128)S(1)}, u32[]{:S(2)}, u32[]{:S(2)}) collective-permute-start(f32[32,512]{1,0:T(8,128)S(1)} %get-tuple-element.20), channel_id=1, source_target_pairs={{0,8},{8,0},{16,24},{24,16},{32,40},{40,32},{48,56},{56,48},{64,72... | collective-permute-start | bytes 196616 | tf_op jit(solution)/shard_map/ppermute | solution.py:306
  4.9 0.0 collective-permute-start.1
  4.9 7.3 %first_inner.1 = (s32[9,32]{1,0:T(8,128)S(4)}, s32[32]{0:T(128)S(4)}, f32[32,9,128,128]{3,2,1,0:T(8,128)S(1)}, f32[32,4096]{1,0:T(8,128)S(1)}, f32[32,128]{1,0:T(8,128)S(1)}, /*index=5*/f32[32,3072]{1,0:T(8,128)S(1)}) custom-call(s32[9,32]{1,0:T(8,128)} %bitcast.5, s32[32]{0:T(128)} %counts_hbm.1, f32[32,128]{1,0:T(8,128)} %bitcast.4, f32[32,4096]{1,0:T(8,128)} %field_hbm.3, ...), custom_call_target="tpu_custom_call" | custom-call | flops 1207959552 | bytes 18874368 | tf_op jit(solution)/shard_map/first_inner/pallas_call | solution.py:322
  12.2 0.0 collective-permute-done.near
  12.2 0.0 collective-permute-done.1.far
  12.2 1.6 %first_edge.1 = (f32[32,1024]{1,0:T(8,128)S(1)}, f32[32,512]{1,0:T(8,128)S(1)}, f32[32,512]{1,0:T(8,128)S(1)}) custom-call(s32[9,32]{1,0:T(8,128)S(4)} %get-tuple-element.17.cols, s32[32]{0:T(128)S(4)} %get-tuple-element.18.counts, f32[32,128]{1,0:T(8,128)S(1)} %get-tuple-element.19.onsite, f32[32,512]{1,0:T(8,128)S(1)} %collective-permute-done.near, ...), custom_call_target="tpu_custom_call" | custom-call | flops 301989888 | bytes 4718592 | tf_op jit(solution)/shard_map/first_edge/pallas_call | solution.py:344
  13.8 3.7 %collective-permute-start.2 = (f32[32,512]{1,0:T(8,128)S(1)}, f32[32,512]{1,0:T(8,128)S(1)}, u32[]{:S(2)}, u32[]{:S(2)}) collective-permute-start(f32[32,512]{1,0:T(8,128)S(1)} %get-tuple-element.24), channel_id=1, source_target_pairs={{0,8},{8,0},{16,24},{24,16},{32,40},{40,32},{48,56},{56,48},{64,72... | collective-permute-start | bytes 196616 | tf_op jit(solution)/shard_map/ppermute | solution.py:306
  17.4 0.0 collective-permute-start.3
  17.5 4.8 %second_inner.1.done = f32[32,3072]{1,0:T(8,128)S(1)} custom-call(s32[9,32]{1,0:T(8,128)S(4)} %get-tuple-element.17.cols, s32[32]{0:T(128)S(4)} %get-tuple-element.18.counts, f32[32,128]{1,0:T(8,128)S(1)} %get-tuple-element.19.onsite, f32[32,1024]{1,0:T(8,128)S(1)} %get-tuple-element.26.edge, f32[32,3072]{1,0:T(8,128)S(1)} %get-tuple-element.27.inner, ...), custom_call_target="tpu_custom_call" | custom-call | flops 905969664 | bytes 14155776 | tf_op jit(solution)/shard_map/second_inner/pallas_call | solution.py:356
  22.2 0.0 collective-permute-done.2.near
  22.2 0.0 collective-permute-done.3.far
  22.2 1.6 %second_edge.1 = (f32[32,4096]{1,0:T(8,128)S(1)}, f32[8,32,512]{2,1,0:T(8,128)S(1)}) custom-call(s32[9,32]{1,0:T(8,128)S(4)} %get-tuple-element.17.cols, s32[32]{0:T(128)S(4)} %get-tuple-element.18.counts, f32[32,128]{1,0:T(8,128)S(1)} %get-tuple-element.19.onsite, f32[32,512]{1,0:T(8,128)S(1)} %collective-permute-done.2.near, ...), custom_call_target="tpu_custom_call" | custom-call | flops 301989888 | bytes 4718592 | tf_op jit(solution)/shard_map/second_edge/pallas_call | solution.py:367
  23.8 22.4 %all_to_all.15.parts = f32[8,32,512]{2,1,0:T(8,128)S(1)} all-to-all(f32[8,32,512]{2,1,0:T(8,128)S(1)} %get-tuple-element.28), channel_id=1, replica_groups=mesh['rows'=32,'cols'=8] {'cols'}, dimensions={0} | all-to-all | bytes 1048576 | tf_op jit(solution)/shard_map/all_to_all | solution.py:381
  46.2 0.4 gram.1
  46.6 4.1 %collective-permute-start.4 = (f32[8,32,128]{2,1,0:T(8,128)S(1)}, f32[8,32,128]{2,1,0:T(8,128)S(1)}, u32[]{:S(2)}, u32[]{:S(2)}) collective-permute-start(f32[8,32,128]{2,1,0:T(8,128)S(1)} %get-tuple-element.30), channel_id=1, source_target_pairs={{0,8},{8,0},{16,24},{24,16},{32,40},{40,32},{48,56},{56,48},{64,72... | collective-permute-start | bytes 393224 | tf_op jit(solution)/shard_map/ppermute | solution.py:391
  50.8 1.0 %collective-permute-done.4 = f32[8,32,128]{2,1,0:T(8,128)S(1)} collective-permute-done((f32[8,32,128]{2,1,0:T(8,128)S(1)}, f32[8,32,128]{2,1,0:T(8,128)S(1)}, u32[]{:S(2)}, u32[]{:S(2)}) %collective-permute-start.4) | collective-permute-done | bytes 131104 | tf_op jit(solution)/shard_map/ppermute | solution.py:391
  51.8 12.8 %all_to_all.16 = f32[32,8,128]{2,1,0:T(8,128)S(1)} all-to-all(f32[32,8,128]{2,1,0:T(8,128)S(1)} %bitcast.3), channel_id=1, replica_groups={{0,64,128,192,1,65,129,193,2,66,130,194,3,67,131,195,4,68,132,196,5,69,..., dimensions={0} | all-to-all | bytes 262144 | tf_op jit(solution)/shard_map/all_to_all | solution.py:401
  64.7 12.6 %all_to_all.17.terms = f32[32,8,128]{2,1,0:T(8,128)S(1)} all-to-all(f32[32,8,128]{2,1,0:T(8,128)S(1)} %broadcast_in_dim.2), channel_id=1, replica_groups=mesh['rows'=32,'cols'=8] {'rows'}, dimensions={0} | all-to-all | bytes 262144 | tf_op jit(solution)/shard_map/all_to_all | solution.py:403
  77.2 0.8 %join.1 = (f32[32,4096]{1,0:T(8,128)}, f32[32,256]{1,0:T(8,128)}) custom-call(f32[32,8,128]{2,1,0:T(8,128)S(1)} %all_to_all.17.terms, f32[32,4096]{1,0:T(8,128)S(1)} %get-tuple-element.31.filtered), custom_call_target="tpu_custom_call" | custom-call | tf_op jit(solution)/shard_map/join/pallas_call | solution.py:404
  (3 shorter events, 0.1 us)
Async XLA Ops:
  1.5 10.6 %collective-permute-start = (f32[32,512]{1,0:T(8,128)S(1)}, f32[32,512]{1,0:T(8,128)S(1)}, u32[]{:S(2)}, u32[]{:S(2)}) collective-permute-start(f32[32,512]{1,0:T(8,128)S(1)} %get-tuple-element.20), channel_id=1, source_target_pairs={{0,8},{8,0},{16,24},{24,16},{32,40},{40,32},{48,56},{56,48},{64,72... | collective-permute-start | bytes 196616 | tf_op jit(solution)/shard_map/ppermute | solution.py:306
  4.9 7.3 %collective-permute-start.1 = (f32[32,512]{1,0:T(8,128)S(1)}, f32[32,512]{1,0:T(8,128)S(1)}, u32[]{:S(2)}, u32[]{:S(2)}) collective-permute-start(f32[32,512]{1,0:T(8,128)S(1)} %get-tuple-element.21), channel_id=1, source_target_pairs={{0,248},{8,16},{16,8},{24,32},{32,24},{40,48},{48,40},{56,64},{64,... | collective-permute-start | bytes 196616 | tf_op jit(solution)/shard_map/ppermute | solution.py:305
  13.8 8.4 %collective-permute-start.2 = (f32[32,512]{1,0:T(8,128)S(1)}, f32[32,512]{1,0:T(8,128)S(1)}, u32[]{:S(2)}, u32[]{:S(2)}) collective-permute-start(f32[32,512]{1,0:T(8,128)S(1)} %get-tuple-element.24), channel_id=1, source_target_pairs={{0,8},{8,0},{16,24},{24,16},{32,40},{40,32},{48,56},{56,48},{64,72... | collective-permute-start | bytes 196616 | tf_op jit(solution)/shard_map/ppermute | solution.py:306
  17.4 4.8 %collective-permute-start.3 = (f32[32,512]{1,0:T(8,128)S(1)}, f32[32,512]{1,0:T(8,128)S(1)}, u32[]{:S(2)}, u32[]{:S(2)}) collective-permute-start(f32[32,512]{1,0:T(8,128)S(1)} %get-tuple-element.25), channel_id=1, source_target_pairs={{0,248},{8,16},{16,8},{24,32},{32,24},{40,48},{48,40},{56,64},{64,... | collective-permute-start | bytes 196616 | tf_op jit(solution)/shard_map/ppermute | solution.py:305
  46.6 5.1 %collective-permute-start.4 = (f32[8,32,128]{2,1,0:T(8,128)S(1)}, f32[8,32,128]{2,1,0:T(8,128)S(1)}, u32[]{:S(2)}, u32[]{:S(2)}) collective-permute-start(f32[8,32,128]{2,1,0:T(8,128)S(1)} %get-tuple-element.30), channel_id=1, source_target_pairs={{0,8},{8,0},{16,24},{24,16},{32,40},{40,32},{48,56},{56,48},{64,72... | collective-permute-start | bytes 393224 | tf_op jit(solution)/shard_map/ppermute | solution.py:391

commit v7 on v6

--- a/solution.py
+++ b/solution.py
@@ -193,7 +193,7 @@
             (edge, REACH, local, REACH),
         ],
     )
-    unroll = 8
+    unroll = 24
 
     def step(s, carry):
         for u in range(unroll):

time: 78.3 us -> 78 us (level)
  no operation moved by 1% of the time
where the time goes in v7:
time: 78 us; the launch traced here: 77.7 us
  blocking collectives  47.3 us (61%)
  Pallas kernels  17 us (22%)
  starting transfers between devices  11.7 us (15%)
  waiting for transfers between devices  1 us (1%)
    all_to_all x1, blocking collectives, on_device(): parts = lax.all_to_all(parts, 'cols', 0, 0)  21.9 us
    all_to_all x1, blocking collectives, on_device(): lax.all_to_all(terms, ('rows', 'cols'), 0, 0, axis_index_groups=same)  12.8 us
    all_to_all x1, blocking collectives, on_device(): lax.all_to_all(jnp.broadcast_to(mine[None], (ranks, *mine.shape)), 'rows'...  12.6 us
    pallas_call x1, Pallas kernels, on_device(): pl.pallas_call(functools.partial(first_inner, nblocks, local), in_specs=[...  7.3 us
    ppermute x2, starting transfers between devices, around(): return (lax.ppermute(near, 'rows', mate), far)  7 us
    ppermute x1, starting transfers between devices, on_device(): keep = keep + lax.ppermute(give, 'rows', mate)  4.66 us
    pallas_call x1, Pallas kernels, on_device(): pl.pallas_call(functools.partial(second_inner, nblocks, local), in_specs=...  4.45 us
    pallas_call x1, Pallas kernels, on_device(): pl.pallas_call(functools.partial(second_edge, nblocks, local), in_specs=[...  1.59 us
  transfers between devices with their start and end apart: 5, of which 1 were waited for; matrix products, arithmetic and copies ran while one was open for 0% of the time, Pallas kernels for 15%

profile of v7, /device:TPU:1, one launch (start us, length us, event | category | flops | bytes accessed | tf_op | source)
XLA Modules:
  0.0 77.7 jit_solution(2418536949407778546)
XLA Ops:
  0.6 0.9 %ends.1 = (f32[32,512]{1,0:T(8,128)S(1)}, f32[32,512]{1,0:T(8,128)S(1)}) custom-call(f32[32,4096]{1,0:T(8,128)} %field_hbm.3), custom_call_target="tpu_custom_call" | custom-call | tf_op jit(solution)/shard_map/ends/pallas_call | solution.py:311
  1.5 3.3 %collective-permute-start = (f32[32,512]{1,0:T(8,128)S(1)}, f32[32,512]{1,0:T(8,128)S(1)}, u32[]{:S(2)}, u32[]{:S(2)}) collective-permute-start(f32[32,512]{1,0:T(8,128)S(1)} %get-tuple-element.20), channel_id=1, source_target_pairs={{0,8},{8,0},{16,24},{24,16},{32,40},{40,32},{48,56},{56,48},{64,72... | collective-permute-start | bytes 196616 | tf_op jit(solution)/shard_map/ppermute | solution.py:306
  4.9 0.0 collective-permute-start.1
  4.9 7.3 %first_inner.1 = (s32[9,32]{1,0:T(8,128)S(4)}, s32[32]{0:T(128)S(4)}, f32[32,9,128,128]{3,2,1,0:T(8,128)S(1)}, f32[32,4096]{1,0:T(8,128)S(1)}, f32[32,128]{1,0:T(8,128)S(1)}, /*index=5*/f32[32,3072]{1,0:T(8,128)S(1)}) custom-call(s32[9,32]{1,0:T(8,128)} %bitcast.5, s32[32]{0:T(128)} %counts_hbm.1, f32[32,128]{1,0:T(8,128)} %bitcast.4, f32[32,4096]{1,0:T(8,128)} %field_hbm.3, ...), custom_call_target="tpu_custom_call" | custom-call | flops 1207959552 | bytes 18874368 | tf_op jit(solution)/shard_map/first_inner/pallas_call | solution.py:322
  12.2 0.0 collective-permute-done.near
  12.2 0.0 collective-permute-done.1.far
  12.2 1.6 %first_edge.1 = (f32[32,1024]{1,0:T(8,128)S(1)}, f32[32,512]{1,0:T(8,128)S(1)}, f32[32,512]{1,0:T(8,128)S(1)}) custom-call(s32[9,32]{1,0:T(8,128)S(4)} %get-tuple-element.17.cols, s32[32]{0:T(128)S(4)} %get-tuple-element.18.counts, f32[32,128]{1,0:T(8,128)S(1)} %get-tuple-element.19.onsite, f32[32,512]{1,0:T(8,128)S(1)} %collective-permute-done.near, ...), custom_call_target="tpu_custom_call" | custom-call | flops 301989888 | bytes 4718592 | tf_op jit(solution)/shard_map/first_edge/pallas_call | solution.py:344
  13.8 3.7 %collective-permute-start.2 = (f32[32,512]{1,0:T(8,128)S(1)}, f32[32,512]{1,0:T(8,128)S(1)}, u32[]{:S(2)}, u32[]{:S(2)}) collective-permute-start(f32[32,512]{1,0:T(8,128)S(1)} %get-tuple-element.24), channel_id=1, source_target_pairs={{0,8},{8,0},{16,24},{24,16},{32,40},{40,32},{48,56},{56,48},{64,72... | collective-permute-start | bytes 196616 | tf_op jit(solution)/shard_map/ppermute | solution.py:306
  17.4 0.0 collective-permute-start.3
  17.5 4.5 %second_inner.1.done = f32[32,3072]{1,0:T(8,128)S(1)} custom-call(s32[9,32]{1,0:T(8,128)S(4)} %get-tuple-element.17.cols, s32[32]{0:T(128)S(4)} %get-tuple-element.18.counts, f32[32,128]{1,0:T(8,128)S(1)} %get-tuple-element.19.onsite, f32[32,1024]{1,0:T(8,128)S(1)} %get-tuple-element.26.edge, f32[32,3072]{1,0:T(8,128)S(1)} %get-tuple-element.27.inner, ...), custom_call_target="tpu_custom_call" | custom-call | flops 905969664 | bytes 14155776 | tf_op jit(solution)/shard_map/second_inner/pallas_call | solution.py:356
  21.9 0.0 collective-permute-done.2.near
  21.9 0.0 collective-permute-done.3.far
  21.9 1.6 %second_edge.1 = (f32[32,4096]{1,0:T(8,128)S(1)}, f32[8,32,512]{2,1,0:T(8,128)S(1)}) custom-call(s32[9,32]{1,0:T(8,128)S(4)} %get-tuple-element.17.cols, s32[32]{0:T(128)S(4)} %get-tuple-element.18.counts, f32[32,128]{1,0:T(8,128)S(1)} %get-tuple-element.19.onsite, f32[32,512]{1,0:T(8,128)S(1)} %collective-permute-done.2.near, ...), custom_call_target="tpu_custom_call" | custom-call | flops 301989888 | bytes 4718592 | tf_op jit(solution)/shard_map/second_edge/pallas_call | solution.py:367
  23.5 21.9 %all_to_all.15.parts = f32[8,32,512]{2,1,0:T(8,128)S(1)} all-to-all(f32[8,32,512]{2,1,0:T(8,128)S(1)} %get-tuple-element.28), channel_id=1, replica_groups=mesh['rows'=32,'cols'=8] {'cols'}, dimensions={0} | all-to-all | bytes 1048576 | tf_op jit(solution)/shard_map/all_to_all | solution.py:381
  45.4 0.4 gram.1
  45.8 4.7 %collective-permute-start.4 = (f32[8,32,128]{2,1,0:T(8,128)S(1)}, f32[8,32,128]{2,1,0:T(8,128)S(1)}, u32[]{:S(2)}, u32[]{:S(2)}) collective-permute-start(f32[8,32,128]{2,1,0:T(8,128)S(1)} %get-tuple-element.30), channel_id=1, source_target_pairs={{0,8},{8,0},{16,24},{24,16},{32,40},{40,32},{48,56},{56,48},{64,72... | collective-permute-start | bytes 393224 | tf_op jit(solution)/shard_map/ppermute | solution.py:391
  50.5 1.0 %collective-permute-done.4 = f32[8,32,128]{2,1,0:T(8,128)S(1)} collective-permute-done((f32[8,32,128]{2,1,0:T(8,128)S(1)}, f32[8,32,128]{2,1,0:T(8,128)S(1)}, u32[]{:S(2)}, u32[]{:S(2)}) %collective-permute-start.4) | collective-permute-done | bytes 131104 | tf_op jit(solution)/shard_map/ppermute | solution.py:391
  51.5 12.8 %all_to_all.16 = f32[32,8,128]{2,1,0:T(8,128)S(1)} all-to-all(f32[32,8,128]{2,1,0:T(8,128)S(1)} %bitcast.3), channel_id=1, replica_groups={{0,64,128,192,1,65,129,193,2,66,130,194,3,67,131,195,4,68,132,196,5,69,..., dimensions={0} | all-to-all | bytes 262144 | tf_op jit(solution)/shard_map/all_to_all | solution.py:401
  64.4 12.6 %all_to_all.17.terms = f32[32,8,128]{2,1,0:T(8,128)S(1)} all-to-all(f32[32,8,128]{2,1,0:T(8,128)S(1)} %broadcast_in_dim.2), channel_id=1, replica_groups=mesh['rows'=32,'cols'=8] {'rows'}, dimensions={0} | all-to-all | bytes 262144 | tf_op jit(solution)/shard_map/all_to_all | solution.py:403
  76.9 0.8 %join.1 = (f32[32,4096]{1,0:T(8,128)}, f32[32,256]{1,0:T(8,128)}) custom-call(f32[32,8,128]{2,1,0:T(8,128)S(1)} %all_to_all.17.terms, f32[32,4096]{1,0:T(8,128)S(1)} %get-tuple-element.31.filtered), custom_call_target="tpu_custom_call" | custom-call | tf_op jit(solution)/shard_map/join/pallas_call | solution.py:404
  (3 shorter events, 0.1 us)
Async XLA Ops:
  1.5 10.6 %collective-permute-start = (f32[32,512]{1,0:T(8,128)S(1)}, f32[32,512]{1,0:T(8,128)S(1)}, u32[]{:S(2)}, u32[]{:S(2)}) collective-permute-start(f32[32,512]{1,0:T(8,128)S(1)} %get-tuple-element.20), channel_id=1, source_target_pairs={{0,8},{8,0},{16,24},{24,16},{32,40},{40,32},{48,56},{56,48},{64,72... | collective-permute-start | bytes 196616 | tf_op jit(solution)/shard_map/ppermute | solution.py:306
  4.9 7.3 %collective-permute-start.1 = (f32[32,512]{1,0:T(8,128)S(1)}, f32[32,512]{1,0:T(8,128)S(1)}, u32[]{:S(2)}, u32[]{:S(2)}) collective-permute-start(f32[32,512]{1,0:T(8,128)S(1)} %get-tuple-element.21), channel_id=1, source_target_pairs={{0,248},{8,16},{16,8},{24,32},{32,24},{40,48},{48,40},{56,64},{64,... | collective-permute-start | bytes 196616 | tf_op jit(solution)/shard_map/ppermute | solution.py:305
  13.8 8.1 %collective-permute-start.2 = (f32[32,512]{1,0:T(8,128)S(1)}, f32[32,512]{1,0:T(8,128)S(1)}, u32[]{:S(2)}, u32[]{:S(2)}) collective-permute-start(f32[32,512]{1,0:T(8,128)S(1)} %get-tuple-element.24), channel_id=1, source_target_pairs={{0,8},{8,0},{16,24},{24,16},{32,40},{40,32},{48,56},{56,48},{64,72... | collective-permute-start | bytes 196616 | tf_op jit(solution)/shard_map/ppermute | solution.py:306
  17.4 4.5 %collective-permute-start.3 = (f32[32,512]{1,0:T(8,128)S(1)}, f32[32,512]{1,0:T(8,128)S(1)}, u32[]{:S(2)}, u32[]{:S(2)}) collective-permute-start(f32[32,512]{1,0:T(8,128)S(1)} %get-tuple-element.25), channel_id=1, source_target_pairs={{0,248},{8,16},{16,8},{24,32},{32,24},{40,48},{48,40},{56,64},{64,... | collective-permute-start | bytes 196616 | tf_op jit(solution)/shard_map/ppermute | solution.py:305
  45.8 5.7 %collective-permute-start.4 = (f32[8,32,128]{2,1,0:T(8,128)S(1)}, f32[8,32,128]{2,1,0:T(8,128)S(1)}, u32[]{:S(2)}, u32[]{:S(2)}) collective-permute-start(f32[8,32,128]{2,1,0:T(8,128)S(1)} %get-tuple-element.30), channel_id=1, source_target_pairs={{0,8},{8,0},{16,24},{24,16},{32,40},{40,32},{48,56},{56,48},{64,72... | collective-permute-start | bytes 393224 | tf_op jit(solution)/shard_map/ppermute | solution.py:391
